TPU v7x, 32 devices: a whole 2x2x4 slice. The times are simulated.
32 devices in a mesh: wide: 8 (over y, x, core), narrow: 4 (over z).
Axes of the slice: x: 2, y: 2, z: 4, core: 2. Of those that a mesh axis runs over, the one named last changes fastest.
Arguments:
- patches: bfloat16 [192, 576, 384], P(('wide', 'narrow')), may hold values from -6 to 6
- valid: int32 [192, 576], P(('wide', 'narrow')), may hold values from 0 to 1, as said below
- attn_weights: bfloat16 [384, 1536], P(None, ('wide', 'narrow')), may hold values from -2.5005208 to 2.5005208
- norm_gains: bfloat16 [768], P(('wide', 'narrow')), may hold values from 0.099609375 to 1.8984375
- vec_biases: bfloat16 [1536], P(('wide', 'narrow')), may hold values from -0.3125 to 0.3125
- slot_params: bfloat16 [3072], P(('wide', 'narrow')), may hold values from -0.625 to 0.625
- expert_in: bfloat16 [8, 384, 1536], P(None, None, ('wide', 'narrow')), may hold values from -0.875 to 0.875
- expert_in_bias: bfloat16 [8, 1536], P(None, ('wide', 'narrow')), may hold values from -1.75 to 1.75
- expert_out: bfloat16 [8, 1536, 384], P(None, ('wide', 'narrow')), may hold values from -0.375 to 0.375
- expert_out_bias: bfloat16 [3072], P(('wide', 'narrow')), may hold values from -0.625 to 0.625
- out_grad: bfloat16 [192, 576, 384], P(('wide', 'narrow')), may hold values from -12 to 12
Outputs:
- mixed_out: bfloat16 [192, 576, 384], P(('wide', 'narrow'))
- patch_grad: bfloat16 [192, 576, 384], P(('wide', 'narrow'))
- attn_weights_grad: float32 [384, 1536], P(None, ('wide', 'narrow'))
- norm_gains_grad: float32 [768], P(('wide', 'narrow'))
- vec_biases_grad: float32 [1536], P(('wide', 'narrow'))
- slot_params_grad: float32 [3072], P(('wide', 'narrow'))
- expert_in_grad: float32 [8, 384, 1536], P(None, None, ('wide', 'narrow'))
- expert_in_bias_grad: float32 [8, 1536], P(None, ('wide', 'narrow'))
- expert_out_grad: float32 [8, 1536, 384], P(None, ('wide', 'narrow'))
- expert_out_bias_grad: float32 [3072], P(('wide', 'narrow'))
Inputs may be any that keep to these rules, and one draw needn't show every extreme that they name: In each image the first 196 patches are valid; the others are either all valid or all padding.
All inputs are finite; a program needn't handle non-finite values.
Results may differ from a plain program's by a relative error of at most 0.019.
Values may be sent and summed in bfloat16 or wider, within the bound.
A program may use at most 192 MiB of HBM per device.

v0:
```python
import jax
import jax.numpy as jnp
from jax import lax
from jax.sharding import PartitionSpec as P

HEAD_DIM = 64


masked_score = -1000000000.0


def normalize(values):
    centred = values - jnp.mean(values, axis=-1, keepdims=True)
    variance = jnp.mean(centred * centred, axis=-1, keepdims=True)
    factor = lax.rsqrt(variance + 1e-06)
    return (centred * factor, factor)


def norm_back(grad_hat, normed, factor):
    return factor * (
        grad_hat
        - jnp.mean(grad_hat, axis=-1, keepdims=True)
        - normed * jnp.mean(grad_hat * normed, axis=-1, keepdims=True)
    )


def smooth(values):
    return jax.nn.gelu(values, approximate=False)


def masked_scores(query, keys, keep):
    scores = jnp.einsum(
        "qhc,khc->hqk", query, keys, preferred_element_type=jnp.float32
    ) * query.shape[-1] ** (-0.5)
    return jnp.where(keep[None, None, :], scores, masked_score)


def attend(item):
    query, keys, values, keep = item
    scores = masked_scores(query, keys, keep)
    peak = jnp.max(scores, axis=-1, keepdims=True)
    spread = peak + jnp.log(jnp.sum(jnp.exp(scores - peak), axis=-1, keepdims=True))
    weights = jnp.exp(scores - spread).astype(jnp.bfloat16)
    attended = jnp.einsum("hqk,khc->qhc", weights, values, preferred_element_type=jnp.float32)
    return (attended.astype(jnp.bfloat16), spread)


def attend_back(item):
    query, keys, values, keep, spread, upstream = item
    weights = jnp.exp(masked_scores(query, keys, keep) - spread)
    prob_grad = jnp.einsum("qhc,khc->hqk", upstream, values, preferred_element_type=jnp.float32)
    score_grad = (
        weights * (prob_grad - jnp.sum(weights * prob_grad, axis=-1, keepdims=True))
    ).astype(jnp.bfloat16)
    factor = query.shape[-1] ** (-0.5)
    query_grad = (
        jnp.einsum("hqk,khc->qhc", score_grad, keys, preferred_element_type=jnp.float32) * factor
    ).astype(jnp.bfloat16)
    key_grad = (
        jnp.einsum("hqk,qhc->khc", score_grad, query, preferred_element_type=jnp.float32) * factor
    ).astype(jnp.bfloat16)
    value_grad = jnp.einsum(
        "hqk,qhc->khc", weights.astype(jnp.bfloat16), upstream, preferred_element_type=jnp.float32
    ).astype(jnp.bfloat16)
    return (query_grad, key_grad, value_grad)


def on_device(
    patches,
    valid,
    attn_weights,
    norm_gains,
    vec_biases,
    slot_params,
    expert_in,
    expert_in_bias,
    expert_out,
    expert_out_bias,
    out_grad,
):
    local_images, patch_count, width = patches.shape
    experts = expert_in.shape[0]
    heads = width // HEAD_DIM
    head_shape = (local_images, patch_count, heads, HEAD_DIM)
    weights, gains, biases, slot_flat, expert_shift = (
        lax.all_gather(attn_weights, ("wide", "narrow"), axis=1, tiled=True),
        lax.all_gather(norm_gains, ("wide", "narrow"), axis=0, tiled=True),
        lax.all_gather(vec_biases, ("wide", "narrow"), axis=0, tiled=True),
        lax.all_gather(slot_params, ("wide", "narrow"), axis=0, tiled=True),
        lax.all_gather(expert_out_bias, ("wide", "narrow"), axis=0, tiled=True),
    )
    gains = gains.astype(jnp.float32)
    biases = biases.astype(jnp.float32)
    first_gain = gains[:width]
    second_gain = gains[width:]
    keep = valid > 0
    images = patches.astype(jnp.float32)
    normed_one, factor_one = normalize(images)
    first = (normed_one * first_gain + biases[:width]).astype(jnp.bfloat16)
    project = jnp.einsum(
        "bpd,de->bpe", first, weights[:, : 3 * width], preferred_element_type=jnp.float32
    )
    query = project[..., :width].astype(jnp.bfloat16).reshape(head_shape)
    keys = project[..., width : 2 * width].astype(jnp.bfloat16).reshape(head_shape)
    values = (
        (project[..., 2 * width :] + biases[width : 2 * width])
        .astype(jnp.bfloat16)
        .reshape(head_shape)
    )
    attended, spread = lax.map(attend, (query, keys, values, keep))
    attended = attended.reshape(local_images, patch_count, width)
    branch = jnp.einsum(
        "bpd,de->bpe", attended, weights[:, 3 * width :], preferred_element_type=jnp.float32
    )
    middle = images + branch + biases[2 * width : 3 * width]
    normed_two, factor_two = normalize(middle)
    second = (normed_two * second_gain + biases[3 * width :]).astype(jnp.bfloat16)
    slot_table = slot_flat.reshape(experts, width)
    logits = jnp.einsum("bpd,ed->bpe", second, slot_table, preferred_element_type=jnp.float32)
    dispatch = jax.nn.softmax(jnp.where(keep[:, :, None], logits, masked_score), axis=1)
    combine = jax.nn.softmax(logits, axis=2)
    dispatch_low = dispatch.astype(jnp.bfloat16)
    combine_low = combine.astype(jnp.bfloat16)
    slots = jnp.einsum(
        "bpe,bpd->bed", dispatch_low, second, preferred_element_type=jnp.float32
    ).astype(jnp.bfloat16)
    shift_rows = expert_shift.reshape(experts, width).astype(jnp.float32)
    expand, hidden_shift, contract = (
        lax.all_gather(expert_in, ("wide", "narrow"), axis=2, tiled=True),
        lax.all_gather(expert_in_bias, ("wide", "narrow"), axis=1, tiled=True),
        lax.all_gather(expert_out, ("wide", "narrow"), axis=1, tiled=True),
    )
    hidden = jnp.einsum(
        "bed,edf->bef", slots, expand, preferred_element_type=jnp.float32
    ) + hidden_shift.astype(jnp.float32)
    active = smooth(hidden).astype(jnp.bfloat16)
    produced = jnp.einsum("bef,efd->bed", active, contract, preferred_element_type=jnp.float32)
    produced = (produced + shift_rows).astype(jnp.bfloat16)
    mixture = jnp.einsum("bpe,bed->bpd", combine_low, produced, preferred_element_type=jnp.float32)
    mixed_out = (middle + mixture).astype(jnp.bfloat16)
    weights, gains, slot_flat = (
        lax.all_gather(attn_weights, ("wide", "narrow"), axis=1, tiled=True),
        lax.all_gather(norm_gains, ("wide", "narrow"), axis=0, tiled=True),
        lax.all_gather(slot_params, ("wide", "narrow"), axis=0, tiled=True),
    )
    gains = gains.astype(jnp.float32)
    first_gain = gains[:width]
    second_gain = gains[width:]
    slot_table = slot_flat.reshape(experts, width)
    upstream = out_grad.astype(jnp.float32)
    combine_grad = jnp.einsum(
        "bpd,bed->bpe", out_grad, produced, preferred_element_type=jnp.float32
    )
    produced_grad = jnp.einsum(
        "bpe,bpd->bed", combine_low, out_grad, preferred_element_type=jnp.float32
    ).astype(jnp.bfloat16)
    shift_grad = jnp.sum(produced_grad.astype(jnp.float32), axis=0).reshape(experts * width)
    gelu_back = jax.vjp(smooth, hidden)[1]
    expand_back, contract_back = (
        lax.all_gather(expert_in, ("wide", "narrow"), axis=2, tiled=True),
        lax.all_gather(expert_out, ("wide", "narrow"), axis=1, tiled=True),
    )
    active_grad = jnp.einsum(
        "bed,efd->bef", produced_grad, contract_back, preferred_element_type=jnp.float32
    )
    hidden_grad = gelu_back(active_grad)[0].astype(jnp.bfloat16)
    contract_grad = jnp.einsum(
        "bef,bed->efd", active, produced_grad, preferred_element_type=jnp.float32
    )
    expand_grad = jnp.einsum("bed,bef->edf", slots, hidden_grad, preferred_element_type=jnp.float32)
    inner_grad = jnp.sum(hidden_grad.astype(jnp.float32), axis=0)
    slot_grad = jnp.einsum(
        "bef,edf->bed", hidden_grad, expand_back, preferred_element_type=jnp.float32
    ).astype(jnp.bfloat16)
    expand_grad, inner_grad, contract_grad = (
        lax.psum_scatter(expand_grad, ("wide", "narrow"), scatter_dimension=2, tiled=True),
        lax.psum_scatter(inner_grad, ("wide", "narrow"), scatter_dimension=1, tiled=True),
        lax.psum_scatter(contract_grad, ("wide", "narrow"), scatter_dimension=1, tiled=True),
    )
    dispatch_grad = jnp.einsum(
        "bpd,bed->bpe", second, slot_grad, preferred_element_type=jnp.float32
    )
    second_grad = jnp.einsum(
        "bpe,bed->bpd", dispatch_low, slot_grad, preferred_element_type=jnp.float32
    )
    logit_grad = dispatch * (
        dispatch_grad - jnp.sum(dispatch * dispatch_grad, axis=1, keepdims=True)
    )
    logit_grad = logit_grad + combine * (
        combine_grad - jnp.sum(combine * combine_grad, axis=2, keepdims=True)
    )
    logit_grad = logit_grad.astype(jnp.bfloat16)
    table_grad = jnp.einsum(
        "bpd,bpe->ed", second, logit_grad, preferred_element_type=jnp.float32
    ).reshape(experts * width)
    second_grad = second_grad + jnp.einsum(
        "bpe,ed->bpd", logit_grad, slot_table, preferred_element_type=jnp.float32
    )
    gain_two = jnp.sum(second_grad * normed_two, axis=(0, 1))
    shift_two = jnp.sum(second_grad, axis=(0, 1))
    middle_grad = upstream + norm_back(second_grad * second_gain, normed_two, factor_two)
    branch_grad = middle_grad.astype(jnp.bfloat16)
    output_grad = jnp.einsum(
        "bpd,bpe->de", attended, branch_grad, preferred_element_type=jnp.float32
    )
    branch_shift = jnp.sum(branch_grad.astype(jnp.float32), axis=(0, 1))
    attended_grad = jnp.einsum(
        "bpe,de->bpd", branch_grad, weights[:, 3 * width :], preferred_element_type=jnp.float32
    ).astype(jnp.bfloat16)
    query_grad, key_grad, value_grad = lax.map(
        attend_back, (query, keys, values, keep, spread, attended_grad.reshape(head_shape))
    )
    flat_shape = (local_images, patch_count, width)
    project_grad = jnp.concatenate(
        [
            query_grad.reshape(flat_shape),
            key_grad.reshape(flat_shape),
            value_grad.reshape(flat_shape),
        ],
        axis=-1,
    )
    weight_front = jnp.einsum(
        "bpd,bpe->de", first, project_grad, preferred_element_type=jnp.float32
    )
    value_shift = jnp.sum(value_grad.astype(jnp.float32), axis=(0, 1)).reshape(width)
    first_grad = jnp.einsum(
        "bpe,de->bpd", project_grad, weights[:, : 3 * width], preferred_element_type=jnp.float32
    )
    gain_one = jnp.sum(first_grad * normed_one, axis=(0, 1))
    shift_one = jnp.sum(first_grad, axis=(0, 1))
    patch_grad = (middle_grad + norm_back(first_grad * first_gain, normed_one, factor_one)).astype(
        jnp.bfloat16
    )
    weight_grad = jnp.concatenate([weight_front, output_grad], axis=1)
    gain_grads = jnp.concatenate([gain_one, gain_two])
    bias_grads = jnp.concatenate([shift_one, value_shift, branch_shift, shift_two])
    weight_grad, gain_grads, bias_grads, table_grad, shift_grad = (
        lax.psum_scatter(weight_grad, ("wide", "narrow"), scatter_dimension=1, tiled=True),
        lax.psum_scatter(gain_grads, ("wide", "narrow"), scatter_dimension=0, tiled=True),
        lax.psum_scatter(bias_grads, ("wide", "narrow"), scatter_dimension=0, tiled=True),
        lax.psum_scatter(table_grad, ("wide", "narrow"), scatter_dimension=0, tiled=True),
        lax.psum_scatter(shift_grad, ("wide", "narrow"), scatter_dimension=0, tiled=True),
    )
    return (
        mixed_out,
        patch_grad,
        weight_grad,
        gain_grads,
        bias_grads,
        table_grad,
        expand_grad,
        inner_grad,
        contract_grad,
        shift_grad,
    )


def solution(mesh):
    return jax.shard_map(
        on_device,
        mesh=mesh,
        in_specs=(
            P(("wide", "narrow"), None, None),
            P(("wide", "narrow"), None),
            P(None, ("wide", "narrow")),
            P(("wide", "narrow")),
            P(("wide", "narrow")),
            P(("wide", "narrow")),
            P(None, None, ("wide", "narrow")),
            P(None, ("wide", "narrow")),
            P(None, ("wide", "narrow"), None),
            P(("wide", "narrow")),
            P(("wide", "narrow"), None, None),
        ),
        out_specs=(
            P(("wide", "narrow"), None, None),
            P(("wide", "narrow"), None, None),
            P(None, ("wide", "narrow")),
            P(("wide", "narrow")),
            P(("wide", "narrow")),
            P(("wide", "narrow")),
            P(None, None, ("wide", "narrow")),
            P(None, ("wide", "narrow")),
            P(None, ("wide", "narrow"), None),
            P(("wide", "narrow")),
        ),
        check_vma=False,
    )
```

profile of v0, /device:TPU:0, one launch (start us, length us, event | category | flops | bytes accessed | tf_op | source)
XLA Modules:
  0.0 1048.0 jit_solution(14531429099008938155)
XLA Ops:
  16.0 42.4 %all-reduce.9 = (bf16[768]{0:T(1024)(128)(2,1)S(1)}, bf16[1536]{0:T(1024)(128)(2,1)S(1)}, bf16[3072]{0:T(1024)(128)(2,1)S(1)}, bf16[3072]{0:T(1024)(128)(2,1)S(1)}) all-reduce(bf16[768]{0:T(1024)(128)(2,1)S(1)} %dynamic-update-slice, bf16[1536]{0:T(1024)(128)(2,1)S(1)} %dynamic-update-slice.1, ...), channel_id=1, replica_groups=mesh['wide'=8,'narrow'=4] {'wide','narrow'}, use_global_device_ids=true, to_apply=%add | all-reduce | flops 8448 | bytes 33792
  59.0 67.4 %all-gather = bf16[32,48,8]{1,2,0:T(8,128)(2,1)S(1)} all-gather(bf16[1,48,8]{1,2,0:T(8,128)(2,1)} %bitcast.265), channel_id=1, replica_groups=mesh['wide'=8,'narrow'=4] {'wide','narrow'}, dimensions={0}, use_global_device_ids=true | all-gather | bytes 25344 | tf_op jit(solution)/shard_map/all_gather | solution.py:130
  128.7 8.1 fusion.156
  138.9 5.4 copy.78
  144.3 5.6 fusion.153
  149.9 5.5 copy.79
  155.3 5.4 copy.80
  162.7 59.9 %while.26 = (s32[]{:T(128)}, bf16[6,576,6,64]{1,3,2,0:T(8,128)(2,1)}, f32[6,6,576,1]{2,1,3,0:T(8,128)}, bf16[6,576,6,64]{1,3,2,0:T(8,128)(2,1)}, pred[6,576]{1,0...) while((s32[]{:T(128)}, ...), condition=%wide.region_5.6_spmd, body=%wide.region_2.5_spmd.sunk | while | flops 531722880 | bytes 25976228 | solution.py:110
  168.7 4.0 fusion.201
  178.7 3.9 fusion.201
  188.6 4.0 fusion.201
  198.6 3.9 fusion.201
  202.5 3.4 fusion.200
  208.7 3.9 fusion.201
  218.6 4.0 fusion.201
  222.6 4.7 fusion.157
  236.6 6.2 convolution_add_fusion.1
  242.9 7.0 convert_reduce_fusion.3
  251.3 3.5 fusion.134
  259.8 8.2 multiply_reduce_fusion.1
  268.0 6.4 convert_reduce_fusion.2
  279.6 3.7 copy.90
  287.7 117.0 %while.27 = (s32[]{:T(128)}, bf16[6,576,6,64]{1,3,2,0:T(8,128)(2,1)}, bf16[6,576,6,64]{1,3,2,0:T(8,128)(2,1)}, bf16[6,576,6,64]{1,3,2,0:T(8,128)(2,1)S(1)}, bf16...) while((s32[]{:T(128)}, ...), condition=%wide.region_18.19_spmd, body=%wide.region_16.18_spmd.sunk | while | flops 1304982144 | bytes 65631612 | solution.py:210
  291.2 4.1 multiply_reduce_fusion.9
  304.0 3.3 fusion.213
  310.6 4.1 multiply_reduce_fusion.9
  323.4 3.3 fusion.213
  330.1 4.1 multiply_reduce_fusion.9
  342.9 3.3 fusion.213
  349.6 4.1 multiply_reduce_fusion.9
  362.4 3.3 fusion.213
  369.0 4.1 multiply_reduce_fusion.9
  381.9 3.3 fusion.213
  388.5 4.1 multiply_reduce_fusion.9
  401.3 3.3 fusion.213
  404.6 3.7 copy.93
  408.4 5.5 copy.92
  413.9 5.3 copy.91
  420.5 8.4 fusion.82
  431.3 8.3 fusion.131
  440.6 8.1 fusion.128
  452.8 10.2 fusion.76
  463.1 38.0 %all-reduce.8 = (f32[768]{0:T(1024)S(1)}, f32[1536]{0:T(1024)S(1)}, f32[3072]{0:T(1024)S(1)}, f32[3072]{0:T(1024)S(1)}) all-reduce(f32[768]{0:T(1024)S(1)} %pad_maximum_fusion.7, f32[1536]{0:T(1024)S(1)} %pad_maximum_fusion.6, f32[3072]{0:T(1024)S(1)} %reshape.160, ...), channel_id=3, replica_groups=mesh['wide'=8,'narrow'=4] {'wide','narrow'}, use_global_device_ids=true, to_apply=%region_24.25.clone | all-reduce | flops 8448 | bytes 67584
  503.4 5.0 add_convert_fusion
  508.4 6.9 fusion.75
  516.6 100.1 %reduce-scatter.13.cloned.1.call-done = f32[48,384]{1,0:T(8,128)} async-done(((f32[1536,384]{1,0:T(8,128)}), f32[48,384]{1,0:T(8,128)}) %reduce-scatter.13.cloned.1.call-update) | async-done | bytes 73744
  616.7 212.0 %reduce-scatter.9.cloned.1.call-done = f32[8,384,48]{1,2,0:T(8,128)} async-done(((f32[8,384,1536]{1,2,0:T(8,128)}), f32[8,384,48]{1,2,0:T(8,128)}) %reduce-scatter.9.cloned.1.call-update) | async-done | bytes 589840 | tf_op jit(solution)/shard_map/reduce_scatter | solution.py:176
  828.8 212.1 %reduce-scatter.11.cloned.1.call-done = f32[8,48,384]{2,1,0:T(8,128)} async-done(((f32[8,1536,384]{2,1,0:T(8,128)}), f32[8,48,384]{2,1,0:T(8,128)}) %reduce-scatter.11.cloned.1.call-update) | async-done | bytes 589840 | tf_op jit(solution)/shard_map/reduce_scatter | solution.py:178
  (249 shorter events, 157.5 us)
Async XLA Ops:
  7.2 120.1 %copy-start.4 = (bf16[6,576,384]{2,1,0:T(8,128)(2,1)S(1)}, bf16[6,576,384]{2,1,0:T(8,128)(2,1)}, u32[]{:S(2)}) copy-start(bf16[6,576,384]{2,1,0:T(8,128)(2,1)} %param.15) | copy-start | bytes 7962628
  7.2 121.5 %all-gather.5.cloned.1.call-start = ((), (), s32[]{:S(2)}) async-start(), calls=%async_computation.4 | async-start | bytes 1216512 | tf_op jit(solution)/shard_map/all_gather | solution.py:86
  7.9 228.7 %all-gather.7.cloned.1.call-start = ((), (), s32[]{:S(2)}) async-start(), calls=%async_computation.5 | async-start | bytes 9732096 | tf_op jit(solution)/shard_map/all_gather | solution.py:129
  8.7 234.2 %all-gather.9.cloned.1.call-start = ((), (), s32[]{:S(2)}) async-start(), calls=%async_computation.6 | async-start | bytes 9732096 | tf_op jit(solution)/shard_map/all_gather | solution.py:131
  9.4 505.8 %reduce-scatter.15.cloned.1.call-start = ((), (), s32[]{:S(2)}) async-start(), calls=%async_computation.10 | async-start | bytes 811008
  127.2 103.0 %copy-start.39 = (bf16[8,384,1]{1,0,2:T(8,128)(2,1)}, bf16[8,384,1]{1,0,2:T(8,128)(2,1)S(1)}, u32[]{:S(2)}) copy-start(bf16[8,384,1]{1,0,2:T(8,128)(2,1)S(1)} %reshape.176) | copy-start | bytes 18436
  127.2 9.7 copy-start.45
  127.2 9.7 copy-start.51
  127.2 101.7 %copy-start.43 = (f32[384]{0:T(512)}, f32[384]{0:T(512)S(1)}, u32[]{:S(2)}) copy-start(f32[384]{0:T(512)S(1)} %get-tuple-element.235) | copy-start | bytes 4612
  127.2 9.6 copy-start.29
  128.7 8.2 copy-start.34
  222.6 9.4 copy-start.32
  230.2 24.6 %copy-start.2 = (bf16[6,576,384]{2,1,0:T(8,128)(2,1)}, bf16[6,576,384]{2,1,0:T(8,128)(2,1)S(1)}, u32[]{:S(2)}) copy-start(bf16[6,576,384]{2,1,0:T(8,128)(2,1)S(1)} %add_convert_fusion.1) | copy-start | bytes 7962628
  231.0 11.8 %copy-start.11 = (f32[6,576,8]{1,2,0:T(8,128)}, f32[6,576,8]{1,2,0:T(8,128)S(1)}, u32[]{:S(2)}) copy-start(f32[6,576,8]{1,2,0:T(8,128)S(1)} %fusion.162) | copy-start | bytes 331780
  232.0 27.7 %copy-start.17 = (f32[6,576,8]{1,2,0:T(8,128)}, f32[6,576,8]{1,2,0:T(8,128)S(1)}, u32[]{:S(2)}) copy-start(f32[6,576,8]{1,2,0:T(8,128)S(1)} %get-tuple-element.227) | copy-start | bytes 331780
  232.0 27.7 %copy-start.23 = (f32[6,576]{1,0:T(8,128)}, f32[6,576]{1,0:T(8,128)S(1)}, u32[]{:S(2)}) copy-start(f32[6,576]{1,0:T(8,128)S(1)} %get-tuple-element.226) | copy-start | bytes 41476
  236.1 6.8 copy-start.27
  236.6 13.4 %copy-start.21 = (bf16[6,8,384]{2,1,0:T(8,128)(2,1)}, bf16[6,8,384]{2,1,0:T(8,128)(2,1)S(1)}, u32[]{:S(2)}) copy-start(bf16[6,8,384]{2,1,0:T(8,128)(2,1)S(1)} %convolution_convert_fusion.3) | copy-start | bytes 110596
  242.9 13.6 %copy-start.13 = (f32[8,6,1536]{2,1,0:T(8,128)}, f32[8,6,1536]{2,1,0:T(8,128)S(1)}, u32[]{:S(2)}) copy-start(f32[8,6,1536]{2,1,0:T(8,128)S(1)} %convolution_add_fusion.1) | copy-start | bytes 884740
  242.9 7.1 copy-start.7
  250.0 6.5 slice-start
  250.0 6.5 slice-start.1
  251.3 5.1 copy-start.47
  251.3 5.1 slice-start.2
  259.7 8.3 copy-start.19
  268.0 6.4 copy-start.9
  283.3 4.4 copy-start.33
  404.6 3.7 copy-start.8
  408.4 10.8 %copy-start.42 = (f32[8,1536]{1,0:T(8,128)S(1)}, f32[8,1536]{1,0:T(8,128)}, u32[]{:S(2)}) copy-start(f32[8,1536]{1,0:T(8,128)} %get-tuple-element.232) | copy-start | bytes 147460
  408.4 12.1 %copy-start.5 = (bf16[6,576,384]{2,1,0:T(8,128)(2,1)S(1)}, bf16[6,576,384]{2,1,0:T(8,128)(2,1)}, u32[]{:S(2)}) copy-start(bf16[6,576,384]{2,1,0:T(8,128)(2,1)} %param.15) | copy-start | bytes 7962628
  408.4 12.1 %copy-start.30 = (f32[6,576]{1,0:T(8,128)S(1)}, f32[6,576]{1,0:T(8,128)}, u32[]{:S(2)}) copy-start(f32[6,576]{1,0:T(8,128)} %copy-done.29) | copy-start | bytes 41476
  408.4 12.1 %copy-start.35 = (f32[6,576]{1,0:T(8,128)S(1)}, f32[6,576]{1,0:T(8,128)}, u32[]{:S(2)}) copy-start(f32[6,576]{1,0:T(8,128)} %copy-done.34) | copy-start | bytes 41476
  408.4 12.1 %copy-start.46 = (f32[384]{0:T(512)S(1)}, f32[384]{0:T(512)}, u32[]{:S(2)}) copy-start(f32[384]{0:T(512)} %copy-done.45) | copy-start | bytes 4612
  408.4 12.1 %copy-start.52 = (f32[384]{0:T(512)S(1)}, f32[384]{0:T(512)}, u32[]{:S(2)}) copy-start(f32[384]{0:T(512)} %copy-done.51) | copy-start | bytes 4612
  420.4 196.3 %reduce-scatter.13.cloned.1.call-start = ((), (), s32[]{:S(2)}) async-start(), calls=%async_computation.9 | async-start | bytes 2433024
  431.3 397.5 %reduce-scatter.9.cloned.1.call-start = ((), (), s32[]{:S(2)}) async-start(), calls=%async_computation.7 | async-start | bytes 19464192 | tf_op jit(solution)/shard_map/reduce_scatter | solution.py:176
  439.6 601.3 %reduce-scatter.11.cloned.1.call-start = ((), (), s32[]{:S(2)}) async-start(), calls=%async_computation.8 | async-start | bytes 19464192 | tf_op jit(solution)/shard_map/reduce_scatter | solution.py:178
  448.8 3.4 copy-start.3
  448.8 3.4 copy-start.18
  448.8 3.4 copy-start.20
  448.8 3.9 copy-start.31
  448.8 3.9 copy-start.36
  452.8 10.2 copy-start.48
  452.8 10.3 copy-start.49
  452.8 10.3 copy-start.50
  452.8 50.6 %copy-start.12 = (f32[6,576,8]{1,2,0:T(8,128)S(1)}, f32[6,576,8]{1,2,0:T(8,128)}, u32[]{:S(2)}) copy-start(f32[6,576,8]{1,2,0:T(8,128)} %copy-done.11) | copy-start | bytes 331780
  452.8 50.6 %copy-start.38 = (bf16[6,8,384]{2,0,1:T(8,128)(2,1)S(1)}, bf16[6,8,384]{2,0,1:T(8,128)(2,1)}, u32[]{:S(2)}) copy-start(bf16[6,8,384]{2,0,1:T(8,128)(2,1)} %copy-done.37) | copy-start | bytes 110596
  463.0 45.4 %copy-start.6 = (bf16[6,576,384]{2,1,0:T(8,128)(2,1)S(1)}, bf16[6,576,384]{2,1,0:T(8,128)(2,1)}, u32[]{:S(2)}) copy-start(bf16[6,576,384]{2,1,0:T(8,128)(2,1)} %param.15) | copy-start | bytes 7962628
  (15 other events, 34.0 us)
Sparse Core Ops, SparseCore 0:
  10.8 56.8 all-gather.4
  70.8 81.4 all-gather.6
  155.4 80.7 all-gather.8
  420.5 92.2 reduce-scatter.14
  518.5 98.1 reduce-scatter.12
  624.7 204.0 reduce-scatter.8
  836.9 203.9 reduce-scatter.10
where the time goes:
time: 1050 us
  waiting for transfers between devices  526 us (50%)
  matrix products  230 us (22%)
  blocking collectives  148 us (14%)
  local copies, waits for them, and re-layouts  66.1 us (6%)
  other arithmetic  61.4 us (6%)
  between operations  15.1 us (1%)
    reduce_scatter x1, waiting for transfers between devices, on_device(): lax.psum_scatter(contract_grad, ('wide', 'narrow'), scatter_dimension=1,...  212 us
    reduce_scatter x1, waiting for transfers between devices, on_device(): lax.psum_scatter(expand_grad, ('wide', 'narrow'), scatter_dimension=2, ti...  212 us
    unnamed x9, waiting for transfers between devices  102 us
    unnamed x2, blocking collectives  80.4 us
    all_gather x1, blocking collectives, on_device(): lax.all_gather(expert_in_bias, ('wide', 'narrow'), axis=1, tiled=True)  67.4 us
    dot_general x12, matrix products, masked_scores(): jnp.einsum('qhc,khc->hqk', query, keys, preferred_element_type=jnp.float32)  34.3 us
    dot_general x6, matrix products, attend_back(): jnp.einsum('qhc,khc->hqk', upstream, values, preferred_element_type=jnp.f...  24.8 us
    dot_general x6, matrix products, attend(): jnp.einsum('hqk,khc->qhc', weights, values, preferred_element_type=jnp.fl...  23.7 us
  transfers between devices with their start and end apart: 7, of which 3 were waited for; matrix products, arithmetic and copies ran while one was open for 17% of the time, Pallas kernels for 0%

commit v1 on v0

v1 whole, which is shorter than its diff:
```python
import jax
import jax.numpy as jnp
from jax import lax
from jax.sharding import PartitionSpec as P

HEAD_DIM = 64
MASKED = -1000000000.0
AXES = ("wide", "narrow")


def normalize(values):
    centred = values - jnp.mean(values, axis=-1, keepdims=True)
    variance = jnp.mean(centred * centred, axis=-1, keepdims=True)
    factor = lax.rsqrt(variance + 1e-06)
    return (centred * factor, factor)


def norm_back(grad_hat, normed, factor):
    return factor * (
        grad_hat
        - jnp.mean(grad_hat, axis=-1, keepdims=True)
        - normed * jnp.mean(grad_hat * normed, axis=-1, keepdims=True)
    )


def smooth(values):
    return jax.nn.gelu(values, approximate=False)


def masked_scores(query, keys, keep):
    scores = jnp.einsum(
        "qhc,khc->hqk", query, keys, preferred_element_type=jnp.float32
    ) * query.shape[-1] ** (-0.5)
    return jnp.where(keep[None, None, :], scores, MASKED)


def attend(item):
    query, keys, values, keep = item
    scores = masked_scores(query, keys, keep)
    peak = jnp.max(scores, axis=-1, keepdims=True)
    spread = peak + jnp.log(jnp.sum(jnp.exp(scores - peak), axis=-1, keepdims=True))
    weights = jnp.exp(scores - spread).astype(jnp.bfloat16)
    attended = jnp.einsum("hqk,khc->qhc", weights, values, preferred_element_type=jnp.float32)
    return (attended.astype(jnp.bfloat16), spread)


def attend_back(item):
    query, keys, values, keep, spread, upstream = item
    weights = jnp.exp(masked_scores(query, keys, keep) - spread)
    prob_grad = jnp.einsum("qhc,khc->hqk", upstream, values, preferred_element_type=jnp.float32)
    score_grad = (
        weights * (prob_grad - jnp.sum(weights * prob_grad, axis=-1, keepdims=True))
    ).astype(jnp.bfloat16)
    factor = query.shape[-1] ** (-0.5)
    query_grad = (
        jnp.einsum("hqk,khc->qhc", score_grad, keys, preferred_element_type=jnp.float32) * factor
    ).astype(jnp.bfloat16)
    key_grad = (
        jnp.einsum("hqk,qhc->khc", score_grad, query, preferred_element_type=jnp.float32) * factor
    ).astype(jnp.bfloat16)
    value_grad = jnp.einsum(
        "hqk,qhc->khc", weights.astype(jnp.bfloat16), upstream, preferred_element_type=jnp.float32
    ).astype(jnp.bfloat16)
    return (query_grad, key_grad, value_grad)


def scatter_sum(parts):
    got = lax.all_to_all(parts.astype(jnp.bfloat16), AXES, 0, 0, tiled=True)
    return jnp.sum(got.astype(jnp.float32), axis=0)


def experts_at_home(slots, produced_grad, expert_in, expert_in_bias, expert_out, devices):
    local_images, experts, width = slots.shape
    every = lax.all_gather(jnp.stack([slots, produced_grad]), AXES, axis=1, tiled=True)
    all_slots, all_grads = every[0], every[1]
    hidden = jnp.einsum(
        "bed,edf->bef", all_slots, expert_in, preferred_element_type=jnp.float32
    ) + expert_in_bias.astype(jnp.float32)
    active, gelu_back = jax.vjp(smooth, hidden)
    active = active.astype(jnp.bfloat16)
    partial = jnp.einsum("bef,efd->bed", active, expert_out, preferred_element_type=jnp.float32)
    active_grad = jnp.einsum(
        "bed,efd->bef", all_grads, expert_out, preferred_element_type=jnp.float32
    )
    hidden_grad = gelu_back(active_grad)[0].astype(jnp.bfloat16)
    partial_back = jnp.einsum(
        "bef,edf->bed", hidden_grad, expert_in, preferred_element_type=jnp.float32
    )
    contract_grad = jnp.einsum(
        "bef,bed->efd", active, all_grads, preferred_element_type=jnp.float32
    )
    expand_grad = jnp.einsum(
        "bed,bef->edf", all_slots, hidden_grad, preferred_element_type=jnp.float32
    )
    inner_grad = jnp.sum(hidden_grad.astype(jnp.float32), axis=0)
    both = jnp.stack([partial, partial_back]).reshape(2, devices, local_images, experts, width)
    both = scatter_sum(jnp.moveaxis(both, 1, 0))
    return (both[0], both[1], expand_grad, inner_grad, contract_grad)


def on_device(
    patches,
    valid,
    attn_weights,
    norm_gains,
    vec_biases,
    slot_params,
    expert_in,
    expert_in_bias,
    expert_out,
    expert_out_bias,
    out_grad,
):
    local_images, patch_count, width = patches.shape
    experts = expert_in.shape[0]
    heads = width // HEAD_DIM
    head_shape = (local_images, patch_count, heads, HEAD_DIM)
    flat_shape = (local_images, patch_count, width)
    devices = lax.axis_size("wide") * lax.axis_size("narrow")

    vectors = (norm_gains, vec_biases, slot_params, expert_out_bias)
    lengths = [v.shape[0] for v in vectors]
    small = lax.all_gather(jnp.concatenate(vectors), AXES)
    pieces = []
    at = 0
    for length in lengths:
        pieces.append(small[:, at : at + length].reshape(devices * length))
        at += length
    gains, biases, slot_flat, expert_shift = pieces
    weights = lax.all_gather(attn_weights.T, AXES, axis=0, tiled=True)
    gains = gains.astype(jnp.float32)
    biases = biases.astype(jnp.float32)
    first_gain = gains[:width]
    second_gain = gains[width:]
    keep = valid > 0
    images = patches.astype(jnp.float32)
    normed_one, factor_one = normalize(images)
    first = (normed_one * first_gain + biases[:width]).astype(jnp.bfloat16)
    project = jnp.einsum(
        "bpd,ed->bpe", first, weights[: 3 * width], preferred_element_type=jnp.float32
    )
    query = project[..., :width].astype(jnp.bfloat16).reshape(head_shape)
    keys = project[..., width : 2 * width].astype(jnp.bfloat16).reshape(head_shape)
    values = (
        (project[..., 2 * width :] + biases[width : 2 * width])
        .astype(jnp.bfloat16)
        .reshape(head_shape)
    )
    attended, spread = lax.map(attend, (query, keys, values, keep))
    attended = attended.reshape(flat_shape)
    branch = jnp.einsum(
        "bpd,ed->bpe", attended, weights[3 * width :], preferred_element_type=jnp.float32
    )
    middle = images + branch + biases[2 * width : 3 * width]
    normed_two, factor_two = normalize(middle)
    second = (normed_two * second_gain + biases[3 * width :]).astype(jnp.bfloat16)
    slot_table = slot_flat.reshape(experts, width)
    logits = jnp.einsum("bpd,ed->bpe", second, slot_table, preferred_element_type=jnp.float32)
    dispatch = jax.nn.softmax(jnp.where(keep[:, :, None], logits, MASKED), axis=1)
    combine = jax.nn.softmax(logits, axis=2)
    dispatch_low = dispatch.astype(jnp.bfloat16)
    combine_low = combine.astype(jnp.bfloat16)
    slots = jnp.einsum(
        "bpe,bpd->bed", dispatch_low, second, preferred_element_type=jnp.float32
    ).astype(jnp.bfloat16)
    produced_grad = jnp.einsum(
        "bpe,bpd->bed", combine_low, out_grad, preferred_element_type=jnp.float32
    ).astype(jnp.bfloat16)

    produced, slot_grad, expand_grad, inner_grad, contract_grad = experts_at_home(
        slots, produced_grad, expert_in, expert_in_bias, expert_out, devices
    )
    shift_rows = expert_shift.reshape(experts, width).astype(jnp.float32)
    produced = (produced + shift_rows).astype(jnp.bfloat16)
    slot_grad = slot_grad.astype(jnp.bfloat16)
    shift_grad = jnp.sum(produced_grad.astype(jnp.float32), axis=0).reshape(experts * width)

    mixture = jnp.einsum("bpe,bed->bpd", combine_low, produced, preferred_element_type=jnp.float32)
    mixed_out = (middle + mixture).astype(jnp.bfloat16)
    upstream = out_grad.astype(jnp.float32)
    combine_grad = jnp.einsum(
        "bpd,bed->bpe", out_grad, produced, preferred_element_type=jnp.float32
    )
    dispatch_grad = jnp.einsum(
        "bpd,bed->bpe", second, slot_grad, preferred_element_type=jnp.float32
    )
    second_grad = jnp.einsum(
        "bpe,bed->bpd", dispatch_low, slot_grad, preferred_element_type=jnp.float32
    )
    logit_grad = dispatch * (
        dispatch_grad - jnp.sum(dispatch * dispatch_grad, axis=1, keepdims=True)
    )
    logit_grad = logit_grad + combine * (
        combine_grad - jnp.sum(combine * combine_grad, axis=2, keepdims=True)
    )
    logit_grad = logit_grad.astype(jnp.bfloat16)
    table_grad = jnp.einsum(
        "bpd,bpe->ed", second, logit_grad, preferred_element_type=jnp.float32
    ).reshape(experts * width)
    second_grad = second_grad + jnp.einsum(
        "bpe,ed->bpd", logit_grad, slot_table, preferred_element_type=jnp.float32
    )
    gain_two = jnp.sum(second_grad * normed_two, axis=(0, 1))
    shift_two = jnp.sum(second_grad, axis=(0, 1))
    middle_grad = upstream + norm_back(second_grad * second_gain, normed_two, factor_two)
    branch_grad = middle_grad.astype(jnp.bfloat16)
    output_grad = jnp.einsum(
        "bpd,bpe->ed", attended, branch_grad, preferred_element_type=jnp.float32
    )
    branch_shift = jnp.sum(branch_grad.astype(jnp.float32), axis=(0, 1))
    attended_grad = jnp.einsum(
        "bpe,ed->bpd", branch_grad, weights[3 * width :], preferred_element_type=jnp.float32
    ).astype(jnp.bfloat16)
    query_grad, key_grad, value_grad = lax.map(
        attend_back, (query, keys, values, keep, spread, attended_grad.reshape(head_shape))
    )
    project_grad = jnp.concatenate(
        [
            query_grad.reshape(flat_shape),
            key_grad.reshape(flat_shape),
            value_grad.reshape(flat_shape),
        ],
        axis=-1,
    )
    weight_front = jnp.einsum(
        "bpd,bpe->ed", first, project_grad, preferred_element_type=jnp.float32
    )
    value_shift = jnp.sum(value_grad.astype(jnp.float32), axis=(0, 1)).reshape(width)
    first_grad = jnp.einsum(
        "bpe,ed->bpd", project_grad, weights[: 3 * width], preferred_element_type=jnp.float32
    )
    gain_one = jnp.sum(first_grad * normed_one, axis=(0, 1))
    shift_one = jnp.sum(first_grad, axis=(0, 1))
    patch_grad = (middle_grad + norm_back(first_grad * first_gain, normed_one, factor_one)).astype(
        jnp.bfloat16
    )
    weight_grad = jnp.concatenate([weight_front, output_grad], axis=0)
    weight_grad = scatter_sum(weight_grad.reshape(devices, -1, width)).T
    gain_grads = jnp.concatenate([gain_one, gain_two])
    bias_grads = jnp.concatenate([shift_one, value_shift, branch_shift, shift_two])
    small_grads = jnp.concatenate(
        [v.reshape(devices, -1) for v in (gain_grads, bias_grads, table_grad, shift_grad)], axis=1
    )
    small_grads = jnp.sum(lax.all_to_all(small_grads, AXES, 0, 0, tiled=True), axis=0)
    grads = []
    at = 0
    for length in lengths:
        grads.append(small_grads[at : at + length])
        at += length
    return (
        mixed_out,
        patch_grad,
        weight_grad,
        grads[0],
        grads[1],
        grads[2],
        expand_grad,
        inner_grad,
        contract_grad,
        grads[3],
    )


def solution(mesh):
    images = P(AXES, None, None)
    vector = P(AXES)
    second = P(None, AXES)
    return jax.shard_map(
        on_device,
        mesh=mesh,
        in_specs=(
            images,
            P(AXES, None),
            second,
            vector,
            vector,
            vector,
            P(None, None, AXES),
            second,
            P(None, AXES, None),
            vector,
            images,
        ),
        out_specs=(
            images,
            images,
            second,
            vector,
            vector,
            vector,
            P(None, None, AXES),
            second,
            P(None, AXES, None),
            vector,
        ),
        check_vma=False,
    )
```

time: 1050 us -> 557 us (0.53)
  waiting for transfers between devices: 526 us -> 132 us
  blocking collectives: 148 us -> 42.2 us
  matrix products: 230 us -> 206 us
  other arithmetic: 61.4 us -> 73.8 us
  starting transfers between devices: 0.28 us -> 11.7 us
    reduce_scatter x2 -> x0, waiting for transfers between devices: 424 us -> none  [the longest x1 212 us: on_device(): lax.psum_scatter(contract_grad, ('wide', 'narrow'), scatter_dimension=1,...]
    unnamed x9 -> x2, waiting for transfers between devices: 102 us -> 0.7 us
    all_gather x1 -> x0, blocking collectives: 67.4 us -> none  [on_device(): lax.all_gather(expert_in_bias, ('wide', 'narrow'), axis=1, tiled=True)]
    all_gather x3 -> x2, waiting for transfers between devices: 0.06 us -> 67.3 us  [the longest x1 56.4 us: experts_at_home(): lax.all_gather(jnp.stack([slots, produced_grad]), AXES, axis=1, tiled=True)]
    all_to_all x0 -> x3, waiting for transfers between devices: none -> 64.5 us  [the longest x2 59.4 us: scatter_sum(): got = lax.all_to_all(parts.astype(jnp.bfloat16), AXES, 0, 0, tiled=True)]
    unnamed x2 -> x1, blocking collectives: 80.4 us -> 42.2 us
    dot_general x12, matrix products: 68.6 us -> 46 us  [the longest x1 9.53 us: on_device(): jnp.einsum('bpd,ed->bpe', first, weights[:3 * width], preferred_element_t...]
    all_to_all x0 -> x3, starting transfers between devices: none -> 11.6 us  [the longest x2 7.16 us: scatter_sum(): got = lax.all_to_all(parts.astype(jnp.bfloat16), AXES, 0, 0, tiled=True)]
  transfers between devices with their start and end apart: 7 -> 5, of which waited for: 3 -> 5; matrix products, arithmetic and copies ran while one was open for 17% -> 6% of each run, Pallas kernels for 0% -> 0%
where the time goes in v1:
time: 557 us; the launch traced here: 546 us
  matrix products  206 us (37%)
  waiting for transfers between devices  132 us (24%)
  other arithmetic  73.8 us (13%)
  local copies, waits for them, and re-layouts  63.9 us (11%)
  blocking collectives  42.2 us (8%)
  between operations  15.1 us (3%)
  starting transfers between devices  11.7 us (2%)
    all_to_all x2, waiting for transfers between devices, scatter_sum(): got = lax.all_to_all(parts.astype(jnp.bfloat16), AXES, 0, 0, tiled=True)  59.4 us
    all_gather x1, waiting for transfers between devices, experts_at_home(): lax.all_gather(jnp.stack([slots, produced_grad]), AXES, axis=1, tiled=True)  56.4 us
    unnamed x1, blocking collectives  42.2 us
    dot_general x12, matrix products, masked_scores(): jnp.einsum('qhc,khc->hqk', query, keys, preferred_element_type=jnp.float32)  34 us
    dot_general x6, matrix products, attend_back(): jnp.einsum('qhc,khc->hqk', upstream, values, preferred_element_type=jnp.f...  24.9 us
    dot_general x6, matrix products, attend(): jnp.einsum('hqk,khc->qhc', weights, values, preferred_element_type=jnp.fl...  23.7 us
    dot_general x6, matrix products, attend_back(): jnp.einsum('hqk,qhc->khc', weights.astype(jnp.bfloat16), upstream, prefer...  20 us
    dot_general x6, matrix products, attend_back(): jnp.einsum('hqk,qhc->khc', score_grad, query, preferred_element_type=jnp....  19.6 us
  transfers between devices with their start and end apart: 5, of which 5 were waited for; matrix products, arithmetic and copies ran while one was open for 6% of the time, Pallas kernels for 0%

profile of v1, /device:TPU:0, one launch (start us, length us, event | category | flops | bytes accessed | tf_op | source)
XLA Modules:
  0.0 546.4 jit_solution(16243063516866330537)
XLA Ops:
  9.1 42.2 %all-reduce = bf16[8448]{0:T(1024)(128)(2,1)S(1)} all-reduce(bf16[8448]{0:T(1024)(128)(2,1)S(1)} %dynamic-update-slice), channel_id=2, replica_groups=mesh['wide'=8,'narrow'=4] {'wide','narrow'}, use_global_device_ids=true, to_apply=%add | all-reduce | flops 8448 | bytes 33792
  56.9 10.9 %all-gather.4.cloned.1.call-done = bf16[1536,384]{1,0:T(8,128)(2,1)} async-done(((bf16[48,384]{1,0:T(8,128)(2,1)}), bf16[1536,384]{1,0:T(8,128)(2,1)}) %all-gather.4.cloned.1.call-update) | async-done | bytes 1179664 | tf_op jit(solution)/shard_map/all_gather | solution.py:130
  67.8 9.5 %fusion.162 = (bf16[6,576,1152]{2,1,0:T(8,128)(2,1)S(1)}, f32[6,576,1152]{2,1,0:T(8,128)}) fusion(bf16[1536,384]{1,0:T(8,128)(2,1)} %all-gather.4.cloned.1.call-done, bf16[6,576,384]{2,1,0:T(8,128)(2,1)S(1)} %copy-done.4, f32[384]{0:T(512)S(1)} %slice.97, f32[384]{0:T(512)S(1)} %slice.94, f32[6,576]{1,0:T(8,128)S(1)} %add_rsqrt_fusion.1, ...), kind=kOutput, calls=%fused_computation.225 | convolution fusion | flops 3069591552 | bytes 27457536 | tf_op jit(solution)/shard_map/bpd,ed->bpe/dot_general | solution.py:139
  80.5 5.4 copy.66
  85.8 4.4 fusion.79
  90.3 5.4 copy.64
  95.6 5.4 copy.65
  103.1 59.9 %while.26 = (s32[]{:T(128)}, bf16[6,576,6,64]{1,3,2,0:T(8,128)(2,1)}, f32[6,6,576,1]{2,1,3,0:T(8,128)}, bf16[6,576,6,64]{1,3,2,0:T(8,128)(2,1)}, pred[6,576]{1,0...) while((s32[]{:T(128)}, ...), condition=%wide.region_5.6_spmd, body=%wide.region_2.5_spmd.sunk | while | flops 531722880 | bytes 25976228 | solution.py:149
  109.3 3.9 fusion.209
  119.3 3.9 fusion.209
  129.2 3.9 fusion.209
  139.1 4.0 fusion.209
  149.0 4.0 fusion.209
  159.0 4.0 fusion.209
  162.9 4.5 fusion.163
  176.8 56.4 %all-gather.6.cloned.1.call-done = bf16[2,192,8,384]{3,2,1,0:T(8,128)(2,1)} async-done(((bf16[2,6,8,384]{3,2,1,0:T(8,128)(2,1)}), bf16[2,192,8,384]{3,2,1,0:T(8,128)(2,1)}) %all-gather.6.cloned.1.call-update) | async-done | bytes 2359312 | tf_op jit(solution)/shard_map/all_gather | solution.py:74
  244.1 3.8 all-to-all-start
  248.6 52.5 %all-to-all-done = bf16[32,2,6,8,384]{4,3,2,1,0:T(8,128)(2,1)} async-done(((bf16[32,2,6,8,384]{4,3,2,1,0:T(8,128)(2,1)}), bf16[32,2,6,8,384]{4,3,2,1,0:T(8,128)(2,1)}, u32[]{:S(2)}, u32[]{:S(2)}) %all-to-all-start) | async-done | bytes 2359328 | tf_op jit(solution)/shard_map/all_to_all | solution.py:68
  304.0 3.4 fusion.141
  309.8 7.8 %multiply_reduce_fusion.1 = (f32[384]{0:T(512)S(1)}, f32[6,576]{1,0:T(8,128)S(1)}, f32[6,576]{1,0:T(8,128)S(1)}, f32[384]{0:T(512)S(1)}, f32[6,576,384]{2,1,0:T(8,128)}) fusion(f32[6,576,384]{2,1,0:T(8,128)} %copy-done.2, f32[6,576]{1,0:T(8,128)S(1)} %add_rsqrt_fusion, f32[6,576]{1,0:T(8,128)S(1)} %broadcast_multiply_fusion.4, f32[384]{0:T(512)S(1)} %slice.108, ...), kind=kOutput, calls=%fused_computation.93 | convolution fusion | flops 34694024 | bytes 16336896 | tf_op jit(solution)/shard_map/bpe,ed->bpd/dot_general | solution.py:200
  317.8 5.8 %convert_reduce_fusion.2 = (f32[384]{0:T(512)S(1)}, f32[6,576,384]{2,1,0:T(8,128)S(1)}) fusion(f32[6,576]{1,0:T(8,128)S(1)} %get-tuple-element.204, f32[6,576,384]{2,1,0:T(8,128)} %copy-done.2, f32[6,576]{1,0:T(8,128)S(1)} %broadcast_multiply_fusion.4, f32[6,576]{1,0:T(8,128)S(1)} %get-tuple-element.205, f32[6,576,384]{2,1,0:T(8,128)} %get-tuple-element.198, ...), kind=kLoop, calls=%fused_computation.92 | loop fusion | flops 15924864 | bytes 18637824 | tf_op jit(solution)/shard_map/reduce_sum | solution.py:210
  327.8 4.3 convolution_convert_fusion
  332.1 3.6 copy.73
  340.2 117.0 %while.27 = (s32[]{:T(128)}, bf16[6,576,6,64]{1,3,2,0:T(8,128)(2,1)}, bf16[6,576,6,64]{1,3,2,0:T(8,128)(2,1)}, bf16[6,576,6,64]{1,3,2,0:T(8,128)(2,1)S(1)}, bf16...) while((s32[]{:T(128)}, ...), condition=%wide.region_19.20_spmd, body=%wide.region_17.19_spmd.sunk | while | flops 1304982144 | bytes 65631612 | solution.py:214
  343.7 3.3 fusion.221
  347.0 4.2 multiply_reduce_fusion.9
  363.1 3.3 fusion.221
  366.5 4.2 multiply_reduce_fusion.9
  382.6 3.3 fusion.221
  385.9 4.2 multiply_reduce_fusion.9
  402.0 3.3 fusion.221
  405.4 4.2 multiply_reduce_fusion.9
  412.2 3.3 fusion.220
  421.5 3.3 fusion.221
  424.8 4.2 multiply_reduce_fusion.9
  441.0 3.3 fusion.221
  444.3 4.2 multiply_reduce_fusion.9
  457.2 5.6 %copy.74 = bf16[6,576,384]{2,1,0:T(8,128)(2,1)} copy(bf16[6,576,384]{1,2,0:T(8,128)(2,1)} %bitcast.272) | data formatting | bytes 5308416 | tf_op jit(solution)/shard_map/reshape | solution.py:219
  462.8 5.3 copy.75
  470.7 5.6 %copy.76 = bf16[6,576,384]{2,1,0:T(8,128)(2,1)} copy(bf16[6,576,384]{1,2,0:T(8,128)(2,1)} %bitcast.268) | data formatting | bytes 5308416 | tf_op jit(solution)/shard_map/reshape | solution.py:221
  476.4 9.0 %fusion.83 = bf16[1152,384]{1,0:T(8,128)(2,1)} fusion(bf16[6,576,384]{2,1,0:T(8,128)(2,1)} %copy.76, bf16[6,576,384]{2,1,0:T(8,128)(2,1)} %copy.75, bf16[6,576,384]{2,1,0:T(8,128)(2,1)} %copy.74, bf16[6,576,384]{2,1,0:T(8,128)(2,1)S(1)} %copy-done.5, f32[384]{0:T(512)S(1)} %copy-done.39, f32[384]{0:T(512)S(1)} %copy-done.37, f32[6,576]{1,0:T(8,128)S(1)} %copy-done.31, ...), kind=kOutput, calls=%fused_computation.106 | convolution fusion | flops 3089940480 | bytes 11532288 | tf_op jit(solution)/shard_map/bpd,bpe->ed/dot_general | solution.py:225
  485.3 7.7 %fusion.76 = (f32[384]{0:T(512)S(1)}, f32[6,576]{1,0:T(8,128)}, f32[6,576]{1,0:T(8,128)}, f32[384]{0:T(512)S(1)}, f32[6,576,384]{2,1,0:T(8,128)}) fusion(bf16[6,576,384]{2,1,0:T(8,128)(2,1)S(1)} %copy-done.5, f32[6,576]{1,0:T(8,128)S(1)} %copy-done.31, f32[6,576]{1,0:T(8,128)S(1)} %copy-done.27, f32[384]{0:T(512)S(1)} %copy-done.37, ...), kind=kOutput, calls=%fused_computation.87 | convolution fusion | flops 3094798336 | bytes 16883712 | tf_op jit(solution)/shard_map/bpe,ed->bpd/dot_general | solution.py:229
  494.0 4.5 all-to-all-start.2
  500.8 5.1 all-to-all-done.2
  505.9 3.4 all-to-all-start.1
  515.8 4.9 add_convert_fusion
  520.7 6.9 %fusion.75 = bf16[6,576,384]{2,1,0:T(8,128)(2,1)} fusion(f32[6,576,384]{2,1,0:T(8,128)} %copy-done.3, bf16[6,576,384]{2,1,0:T(8,128)(2,1)S(1)} %copy-done.5, f32[6,576,384]{2,1,0:T(8,128)} %get-tuple-element.199, f32[6,576]{1,0:T(8,128)S(1)} %broadcast_multiply_fusion, f32[6,576]{1,0:T(8,128)S(1)} %broadcast_multiply_fusion.1, f32[384]{0:T(512)S(1)} %copy-done.37, ...), kind=kLoop, calls=%fused_computation.86 | loop fusion | flops 13271040 | bytes 15982080 | tf_op jit(solution)/shard_map/convert_element_type | solution.py:234
  530.1 6.9 %all-to-all-done.1 = bf16[32,48,384]{2,1,0:T(8,128)(2,1)} async-done(((bf16[32,48,384]{2,1,0:T(8,128)(2,1)}), bf16[32,48,384]{2,1,0:T(8,128)(2,1)}, u32[]{:S(2)}, u32[]{:S(2)}) %all-to-all-start.1) | async-done | bytes 1179680 | tf_op jit(solution)/shard_map/all_to_all | solution.py:68
  (221 shorter events, 168.6 us)
Async XLA Ops:
  7.2 227.9 %copy-start = (bf16[8,384,48]{1,2,0:T(8,128)(2,1)S(1)}, bf16[8,384,48]{1,2,0:T(8,128)(2,1)}, u32[]{:S(2)}) copy-start(bf16[8,384,48]{1,2,0:T(8,128)(2,1)} %param.21) | copy-start | bytes 884740
  7.2 48.3 %copy-start.4 = (bf16[6,576,384]{2,1,0:T(8,128)(2,1)S(1)}, bf16[6,576,384]{2,1,0:T(8,128)(2,1)}, u32[]{:S(2)}) copy-start(bf16[6,576,384]{2,1,0:T(8,128)(2,1)} %param.15) | copy-start | bytes 7962628
  7.2 60.6 %all-gather.4.cloned.1.call-start = ((), (), s32[]{:S(2)}) async-start(), calls=%async_computation.3 | async-start | bytes 1216512 | tf_op jit(solution)/shard_map/all_gather | solution.py:130
  7.9 225.3 %all-gather.6.cloned.1.call-start = ((), (), s32[]{:S(2)}) async-start(), calls=%async_computation.4 | async-start | bytes 2433024 | tf_op jit(solution)/shard_map/all_gather | solution.py:74
  51.7 25.7 %copy-start.38 = (f32[384]{0:T(512)}, f32[384]{0:T(512)S(1)}, u32[]{:S(2)}) copy-start(f32[384]{0:T(512)S(1)} %slice.97) | copy-start | bytes 4612
  52.0 25.3 %copy-start.36 = (f32[384]{0:T(512)}, f32[384]{0:T(512)S(1)}, u32[]{:S(2)}) copy-start(f32[384]{0:T(512)S(1)} %slice.94) | copy-start | bytes 4612
  55.5 21.9 %copy-start.26 = (f32[6,576]{1,0:T(8,128)}, f32[6,576]{1,0:T(8,128)S(1)}, u32[]{:S(2)}) copy-start(f32[6,576]{1,0:T(8,128)S(1)} %broadcast_multiply_fusion.5) | copy-start | bytes 41476
  56.9 20.4 %copy-start.30 = (f32[6,576]{1,0:T(8,128)}, f32[6,576]{1,0:T(8,128)S(1)}, u32[]{:S(2)}) copy-start(f32[6,576]{1,0:T(8,128)S(1)} %add_rsqrt_fusion.1) | copy-start | bytes 41476
  167.4 2.5 copy-start.2
  169.9 6.9 %copy-start.40 = (bf16[8,48]{1,0:T(8,128)(2,1)S(1)}, bf16[8,48]{1,0:T(8,128)(2,1)}, u32[]{:S(2)}) copy-start(bf16[8,48]{1,0:T(8,128)(2,1)} %param.22) | copy-start | bytes 2308
  170.7 64.4 %copy-start.12 = (f32[6,576,8]{1,2,0:T(8,128)}, f32[6,576,8]{1,2,0:T(8,128)S(1)}, u32[]{:S(2)}) copy-start(f32[6,576,8]{1,2,0:T(8,128)S(1)} %fusion.168) | copy-start | bytes 331780
  173.3 136.5 %copy-start.24 = (f32[6,576]{1,0:T(8,128)}, f32[6,576]{1,0:T(8,128)S(1)}, u32[]{:S(2)}) copy-start(f32[6,576]{1,0:T(8,128)S(1)} %get-tuple-element.192) | copy-start | bytes 41476
  235.1 1.3 copy-start.10
  235.1 3.2 copy-start.11
  235.1 1.9 copy-start.29
  236.4 0.7 copy-start.20
  240.3 0.7 copy-start.22
  244.1 57.1 %all-to-all-start = ((bf16[32,2,6,8,384]{4,3,2,1,0:T(8,128)(2,1)}), bf16[32,2,6,8,384]{4,3,2,1,0:T(8,128)(2,1)}, u32[]{:S(2)}, u32[]{:S(2)}) async-start(bf16[32,2,6,8,384]{4,3,2,1,0:T(8,128)(2,1)} %copy.72), calls=%async_computation | async-start | bytes 4718592 | tf_op jit(solution)/shard_map/all_to_all | solution.py:68
  247.9 59.5 %copy-start.33 = (f32[8,384]{1,0:T(8,128)}, f32[8,384]{1,0:T(8,128)S(1)}, u32[]{:S(2)}) copy-start(f32[8,384]{1,0:T(8,128)S(1)} %reshape.176) | copy-start | bytes 36868
  303.2 5.1 copy-start.18
  303.2 4.2 copy-start.8
  309.8 8.0 %copy-start.9 = (bf16[6,576,384]{2,1,0:T(8,128)(2,1)S(1)}, bf16[6,576,384]{2,1,0:T(8,128)(2,1)}, u32[]{:S(2)}) copy-start(bf16[6,576,384]{2,1,0:T(8,128)(2,1)} %param.25) | copy-start | bytes 7962628
  317.8 8.2 %copy-start.7 = (bf16[6,576,6,64]{1,3,2,0:T(8,128)(2,1)S(1)}, bf16[6,576,6,64]{1,3,2,0:T(8,128)(2,1)}, u32[]{:S(2)}) copy-start(bf16[6,576,6,64]{1,3,2,0:T(8,128)(2,1)} %get-tuple-element.102) | copy-start | bytes 7962628
  323.6 2.3 copy-start.3
  457.2 5.6 %copy-start.6 = (bf16[6,576,6,64]{1,3,2,0:T(8,128)(2,1)}, bf16[6,576,6,64]{1,3,2,0:T(8,128)(2,1)S(1)}, u32[]{:S(2)}) copy-start(bf16[6,576,6,64]{1,3,2,0:T(8,128)(2,1)S(1)} %get-tuple-element.106) | copy-start | bytes 7962628
  468.1 8.1 %copy-start.5 = (bf16[6,576,384]{2,1,0:T(8,128)(2,1)S(1)}, bf16[6,576,384]{2,1,0:T(8,128)(2,1)}, u32[]{:S(2)}) copy-start(bf16[6,576,384]{2,1,0:T(8,128)(2,1)} %param.15) | copy-start | bytes 7962628
  468.1 8.2 %copy-start.27 = (f32[6,576]{1,0:T(8,128)S(1)}, f32[6,576]{1,0:T(8,128)}, u32[]{:S(2)}) copy-start(f32[6,576]{1,0:T(8,128)} %copy-done.26) | copy-start | bytes 41476
  468.1 8.2 %copy-start.31 = (f32[6,576]{1,0:T(8,128)S(1)}, f32[6,576]{1,0:T(8,128)}, u32[]{:S(2)}) copy-start(f32[6,576]{1,0:T(8,128)} %copy-done.30) | copy-start | bytes 41476
  468.1 8.2 %copy-start.37 = (f32[384]{0:T(512)S(1)}, f32[384]{0:T(512)}, u32[]{:S(2)}) copy-start(f32[384]{0:T(512)} %copy-done.36) | copy-start | bytes 4612
  468.1 8.2 %copy-start.39 = (f32[384]{0:T(512)S(1)}, f32[384]{0:T(512)}, u32[]{:S(2)}) copy-start(f32[384]{0:T(512)} %copy-done.38) | copy-start | bytes 4612
  476.3 9.0 %copy-start.14 = (bf16[6,576,384]{2,1,0:T(8,128)(2,1)S(1)}, bf16[6,576,384]{2,1,0:T(8,128)(2,1)}, u32[]{:S(2)}) copy-start(bf16[6,576,384]{2,1,0:T(8,128)(2,1)} %copy.74) | copy-start | bytes 7962628
  476.3 9.0 %copy-start.15 = (bf16[6,576,384]{2,1,0:T(8,128)(2,1)S(1)}, bf16[6,576,384]{2,1,0:T(8,128)(2,1)}, u32[]{:S(2)}) copy-start(bf16[6,576,384]{2,1,0:T(8,128)(2,1)} %copy.75) | copy-start | bytes 7962628
  476.3 9.0 %copy-start.16 = (bf16[6,576,384]{2,1,0:T(8,128)(2,1)S(1)}, bf16[6,576,384]{2,1,0:T(8,128)(2,1)}, u32[]{:S(2)}) copy-start(bf16[6,576,384]{2,1,0:T(8,128)(2,1)} %copy.76) | copy-start | bytes 7962628
  476.3 9.0 %copy-start.17 = (bf16[1536,384]{1,0:T(8,128)(2,1)S(1)}, bf16[1536,384]{1,0:T(8,128)(2,1)}, u32[]{:S(2)}) copy-start(bf16[1536,384]{1,0:T(8,128)(2,1)} %all-gather.4.cloned.1.call-done) | copy-start | bytes 3538948
  485.3 7.9 %copy-start.35 = (f32[32,96]{1,0:T(8,128)S(1)}, f32[32,96]{1,0:T(8,128)}, u32[]{:S(2)}) copy-start(f32[32,96]{1,0:T(8,128)} %reshape_reshape.12) | copy-start | bytes 36868
  493.1 16.2 %copy-start.21 = (bf16[192,8,48]{0,2,1:T(8,128)(2,1)S(1)}, bf16[192,8,48]{0,2,1:T(8,128)(2,1)}, u32[]{:S(2)}) copy-start(bf16[192,8,48]{0,2,1:T(8,128)(2,1)} %copy-done.20) | copy-start | bytes 442372
  494.0 21.8 %copy-start.13 = (f32[6,576,8]{1,2,0:T(8,128)S(1)}, f32[6,576,8]{1,2,0:T(8,128)}, u32[]{:S(2)}) copy-start(f32[6,576,8]{1,2,0:T(8,128)} %copy-done.12) | copy-start | bytes 331780
  494.0 21.8 %copy-start.19 = (f32[2,6,8,384]{3,2,1,0:T(8,128)S(1)}, f32[2,6,8,384]{3,2,1,0:T(8,128)}, u32[]{:S(2)}) copy-start(f32[2,6,8,384]{3,2,1,0:T(8,128)} %copy-done.18) | copy-start | bytes 442372
  494.0 21.8 %copy-start.25 = (f32[6,576]{1,0:T(8,128)S(1)}, f32[6,576]{1,0:T(8,128)}, u32[]{:S(2)}) copy-start(f32[6,576]{1,0:T(8,128)} %copy-done.24) | copy-start | bytes 41476
  494.0 21.8 %copy-start.34 = (f32[8,384]{1,0:T(8,128)S(1)}, f32[8,384]{1,0:T(8,128)}, u32[]{:S(2)}) copy-start(f32[8,384]{1,0:T(8,128)} %copy-done.33) | copy-start | bytes 36868
  494.0 11.9 %all-to-all-start.2 = ((f32[32,1,264]{2,1,0:T(1,128)}), f32[32,1,264]{2,1,0:T(1,128)}, u32[]{:S(2)}, u32[]{:S(2)}) async-start(f32[32,1,264]{2,1,0:T(1,128)} %all_to_all.14), calls=%async_computation.2 | async-start | bytes 98304 | tf_op jit(solution)/shard_map/all_to_all | solution.py:244
  500.8 11.0 %copy-start.23 = (bf16[192,8,48]{0,2,1:T(8,128)(2,1)S(1)}, bf16[192,8,48]{0,2,1:T(8,128)(2,1)}, u32[]{:S(2)}) copy-start(bf16[192,8,48]{0,2,1:T(8,128)(2,1)} %copy-done.22) | copy-start | bytes 442372
  505.9 31.1 %all-to-all-start.1 = ((bf16[32,48,384]{2,1,0:T(8,128)(2,1)}), bf16[32,48,384]{2,1,0:T(8,128)(2,1)}, u32[]{:S(2)}, u32[]{:S(2)}) async-start(bf16[32,48,384]{2,1,0:T(8,128)(2,1)} %bitcast.275), calls=%async_computation.1 | async-start | bytes 2359296 | tf_op jit(solution)/shard_map/all_to_all | solution.py:68
  514.3 6.4 %copy-start.28 = (f32[6,576]{1,0:T(8,128)S(1)}, f32[6,576]{1,0:T(8,128)}, u32[]{:S(2)}) copy-start(f32[6,576]{1,0:T(8,128)} %copy-done.26) | copy-start | bytes 41476
  514.3 6.4 %copy-start.32 = (f32[6,576]{1,0:T(8,128)S(1)}, f32[6,576]{1,0:T(8,128)}, u32[]{:S(2)}) copy-start(f32[6,576]{1,0:T(8,128)} %copy-done.30) | copy-start | bytes 41476
  520.7 18.4 %copy-start.1 = (bf16[8,384,48]{1,2,0:T(8,128)(2,1)S(1)}, bf16[8,384,48]{1,2,0:T(8,128)(2,1)}, u32[]{:S(2)}) copy-start(bf16[8,384,48]{1,2,0:T(8,128)(2,1)} %param.21) | copy-start | bytes 884740
Sparse Core Ops, SparseCore 0:
  10.8 56.9 all-gather.3
  176.9 56.2 all-gather.5

commit v2 on v1

v2 whole, which is shorter than its diff:
```python
import jax
import jax.numpy as jnp
from jax import lax
from jax.experimental import pallas as pl
from jax.experimental.pallas import tpu as pltpu
from jax.sharding import PartitionSpec as P

HEAD_DIM = 64
PAIR = 2 * HEAD_DIM
MASKED = -1000000000.0
AXES = ("wide", "narrow")
BF16 = jnp.bfloat16
F32 = jnp.float32
VMEM_LIMIT = 60 * 1024 * 1024
GAIN1, GAIN2, BIAS1, VBIAS, OBIAS, BIAS2 = range(6)


def dot(left, right, left_dim, right_dim):
    return lax.dot_general(
        left, right, (((left_dim,), (right_dim,)), ((), ())), preferred_element_type=F32
    )


def normalize(values):
    centred = values - jnp.mean(values, axis=-1, keepdims=True)
    factor = lax.rsqrt(jnp.mean(centred * centred, axis=-1, keepdims=True) + 1e-06)
    return (centred * factor, factor)


def norm_back(grad_hat, normed, factor):
    return factor * (
        grad_hat
        - jnp.mean(grad_hat, axis=-1, keepdims=True)
        - normed * jnp.mean(grad_hat * normed, axis=-1, keepdims=True)
    )


def smooth(values):
    return jax.nn.gelu(values, approximate=False)


def lower_half(shape):
    return lax.broadcasted_iota(jnp.int32, shape, 1) < HEAD_DIM


def own_half(low, head, own, other):
    return jnp.where(low, own, other) if head % 2 == 0 else jnp.where(low, other, own)


def forward_image(x, g, valid_row, wt, vec, table, q_ref, k_ref, v_ref, p_ref, att_ref, inv_ref):
    patches, width = x.shape
    heads = width // HEAD_DIM
    images = x.astype(F32)
    normed, _ = normalize(images)
    first = (normed * vec[GAIN1 : GAIN1 + 1] + vec[BIAS1 : BIAS1 + 1]).astype(BF16)
    q_ref[...] = (dot(first, wt[:width], 1, 1) * HEAD_DIM ** (-0.5)).astype(BF16)
    k_ref[...] = dot(first, wt[width : 2 * width], 1, 1).astype(BF16)
    v_ref[...] = (dot(first, wt[2 * width : 3 * width], 1, 1) + vec[VBIAS : VBIAS + 1]).astype(BF16)
    bias_row = jnp.where(valid_row > 0, 0.0, MASKED).astype(F32)
    fill = jnp.broadcast_to(bias_row * (1.0 / HEAD_DIM), (PAIR, patches)).T.astype(BF16)
    low = lower_half((patches, PAIR))
    one = jnp.ones((patches, PAIR), BF16)
    scores = {}

    def pair_of(ref, head):
        at = head // 2 * PAIR
        return ref[:, at : at + PAIR]

    def score(head):
        scores[head] = dot(
            own_half(low, head, pair_of(q_ref, head), one),
            own_half(low, head, pair_of(k_ref, head), fill),
            1,
            1,
        )

    sums = {}
    score(0)
    for head in range(heads):
        if head + 1 < heads:
            score(head + 1)
        raw = scores.pop(head)
        prob = jnp.exp(raw - jnp.max(raw, axis=1, keepdims=True)).astype(BF16)
        p_ref[head] = prob
        sums[head] = dot(prob, own_half(low, head, pair_of(v_ref, head), one), 1, 0)
        if head % 2 == 1:
            even, odd = sums.pop(head - 1), sums.pop(head)
            inverse = 1.0 / pltpu.roll(jnp.where(low, odd, even), HEAD_DIM, 1)
            at = head // 2 * PAIR
            inv_ref[:, at : at + PAIR] = inverse
            att_ref[:, at : at + PAIR] = (jnp.where(low, even, odd) * inverse).astype(BF16)
    branch = dot(att_ref[...], wt[3 * width :], 1, 1)
    middle = images + branch + vec[OBIAS : OBIAS + 1]
    normed, _ = normalize(middle)
    second = (normed * vec[GAIN2 : GAIN2 + 1] + vec[BIAS2 : BIAS2 + 1]).astype(BF16)
    logits = dot(table, second, 1, 1)
    masked = jnp.where(valid_row > 0, logits, MASKED)
    dispatch = jnp.exp(masked - jnp.max(masked, axis=1, keepdims=True))
    dispatch = dispatch / jnp.sum(dispatch, axis=1, keepdims=True)
    combine = jnp.exp(logits - jnp.max(logits, axis=0, keepdims=True))
    combine = combine / jnp.sum(combine, axis=0, keepdims=True)
    slots = dot(dispatch.astype(BF16), second, 1, 0).astype(BF16)
    produced_grad = dot(combine.astype(BF16), g, 1, 0).astype(BF16)
    return middle, second, dispatch, combine, slots, produced_grad


def backward_image(
    x, g, middle, second, dispatch, combine, produced, slot_grad, wt, vec, table,
    q_ref, k_ref, v_ref, p_ref, att_ref, inv_ref, ds_ref, grad_t_ref, grad_ref,
):
    patches, width = x.shape
    heads = width // HEAD_DIM
    combine_low = combine.astype(BF16)
    dispatch_low = dispatch.astype(BF16)
    mixed = (middle + dot(combine_low, produced, 0, 0)).astype(BF16)
    combine_grad = dot(produced, g, 1, 1)
    dispatch_grad = dot(slot_grad, second, 1, 1)
    logit_grad = dispatch * (
        dispatch_grad - jnp.sum(dispatch * dispatch_grad, axis=1, keepdims=True)
    ) + combine * (combine_grad - jnp.sum(combine * combine_grad, axis=0, keepdims=True))
    logit_grad = logit_grad.astype(BF16)
    table_grad = dot(logit_grad, second, 1, 0)
    second_grad = dot(
        jnp.concatenate([dispatch_low, logit_grad], axis=0),
        jnp.concatenate([slot_grad, table], axis=0),
        0,
        0,
    )
    normed, factor = normalize(middle)
    gain_two = jnp.sum(second_grad * normed, axis=0, keepdims=True)
    shift_two = jnp.sum(second_grad, axis=0, keepdims=True)
    middle_grad = g.astype(F32) + norm_back(second_grad * vec[GAIN2 : GAIN2 + 1], normed, factor)
    branch_grad = middle_grad.astype(BF16)
    branch_shift = jnp.sum(branch_grad.astype(F32), axis=0, keepdims=True)
    output_grad = dot(branch_grad.T, att_ref[...], 1, 0)
    attended_grad = dot(branch_grad, wt[3 * width :], 1, 0).astype(BF16).astype(F32)
    scaled = attended_grad * inv_ref[...]
    drop = -(scaled * att_ref[...].astype(F32))
    scaled = scaled.astype(BF16)
    scaled_t = scaled.T
    query_t = q_ref[...].T
    low = lower_half((patches, PAIR))
    one = jnp.ones((patches, PAIR), BF16)
    prob_grads = {}

    def pair_of(ref, head):
        at = head // 2 * PAIR
        return ref[:, at : at + PAIR]

    def prob_grad(head):
        rolled = pltpu.roll(pair_of(drop, head), HEAD_DIM, 1).astype(BF16)
        prob_grads[head] = dot(
            own_half(low, head, pair_of(scaled, head), rolled),
            own_half(low, head, pair_of(v_ref, head), one),
            1,
            1,
        )

    query_grads = {}
    prob_grad(0)
    for head in range(heads):
        if head + 1 < heads:
            prob_grad(head + 1)
        rows = slice(head * HEAD_DIM, (head + 1) * HEAD_DIM)
        prob = p_ref[head]
        grad_t_ref[2 * width + rows.start : 2 * width + rows.stop, :] = dot(
            scaled_t[rows], prob, 1, 0
        ).astype(BF16)
        score_grad = (prob.astype(F32) * prob_grads.pop(head)).astype(BF16)
        ds_ref[head % 2] = score_grad
        score_grad = ds_ref[head % 2]
        query_grads[head] = dot(score_grad, pair_of(k_ref, head), 1, 0)
        grad_t_ref[width + rows.start : width + rows.stop, :] = dot(
            query_t[rows], score_grad, 1, 0
        ).astype(BF16)
        if head % 2 == 1:
            both = jnp.where(low, query_grads.pop(head - 1), query_grads.pop(head))
            at = head // 2 * PAIR
            grad_ref[:, at : at + PAIR] = (both * HEAD_DIM ** (-0.5)).astype(BF16)
    grad_t_ref[:width, :] = grad_ref[:, :width].T
    grad_ref[:, width:] = grad_t_ref[width:, :].T
    normed, factor = normalize(x.astype(F32))
    first = (normed * vec[GAIN1 : GAIN1 + 1] + vec[BIAS1 : BIAS1 + 1]).astype(BF16)
    front_grad = dot(grad_t_ref[...], first, 1, 0)
    value_shift = jnp.sum(grad_ref[:, 2 * width :].astype(F32), axis=0, keepdims=True)
    first_grad = dot(grad_ref[...], wt[: 3 * width], 1, 0)
    gain_one = jnp.sum(first_grad * normed, axis=0, keepdims=True)
    shift_one = jnp.sum(first_grad, axis=0, keepdims=True)
    patch_grad = middle_grad + norm_back(first_grad * vec[GAIN1 : GAIN1 + 1], normed, factor)
    rows = jnp.concatenate(
        [gain_one, gain_two, shift_one, value_shift, branch_shift, shift_two, jnp.zeros((2, width), F32)],
        axis=0,
    )
    return mixed, patch_grad.astype(BF16), front_grad, output_grad, rows, table_grad


def forward_kernel(
    x, g, valid, wt, vec, table,
    q, k, v, p, att, inv, middle, second, dispatch, combine, slots, produced_grad,
):
    got = forward_image(
        x[0], g[0], valid[0], wt[...], vec[...], table[...],
        q.at[0], k.at[0], v.at[0], p.at[0], att.at[0], inv.at[0],
    )
    for ref, value in zip((middle, second, dispatch, combine, slots, produced_grad), got):
        ref[0] = value


def backward_kernel(
    x, g, middle, second, dispatch, combine, produced, slot_grad, wt, vec, table,
    q, k, v, p, att, inv,
    mixed, patch_grad, weight_grad, rows, table_grad,
    ds, grad_t, grad,
):
    @pl.when(pl.program_id(0) == 0)
    def _():
        weight_grad[...] = jnp.zeros_like(weight_grad)
        rows[...] = jnp.zeros_like(rows)
        table_grad[...] = jnp.zeros_like(table_grad)

    width = x.shape[-1]
    got = backward_image(
        x[0], g[0], middle[0], second[0], dispatch[0], combine[0], produced[0], slot_grad[0],
        wt[...], vec[...], table[...],
        q.at[0], k.at[0], v.at[0], p.at[0], att.at[0], inv.at[0], ds, grad_t, grad,
    )
    mixed[0] = got[0]
    patch_grad[0] = got[1]
    weight_grad[: 3 * width, :] += got[2]
    weight_grad[3 * width :, :] += got[3]
    rows[...] += got[4]
    table_grad[...] += got[5]


def per_image(*shape):
    return pl.BlockSpec((1,) + shape, lambda i: (i,) + (0,) * len(shape))


def whole(*shape):
    return pl.BlockSpec(shape, lambda i: (0,) * len(shape))


def run_forward(x, g, valid, wt, vec, table):
    count, patches, width = x.shape
    heads = width // HEAD_DIM
    experts = table.shape[0]
    flat = (patches, width)
    outs = [
        (flat, BF16), (flat, BF16), (flat, BF16), ((heads, patches, patches), BF16),
        (flat, BF16), (flat, F32), (flat, F32), (flat, BF16),
        ((experts, patches), F32), ((experts, patches), F32),
        ((experts, width), BF16), ((experts, width), BF16),
    ]
    return pl.pallas_call(
        forward_kernel,
        grid=(count,),
        in_specs=[
            per_image(*flat), per_image(*flat), per_image(1, patches),
            whole(*wt.shape), whole(*vec.shape), whole(*table.shape),
        ],
        out_specs=[per_image(*shape) for shape, _ in outs],
        out_shape=[jax.ShapeDtypeStruct((count,) + shape, kind) for shape, kind in outs],
        compiler_params=pltpu.CompilerParams(vmem_limit_bytes=VMEM_LIMIT),
        name="forward",
    )(x, g, valid, wt, vec, table)


def run_backward(x, g, kept, produced, slot_grad, wt, vec, table):
    count, patches, width = x.shape
    heads = width // HEAD_DIM
    experts = table.shape[0]
    flat = (patches, width)
    q, k, v, p, att, inv, middle, second, dispatch, combine = kept
    return pl.pallas_call(
        backward_kernel,
        grid=(count,),
        in_specs=[
            per_image(*flat), per_image(*flat), per_image(*flat), per_image(*flat),
            per_image(experts, patches), per_image(experts, patches),
            per_image(experts, width), per_image(experts, width),
            whole(*wt.shape), whole(*vec.shape), whole(*table.shape),
            per_image(*flat), per_image(*flat), per_image(*flat),
            per_image(heads, patches, patches), per_image(*flat), per_image(*flat),
        ],
        out_specs=[
            per_image(*flat), per_image(*flat),
            whole(4 * width, width), whole(8, width), whole(experts, width),
        ],
        out_shape=[
            jax.ShapeDtypeStruct(x.shape, BF16), jax.ShapeDtypeStruct(x.shape, BF16),
            jax.ShapeDtypeStruct((4 * width, width), F32), jax.ShapeDtypeStruct((8, width), F32),
            jax.ShapeDtypeStruct((experts, width), F32),
        ],
        scratch_shapes=[
            pltpu.VMEM((2, patches, patches), BF16),
            pltpu.VMEM((3 * width, patches), BF16),
            pltpu.VMEM((patches, 3 * width), BF16),
        ],
        compiler_params=pltpu.CompilerParams(vmem_limit_bytes=VMEM_LIMIT),
        name="backward",
    )(x, g, middle, second, dispatch, combine, produced, slot_grad, wt, vec, table, q, k, v, p, att, inv)


def scatter_sum(parts):
    got = lax.all_to_all(parts.astype(BF16), AXES, 0, 0, tiled=True)
    return jnp.sum(got.astype(F32), axis=0)


def experts_at_home(slots, produced_grad, expert_in, expert_in_bias, expert_out, devices):
    local_images, experts, width = slots.shape
    every = lax.all_gather(jnp.stack([slots, produced_grad]), AXES, axis=1, tiled=True)
    all_slots, all_grads = every[0], every[1]
    hidden = jnp.einsum(
        "bed,edf->bef", all_slots, expert_in, preferred_element_type=F32
    ) + expert_in_bias.astype(F32)
    active, gelu_back = jax.vjp(smooth, hidden)
    active = active.astype(BF16)
    partial = jnp.einsum("bef,efd->bed", active, expert_out, preferred_element_type=F32)
    active_grad = jnp.einsum("bed,efd->bef", all_grads, expert_out, preferred_element_type=F32)
    hidden_grad = gelu_back(active_grad)[0].astype(BF16)
    partial_back = jnp.einsum("bef,edf->bed", hidden_grad, expert_in, preferred_element_type=F32)
    contract_grad = jnp.einsum("bef,bed->efd", active, all_grads, preferred_element_type=F32)
    expand_grad = jnp.einsum("bed,bef->edf", all_slots, hidden_grad, preferred_element_type=F32)
    inner_grad = jnp.sum(hidden_grad.astype(F32), axis=0)
    both = jnp.stack([partial, partial_back]).reshape(2, devices, local_images, experts, width)
    both = scatter_sum(jnp.moveaxis(both, 1, 0))
    return (both[0], both[1], expand_grad, inner_grad, contract_grad)


def on_device(
    patches,
    valid,
    attn_weights,
    norm_gains,
    vec_biases,
    slot_params,
    expert_in,
    expert_in_bias,
    expert_out,
    expert_out_bias,
    out_grad,
):
    local_images, patch_count, width = patches.shape
    experts = expert_in.shape[0]
    devices = lax.axis_size("wide") * lax.axis_size("narrow")

    vectors = (norm_gains, vec_biases, slot_params, expert_out_bias)
    lengths = [v.shape[0] for v in vectors]
    small = lax.all_gather(jnp.concatenate(vectors), AXES)
    pieces = []
    at = 0
    for length in lengths:
        pieces.append(small[:, at : at + length].reshape(-1, width))
        at += length
    gains, biases, table, expert_shift = pieces
    vec = jnp.concatenate([gains, biases, jnp.zeros((2, width), BF16)]).astype(F32)
    wt = lax.all_gather(attn_weights.T, AXES, axis=0, tiled=True)

    *kept, slots, produced_grad = run_forward(
        patches, out_grad, valid.reshape(local_images, 1, patch_count), wt, vec, table
    )
    produced, slot_grad, expand_grad, inner_grad, contract_grad = experts_at_home(
        slots, produced_grad, expert_in, expert_in_bias, expert_out, devices
    )
    produced = (produced + expert_shift.astype(F32)).astype(BF16)
    slot_grad = slot_grad.astype(BF16)
    shift_grad = jnp.sum(produced_grad.astype(F32), axis=0)
    mixed_out, patch_grad, weight_grad, rows, table_grad = run_backward(
        patches, out_grad, kept, produced, slot_grad, wt, vec, table
    )
    weight_grad = scatter_sum(weight_grad.reshape(devices, -1, width)).T
    small_grads = jnp.concatenate(
        [v.reshape(devices, -1) for v in (rows[:2], rows[2:6], table_grad, shift_grad)], axis=1
    )
    small_grads = jnp.sum(lax.all_to_all(small_grads, AXES, 0, 0, tiled=True), axis=0)
    grads = []
    at = 0
    for length in lengths:
        grads.append(small_grads[at : at + length])
        at += length
    return (
        mixed_out,
        patch_grad,
        weight_grad,
        grads[0],
        grads[1],
        grads[2],
        expand_grad,
        inner_grad,
        contract_grad,
        grads[3],
    )


def solution(mesh):
    images = P(AXES, None, None)
    vector = P(AXES)
    second = P(None, AXES)
    return jax.shard_map(
        on_device,
        mesh=mesh,
        in_specs=(
            images, P(AXES, None), second, vector, vector, vector,
            P(None, None, AXES), second, P(None, AXES, None), vector, images,
        ),
        out_specs=(
            images, images, second, vector, vector, vector,
            P(None, None, AXES), second, P(None, AXES, None), vector,
        ),
        check_vma=False,
    )
```

time: 557 us -> 339 us (0.61); the launches traced: 546 us -> 337 us
  matrix products: 206 us -> 6.7 us
  Pallas kernels: 0 us -> 90.3 us
  other arithmetic: 73.8 us -> 7.96 us
  local copies, waits for them, and re-layouts: 63.9 us -> 13.1 us
  waiting for transfers between devices: 132 us -> 151 us
    dot_general x60 -> x3, matrix products: 201 us -> 2.99 us  [the longest x1 1.24 us: experts_at_home(): jnp.einsum('bef,bed->efd', active, all_grads, preferred_element_type=F32)]
    pallas_call x0 -> x2, Pallas kernels: none -> 90.3 us  [the longest x1 53.1 us: run_backward(): pl.pallas_call(backward_kernel, grid=(count,), in_specs=[per_image(*flat)...]
    reduce_sum x13 -> x3, other arithmetic: 30.6 us -> 1.14 us  [the longest x2 1.12 us: scatter_sum(): return jnp.sum(got.astype(F32), axis=0)]
    convert_element_type x14 -> x6, other arithmetic: 29 us -> 4.46 us  [the longest x2 3.08 us: scatter_sum(): got = lax.all_to_all(parts.astype(BF16), AXES, 0, 0, tiled=True)]
    all_to_all x2, waiting for transfers between devices: 59.4 us -> 76.5 us  [scatter_sum(): got = lax.all_to_all(parts.astype(BF16), AXES, 0, 0, tiled=True)]
    reshape x3 -> x8, local copies, waits for them, and re-layouts: 16.5 us -> 3.22 us  [the longest x1 1.35 us: on_device(): valid.reshape(local_images, 1, patch_count)]
    slice x11 -> x4, local copies, waits for them, and re-layouts: 14.4 us -> 1.5 us  [the longest x1 0.71 us: on_device(): rows[:2]]
    convert_element_type x4 -> x3, local copies, waits for them, and re-layouts: 10.7 us -> 2.35 us  [the longest x1 1.66 us: scatter_sum(): got = lax.all_to_all(parts.astype(BF16), AXES, 0, 0, tiled=True)]
  transfers between devices with their start and end apart: 5 -> 5, of which waited for: 5 -> 5; matrix products, arithmetic and copies ran while one was open for 6% -> 3% of each run, Pallas kernels for 0% -> 0%
where the time goes in v2:
time: 339 us; the launch traced here: 337 us
  waiting for transfers between devices  151 us (45%)
  Pallas kernels  90.3 us (27%)
  blocking collectives  42.2 us (12%)
  between operations  14.3 us (4%)
  local copies, waits for them, and re-layouts  13.1 us (4%)
  starting transfers between devices  10.9 us (3%)
  other arithmetic  7.96 us (2%)
  matrix products  6.7 us (2%)
    all_to_all x2, waiting for transfers between devices, scatter_sum(): got = lax.all_to_all(parts.astype(BF16), AXES, 0, 0, tiled=True)  76.5 us
    all_gather x1, waiting for transfers between devices, experts_at_home(): lax.all_gather(jnp.stack([slots, produced_grad]), AXES, axis=1, tiled=True)  56.5 us
    pallas_call x1, Pallas kernels, run_backward(): pl.pallas_call(backward_kernel, grid=(count,), in_specs=[per_image(*flat)...  53.1 us
    unnamed x1, blocking collectives  42.2 us
    pallas_call x1, Pallas kernels, run_forward(): pl.pallas_call(forward_kernel, grid=(count,), in_specs=[per_image(*flat),...  37.2 us
    all_gather x1, waiting for transfers between devices, on_device(): wt = lax.all_gather(attn_weights.T, AXES, axis=0, tiled=True)  13.3 us
  transfers between devices with their start and end apart: 5, of which 5 were waited for; matrix products, arithmetic and copies ran while one was open for 3% of the time, Pallas kernels for 0%

profile of v2, /device:TPU:0, one launch (start us, length us, event | category | flops | bytes accessed | tf_op | source)
XLA Modules:
  0.0 337.0 jit_solution(9194492146546976236)
XLA Ops:
  7.2 0.7 all-gather.4.cloned.1.call-update
  8.0 0.8 pad_maximum_fusion.2
  8.8 0.2 dynamic-update-slice
  9.0 42.2 %all-reduce = bf16[8448]{0:T(1024)(128)(2,1)S(1)} all-reduce(bf16[8448]{0:T(1024)(128)(2,1)S(1)} %dynamic-update-slice), channel_id=2, replica_groups=mesh['wide'=8,'narrow'=4] {'wide','narrow'}, use_global_device_ids=true, to_apply=%add | all-reduce | flops 8448 | bytes 33792
  51.2 0.1 reshape.74
  51.4 1.3 reshape.65.valid
  52.8 0.1 reshape.67
  52.9 0.1 reshape.66
  53.0 0.7 reshape.68.table
  53.7 0.1 pad.10.clone
  53.8 0.7 maximum_convert_fusion.vec
  54.5 13.3 %all-gather.4.cloned.1.call-done.wt = bf16[1536,384]{1,0:T(8,128)(2,1)} async-done(((bf16[48,384]{1,0:T(8,128)(2,1)}), bf16[1536,384]{1,0:T(8,128)(2,1)}) %all-gather.4.cloned.1.call-update) | async-done | bytes 1179664 | tf_op jit(solution)/shard_map/all_gather | solution.py:357
  67.8 37.2 %forward.1 = (bf16[6,576,384]{2,1,0:T(8,128)(2,1)}, bf16[6,576,384]{2,1,0:T(8,128)(2,1)}, bf16[6,576,384]{2,1,0:T(8,128)(2,1)}, bf16[6,6,576,576]{3,2,1,0:T(8,12...) custom-call(bf16[6,576,384]{2,1,0:T(8,128)(2,1)} %x.4, ...), custom_call_target="tpu_custom_call" | custom-call | tf_op jit(solution)/shard_map/forward/pallas_call | solution.py:254
  105.0 1.4 pad_maximum_fusion
  106.4 56.5 %all-gather.6.cloned.1.call-done = bf16[2,192,8,384]{3,2,1,0:T(8,128)(2,1)} async-done(((bf16[2,6,8,384]{3,2,1,0:T(8,128)(2,1)}), bf16[2,192,8,384]{3,2,1,0:T(8,128)(2,1)}) %all-gather.6.cloned.1.call-update) | async-done | bytes 2359312 | tf_op jit(solution)/shard_map/all_gather | solution.py:311
  162.9 1.9 slice_bitcast_fusion.1
  164.8 1.2 fusion.10
  166.1 0.5 fusion
  166.6 0.7 copy.32
  167.3 2.0 convert_reduce_fusion.2
  169.3 0.5 fusion.1
  169.8 0.7 copy.34
  170.5 0.3 maximum_bitcast_fusion
  170.8 1.7 copy.35
  172.4 3.7 %all-to-all-start = ((bf16[32,2,6,8,384]{4,3,2,1,0:T(8,128)(2,1)}), bf16[32,2,6,8,384]{4,3,2,1,0:T(8,128)(2,1)S(1)}, u32[]{:S(2)}, u32[]{:S(2)}) async-start(bf16[32,2,6,8,384]{4,3,2,1,0:T(8,128)(2,1)} %copy.35), calls=%async_computation | async-start | bytes 4718592 | tf_op jit(solution)/shard_map/all_to_all | solution.py:305
  176.3 53.0 %all-to-all-done = bf16[32,2,6,8,384]{4,3,2,1,0:T(8,128)(2,1)S(1)} async-done(((bf16[32,2,6,8,384]{4,3,2,1,0:T(8,128)(2,1)}), bf16[32,2,6,8,384]{4,3,2,1,0:T(8,128)(2,1)S(1)}, u32[]{:S(2)}, u32[]{:S(2)}) %all-to-all-start) | async-done | bytes 2359328 | tf_op jit(solution)/shard_map/all_to_all | solution.py:305
  229.2 0.3 convert_reduce_fusion
  229.6 0.6 fusion.33.slot_grad
  230.2 0.6 fusion.32.produced
  230.8 53.1 %backward.1 = (bf16[6,576,384]{2,1,0:T(8,128)(2,1)}, bf16[6,576,384]{2,1,0:T(8,128)(2,1)}, f32[1536,384]{1,0:T(8,128)}, f32[8,384]{1,0:T(8,128)}, f32[8,384]{1,0:T(8,128)}) custom-call(bf16[6,576,384]{2,1,0:T(8,128)(2,1)} %x.4, bf16[6,576,384]{2,1,0:T(8,128)(2,1)} %g.3, f32[6,576,384]{2,1,0:T(8,128)} %get-tuple-element.27.middle, ...), custom_call_target="tpu_custom_call" | custom-call | tf_op jit(solution)/shard_map/backward/pallas_call | solution.py:274
  283.9 0.7 slice.51
  284.6 0.7 slice.52
  285.3 0.1 reshape.70
  285.4 0.1 reshape.69
  285.5 0.8 reshape.71
  286.3 0.1 pad_maximum_fusion.1
  286.4 0.7 all_to_all.14
  287.0 4.3 %all-to-all-start.2 = ((f32[32,1,264]{2,1,0:T(1,128)}), f32[32,1,264]{2,1,0:T(1,128)S(1)}, u32[]{:S(2)}, u32[]{:S(2)}) async-start(f32[32,1,264]{2,1,0:T(1,128)} %all_to_all.14), calls=%async_computation.2 | async-start | bytes 98304 | tf_op jit(solution)/shard_map/all_to_all | solution.py:375
  291.4 2.8 convert_element_type.60
  294.2 4.6 %all-to-all-done.2 = f32[32,1,264]{2,1,0:T(1,128)S(1)} async-done(((f32[32,1,264]{2,1,0:T(1,128)}), f32[32,1,264]{2,1,0:T(1,128)S(1)}, u32[]{:S(2)}, u32[]{:S(2)}) %all-to-all-start.2) | async-done | bytes 33824 | tf_op jit(solution)/shard_map/all_to_all | solution.py:375
  298.8 2.8 all-to-all-start.1
  301.6 1.2 fusion.2
  302.8 1.2 fusion.5
  304.1 0.6 slice.54
  304.7 0.5 slice.53
  305.2 0.6 fusion.34
  305.8 23.5 %all-to-all-done.1 = bf16[32,48,384]{2,1,0:T(8,128)(2,1)S(1)} async-done(((bf16[32,48,384]{2,1,0:T(8,128)(2,1)}), bf16[32,48,384]{2,1,0:T(8,128)(2,1)S(1)}, u32[]{:S(2)}, u32[]{:S(2)}) %all-to-all-start.1) | async-done | bytes 1179680 | tf_op jit(solution)/shard_map/all_to_all | solution.py:305
  329.3 0.8 convert_reduce_fusion.1
  (31 shorter events, 0.5 us)
Async XLA Ops:
  7.2 157.6 %copy-start = (bf16[8,384,48]{1,2,0:T(8,128)(2,1)S(1)}, bf16[8,384,48]{1,2,0:T(8,128)(2,1)}, u32[]{:S(2)}) copy-start(bf16[8,384,48]{1,2,0:T(8,128)(2,1)} %param.17) | copy-start | bytes 884740
  7.2 60.6 %all-gather.4.cloned.1.call-start = ((), (), s32[]{:S(2)}) async-start(), calls=%async_computation.3 | async-start | bytes 1216512 | tf_op jit(solution)/shard_map/all_gather | solution.py:357
  7.9 155.0 %all-gather.6.cloned.1.call-start = ((), (), s32[]{:S(2)}) async-start(), calls=%async_computation.4 | async-start | bytes 2433024 | tf_op jit(solution)/shard_map/all_gather | solution.py:311
  54.5 52.0 %copy-start.8 = (bf16[8,48]{1,0:T(8,128)(2,1)S(1)}, bf16[8,48]{1,0:T(8,128)(2,1)}, u32[]{:S(2)}) copy-start(bf16[8,48]{1,0:T(8,128)(2,1)} %param.18) | copy-start | bytes 2308
  164.8 1.3 copy-start.2
  164.8 2.5 copy-start.4
  164.8 1.3 copy-start.6
  172.4 3.8 %copy-start.7 = (bf16[6,8,384]{2,1,0:T(8,128)(2,1)S(1)}, bf16[6,8,384]{2,1,0:T(8,128)(2,1)}, u32[]{:S(2)}) copy-start(bf16[6,8,384]{2,1,0:T(8,128)(2,1)} %get-tuple-element.32) | copy-start | bytes 110596
  172.4 56.8 %all-to-all-start = ((bf16[32,2,6,8,384]{4,3,2,1,0:T(8,128)(2,1)}), bf16[32,2,6,8,384]{4,3,2,1,0:T(8,128)(2,1)S(1)}, u32[]{:S(2)}, u32[]{:S(2)}) async-start(bf16[32,2,6,8,384]{4,3,2,1,0:T(8,128)(2,1)} %copy.35), calls=%async_computation | async-start | bytes 4718592 | tf_op jit(solution)/shard_map/all_to_all | solution.py:305
  287.0 11.7 %all-to-all-start.2 = ((f32[32,1,264]{2,1,0:T(1,128)}), f32[32,1,264]{2,1,0:T(1,128)S(1)}, u32[]{:S(2)}, u32[]{:S(2)}) async-start(f32[32,1,264]{2,1,0:T(1,128)} %all_to_all.14), calls=%async_computation.2 | async-start | bytes 98304 | tf_op jit(solution)/shard_map/all_to_all | solution.py:375
  298.8 2.8 copy-start.5
  298.8 30.6 %all-to-all-start.1 = ((bf16[32,48,384]{2,1,0:T(8,128)(2,1)}), bf16[32,48,384]{2,1,0:T(8,128)(2,1)S(1)}, u32[]{:S(2)}, u32[]{:S(2)}) async-start(bf16[32,48,384]{2,1,0:T(8,128)(2,1)} %bitcast.15), calls=%async_computation.1 | async-start | bytes 2359296 | tf_op jit(solution)/shard_map/all_to_all | solution.py:305
  301.6 1.3 copy-start.3
  301.6 28.5 %copy-start.1 = (bf16[8,384,48]{1,2,0:T(8,128)(2,1)S(1)}, bf16[8,384,48]{1,2,0:T(8,128)(2,1)}, u32[]{:S(2)}) copy-start(bf16[8,384,48]{1,2,0:T(8,128)(2,1)} %param.17) | copy-start | bytes 884740
Sparse Core Ops, SparseCore 0:
  10.8 56.8 all-gather.3
  106.5 56.3 all-gather.5

commit v3 on v2

--- a/solution.py
+++ b/solution.py
@@ -11,6 +11,7 @@
 AXES = ("wide", "narrow")
 BF16 = jnp.bfloat16
 F32 = jnp.float32
+MESH = pl.DeviceIdType.MESH
 VMEM_LIMIT = 60 * 1024 * 1024
 GAIN1, GAIN2, BIAS1, VBIAS, OBIAS, BIAS2 = range(6)
 
@@ -301,6 +302,312 @@
     )(x, g, middle, second, dispatch, combine, produced, slot_grad, wt, vec, table, q, k, v, p, att, inv)
 
 
+def here():
+    return lax.axis_index("wide"), lax.axis_index("narrow")
+
+
+def along_z(w, z):
+    return [(w, lax.rem(z + step, 4)) for step in (1, 2, 3)]
+
+
+def in_plane(w, z):
+    x_flip = 2 - 4 * lax.rem(w // 2, 2)
+    y_flip = 4 - 8 * (w // 4)
+    return [(w + x_flip, z), (w + y_flip, z), (w + x_flip + y_flip, z)]
+
+
+def other_core(w, z):
+    return (w + 1 - 2 * lax.rem(w, 2), z)
+
+
+def greet():
+    w, z = here()
+    barrier = pltpu.get_barrier_semaphore()
+    peers = along_z(w, z) + in_plane(w, z) + [other_core(w, z)]
+    for peer in peers:
+        pl.semaphore_signal(barrier, inc=1, device_id=peer, device_id_type=MESH)
+    pl.semaphore_wait(barrier, len(peers))
+
+
+def remote(src, dst, send, recv, peer):
+    return pltpu.make_async_remote_copy(
+        src_ref=src, dst_ref=dst, send_sem=send, recv_sem=recv, device_id=peer, device_id_type=MESH
+    )
+
+
+class Gather:
+    def __init__(self, every, send, recv):
+        self.every, self.send, self.recv = every, send, recv
+        self.w, self.z = here()
+
+    def z_copies(self):
+        own = self.every.at[self.w, self.z]
+        return [
+            remote(own, own, self.send.at[n], self.recv.at[n], peer)
+            for n, peer in enumerate(along_z(self.w, self.z))
+        ]
+
+    def plane_copies(self):
+        own = self.every.at[self.w]
+        return [
+            remote(own, own, self.send.at[3 + n], self.recv.at[3 + n], peer)
+            for n, peer in enumerate(in_plane(self.w, self.z))
+        ]
+
+    def core_copies(self):
+        peer = other_core(self.w, self.z)
+        groups = [self.w] + [there for there, _ in in_plane(self.w, self.z)]
+        return [
+            remote(self.every.at[g], self.every.at[g], self.send.at[6 + n], self.recv.at[6 + n], peer)
+            for n, g in enumerate(groups)
+        ]
+
+    def start_z(self):
+        for copy in self.z_copies():
+            copy.start()
+
+    def start_plane(self):
+        for copy in self.z_copies():
+            copy.wait()
+        for copy in self.plane_copies():
+            copy.start()
+        self.core_copies()[0].start()
+
+    def start_core(self):
+        for copy, onward in zip(self.plane_copies(), self.core_copies()[1:]):
+            copy.wait()
+            onward.start()
+
+    def finish(self):
+        for copy in self.core_copies():
+            copy.wait()
+
+
+class Scatter:
+    def __init__(self, parts, from_core, chips, from_plane, column, from_z, send, recv):
+        self.parts, self.from_core, self.chips = parts, from_core, chips
+        self.from_plane, self.column, self.from_z = from_plane, column, from_z
+        self.send, self.recv = send, recv
+        self.w, self.z = here()
+        self.core = lax.rem(self.w, 2)
+
+    def core_copies(self):
+        peer = other_core(self.w, self.z)
+        return [
+            remote(
+                self.parts.at[2 * chip + 1 - self.core], self.from_core.at[chip],
+                self.send.at[chip], self.recv.at[chip], peer,
+            )
+            for chip in range(4)
+        ]
+
+    def plane_copies(self):
+        return [
+            remote(
+                self.chips.at[peer[0] // 2], self.from_plane.at[n],
+                self.send.at[4 + n], self.recv.at[4 + n], peer,
+            )
+            for n, peer in enumerate(in_plane(self.w, self.z))
+        ]
+
+    def z_copies(self):
+        return [
+            remote(
+                self.column.at[peer[1]], self.from_z.at[n],
+                self.send.at[7 + n], self.recv.at[7 + n], peer,
+            )
+            for n, peer in enumerate(along_z(self.w, self.z))
+        ]
+
+    def start_core(self):
+        for copy in self.core_copies():
+            copy.start()
+
+    def start_plane(self):
+        for chip, copy in enumerate(self.core_copies()):
+            copy.wait()
+            own = self.parts[2 * chip + self.core].astype(F32)
+            self.chips[chip] = (own + self.from_core[chip].astype(F32)).astype(BF16)
+        for copy in self.plane_copies():
+            copy.start()
+
+    def start_z(self):
+        for copy in self.plane_copies():
+            copy.wait()
+        total = self.chips[self.w // 2].astype(F32)
+        for n in range(3):
+            total = total + self.from_plane[n].astype(F32)
+        self.column[...] = total.astype(BF16)
+        for copy in self.z_copies():
+            copy.start()
+
+    def finish(self):
+        for copy in self.z_copies():
+            copy.wait()
+        total = self.column[self.z].astype(F32)
+        for n in range(3):
+            total = total + self.from_z[n].astype(F32)
+        return total
+
+
+def gather_scratch(rows, width):
+    return [
+        pltpu.VMEM((8, 4, rows, width), BF16),
+        pltpu.SemaphoreType.DMA((10,)),
+        pltpu.SemaphoreType.DMA((10,)),
+    ]
+
+
+def scatter_scratch(rows, width):
+    return [
+        pltpu.VMEM((8, 4, rows, width), BF16),
+        pltpu.VMEM((4, 4, rows, width), BF16),
+        pltpu.VMEM((4, 4, rows, width), BF16),
+        pltpu.VMEM((3, 4, rows, width), BF16),
+        pltpu.VMEM((4, rows, width), BF16),
+        pltpu.VMEM((3, rows, width), BF16),
+        pltpu.SemaphoreType.DMA((10,)),
+        pltpu.SemaphoreType.DMA((10,)),
+    ]
+
+def gather_kernel(own, out, every, send, recv):
+    w, z = here()
+    every[w, z] = own[...]
+    greet()
+    gather = Gather(every, send, recv)
+    gather.start_z()
+    gather.start_plane()
+    gather.start_core()
+    gather.finish()
+    out[...] = every[...]
+
+
+def run_gather(own):
+    rows, width = own.shape
+    return pl.pallas_call(
+        gather_kernel,
+        out_shape=jax.ShapeDtypeStruct((8, 4, rows, width), BF16),
+        in_specs=[pl.BlockSpec(memory_space=pltpu.VMEM)],
+        out_specs=pl.BlockSpec(memory_space=pltpu.VMEM),
+        scratch_shapes=gather_scratch(rows, width),
+        compiler_params=pltpu.CompilerParams(
+            collective_id=0, has_side_effects=True, vmem_limit_bytes=VMEM_LIMIT
+        ),
+        name="gather",
+    )(own)
+
+
+def scatter_kernel(parts_in, out, parts, *rest):
+    parts[...] = parts_in[...].astype(BF16)
+    greet()
+    scatter = Scatter(parts, *rest)
+    scatter.start_core()
+    scatter.start_plane()
+    scatter.start_z()
+    out[...] = scatter.finish()
+
+
+def run_scatter(parts):
+    _, rows, width = parts.shape
+    return pl.pallas_call(
+        scatter_kernel,
+        out_shape=jax.ShapeDtypeStruct((rows, width), F32),
+        in_specs=[pl.BlockSpec(memory_space=pltpu.VMEM)],
+        out_specs=pl.BlockSpec(memory_space=pltpu.VMEM),
+        scratch_shapes=scatter_scratch(rows, width),
+        compiler_params=pltpu.CompilerParams(
+            collective_id=1, has_side_effects=True, vmem_limit_bytes=VMEM_LIMIT
+        ),
+        name="scatter",
+    )(parts.reshape(8, 4, rows, width))
+
+
+def expert_rows(slots, grads, w_in, bias, w_out):
+    rows, width = slots.shape
+    units = w_in.shape[0]
+    shape = (rows, units)
+    own = lax.rem(lax.broadcasted_iota(jnp.int32, shape, 0), 8)
+    start = own * (units // 8)
+    lane = lax.broadcasted_iota(jnp.int32, shape, 1)
+    keep = (lane >= start) & (lane < start + units // 8)
+    hidden = dot(slots, w_in, 1, 1) + bias
+    active_grad = dot(grads, w_out, 1, 1)
+    half = 0.5 * (1.0 + lax.erf(hidden * 0.7071067811865476))
+    active = jnp.where(keep, hidden * half, 0.0).astype(BF16)
+    slope = half + hidden * jnp.exp(hidden * hidden * -0.5) * 0.3989422804014327
+    hidden_grad = jnp.where(keep, active_grad * slope, 0.0).astype(BF16)
+    produced = dot(active, w_out, 1, 0).astype(BF16)
+    slot_grad = dot(hidden_grad, w_in, 1, 0).astype(BF16)
+    in_grad = dot(hidden_grad, slots, 0, 0)
+    out_grad = dot(active, grads, 0, 0)
+    bias_grad = jnp.sum(hidden_grad.astype(F32), axis=0, keepdims=True)
+    return produced, slot_grad, in_grad, out_grad, bias_grad
+
+
+def experts_kernel(
+    slots, grads, w_in, bias, w_out, produced, slot_grad, in_grad, out_grad, bias_grad,
+    every, g_send, g_recv, parts, *rest,
+):
+    w, z = here()
+    count = slots.shape[0]
+    every[w, z, :count] = slots[...]
+    every[w, z, count:] = grads[...]
+    greet()
+    gather = Gather(every, g_send, g_recv)
+    gather.start_z()
+    gather.start_plane()
+    gather.start_core()
+    gather.finish()
+    in_grad[...] = jnp.zeros_like(in_grad)
+    out_grad[...] = jnp.zeros_like(out_grad)
+    bias_grad[...] = jnp.zeros_like(bias_grad)
+    width = slots.shape[1]
+    rows = 8 * count
+
+    def step(n, carry):
+        at = pl.ds(n * 2, 2)
+        got = expert_rows(
+            every[at, :, :count].reshape(rows, width), every[at, :, count:].reshape(rows, width),
+            w_in[...], bias[...], w_out[...],
+        )
+        parts[at, :, :count] = got[0].reshape(2, 4, count, width)
+        parts[at, :, count:] = got[1].reshape(2, 4, count, width)
+        in_grad[...] += got[2]
+        out_grad[...] += got[3]
+        bias_grad[...] += got[4]
+        return carry
+
+    lax.fori_loop(0, 4, step, 0)
+    scatter = Scatter(parts, *rest)
+    scatter.start_core()
+    scatter.start_plane()
+    scatter.start_z()
+    total = scatter.finish()
+    produced[...] = total[:count]
+    slot_grad[...] = total[count:]
+
+
+def run_experts(slots, grads, w_in, bias, w_out):
+    count, width = slots.shape
+    units = w_in.shape[0]
+    full = pl.BlockSpec(memory_space=pltpu.VMEM)
+    return pl.pallas_call(
+        experts_kernel,
+        out_shape=[
+            jax.ShapeDtypeStruct((count, width), F32), jax.ShapeDtypeStruct((count, width), F32),
+            jax.ShapeDtypeStruct((units, width), F32), jax.ShapeDtypeStruct((units, width), F32),
+            jax.ShapeDtypeStruct((1, units), F32),
+        ],
+        in_specs=[full] * 5,
+        out_specs=[full] * 5,
+        scratch_shapes=gather_scratch(2 * count, width) + scatter_scratch(2 * count, width),
+        compiler_params=pltpu.CompilerParams(
+            collective_id=2, has_side_effects=True, vmem_limit_bytes=VMEM_LIMIT
+        ),
+        name="experts",
+    )(slots, grads, w_in, bias, w_out)
+
+
 def scatter_sum(parts):
     got = lax.all_to_all(parts.astype(BF16), AXES, 0, 0, tiled=True)
     return jnp.sum(got.astype(F32), axis=0)
@@ -346,7 +653,18 @@
 
     vectors = (norm_gains, vec_biases, slot_params, expert_out_bias)
     lengths = [v.shape[0] for v in vectors]
-    small = lax.all_gather(jnp.concatenate(vectors), AXES)
+    small = jnp.concatenate(vectors)
+    by_hand = lax.axis_size("wide") == 8 and lax.axis_size("narrow") == 4
+    if by_hand:
+        rows = attn_weights.shape[1]
+        every = run_gather(
+            jnp.concatenate([attn_weights.T, jnp.pad(small[None], ((0, 15), (0, width - small.shape[0])))])
+        )
+        wt = every[:, :, :rows].reshape(-1, width)
+        small = every[:, :, rows].reshape(devices, width)
+    else:
+        wt = lax.all_gather(attn_weights.T, AXES, axis=0, tiled=True)
+        small = lax.all_gather(small, AXES)
     pieces = []
     at = 0
     for length in lengths:
@@ -354,25 +672,47 @@
         at += length
     gains, biases, table, expert_shift = pieces
     vec = jnp.concatenate([gains, biases, jnp.zeros((2, width), BF16)]).astype(F32)
-    wt = lax.all_gather(attn_weights.T, AXES, axis=0, tiled=True)
 
     *kept, slots, produced_grad = run_forward(
         patches, out_grad, valid.reshape(local_images, 1, patch_count), wt, vec, table
     )
-    produced, slot_grad, expand_grad, inner_grad, contract_grad = experts_at_home(
-        slots, produced_grad, expert_in, expert_in_bias, expert_out, devices
-    )
+    if by_hand:
+        units = expert_in.shape[2]
+        produced, slot_grad, expand_grad, contract_grad, inner_grad = run_experts(
+            slots.reshape(-1, width), produced_grad.reshape(-1, width),
+            expert_in.transpose(0, 2, 1).reshape(experts * units, width),
+            expert_in_bias.reshape(1, experts * units).astype(F32),
+            expert_out.reshape(experts * units, width),
+        )
+        produced = produced.reshape(slots.shape)
+        slot_grad = slot_grad.reshape(slots.shape)
+        expand_grad = expand_grad.reshape(experts, units, width).transpose(0, 2, 1)
+        contract_grad = contract_grad.reshape(experts, units, width)
+        inner_grad = inner_grad.reshape(experts, units)
+    else:
+        produced, slot_grad, expand_grad, inner_grad, contract_grad = experts_at_home(
+            slots, produced_grad, expert_in, expert_in_bias, expert_out, devices
+        )
     produced = (produced + expert_shift.astype(F32)).astype(BF16)
     slot_grad = slot_grad.astype(BF16)
     shift_grad = jnp.sum(produced_grad.astype(F32), axis=0)
     mixed_out, patch_grad, weight_grad, rows, table_grad = run_backward(
         patches, out_grad, kept, produced, slot_grad, wt, vec, table
     )
-    weight_grad = scatter_sum(weight_grad.reshape(devices, -1, width)).T
+    weight_grad = weight_grad.reshape(devices, -1, width)
     small_grads = jnp.concatenate(
         [v.reshape(devices, -1) for v in (rows[:2], rows[2:6], table_grad, shift_grad)], axis=1
     )
-    small_grads = jnp.sum(lax.all_to_all(small_grads, AXES, 0, 0, tiled=True), axis=0)
+    if by_hand:
+        small_grads = jnp.pad(
+            small_grads[:, None], ((0, 0), (0, 15), (0, width - small_grads.shape[1]))
+        )
+        total = run_scatter(jnp.concatenate([weight_grad, small_grads], axis=1))
+        small_grads = total[weight_grad.shape[1]]
+        weight_grad = total[: weight_grad.shape[1]].T
+    else:
+        weight_grad = scatter_sum(weight_grad).T
+        small_grads = jnp.sum(lax.all_to_all(small_grads, AXES, 0, 0, tiled=True), axis=0)
     grads = []
     at = 0
     for length in lengths:

time: 339 us -> 227 us (0.67)
  waiting for transfers between devices: 151 us -> 0 us
  Pallas kernels: 90.3 us -> 197 us
  blocking collectives: 42.2 us -> 0 us
  between operations: 14.3 us -> 0.75 us
  starting transfers between devices: 10.9 us -> 0 us
  matrix products: 6.7 us -> 0 us
  local copies, waits for them, and re-layouts: 13.1 us -> 17.4 us
    pallas_call x0 -> x3, Pallas kernels: none -> 106 us  [the longest x1 58.1 us: run_experts(): pl.pallas_call(experts_kernel, out_shape=[jax.ShapeDtypeStruct((count, wi...]
    all_to_all x3 -> x0, waiting for transfers between devices: 81 us -> none  [the longest x2 76.5 us: scatter_sum(): got = lax.all_to_all(parts.astype(BF16), AXES, 0, 0, tiled=True)]
    all_gather x2 -> x0, waiting for transfers between devices: 69.8 us -> none  [the longest x1 56.5 us: experts_at_home(): lax.all_gather(jnp.stack([slots, produced_grad]), AXES, axis=1, tiled=True)]
    unnamed x1 -> x0, blocking collectives: 42.2 us -> none
    all_to_all x3 -> x0, starting transfers between devices: 10.8 us -> none  [the longest x2 6.46 us: scatter_sum(): got = lax.all_to_all(parts.astype(BF16), AXES, 0, 0, tiled=True)]
    dot_general x6 -> x0, matrix products: 6.7 us -> none  [the longest x1 1.96 us: experts_at_home(): jnp.einsum('bed,efd->bef', all_grads, expert_out, preferred_element_type=...]
    concatenate x1 -> x3, other arithmetic: 0.78 us -> 5.89 us  [the longest x1 3.71 us: on_device(): total = run_scatter(jnp.concatenate([weight_grad, small_grads], axis=1))]
    slice x0 -> x2, local copies, waits for them, and re-layouts: none -> 3.49 us  [the longest x1 2.43 us: on_device(): wt = every[:, :, :rows].reshape(-1, width)]
  transfers between devices with their start and end apart: 5 -> 0, of which waited for: 5 -> 0; matrix products, arithmetic and copies ran while one was open for 3% -> 0% of each run, Pallas kernels for 0% -> 0%
where the time goes in v3:
time: 227 us; the launch traced here: 226 us
  Pallas kernels  197 us (87%)
  local copies, waits for them, and re-layouts  17.4 us (8%)
  other arithmetic  11.2 us (5%)
    pallas_call x1, Pallas kernels, run_experts(): pl.pallas_call(experts_kernel, out_shape=[jax.ShapeDtypeStruct((count, wi...  58.1 us
    pallas_call x1, Pallas kernels, run_backward(): pl.pallas_call(backward_kernel, grid=(count,), in_specs=[per_image(*flat)...  53.3 us
    pallas_call x1, Pallas kernels, run_forward(): pl.pallas_call(forward_kernel, grid=(count,), in_specs=[per_image(*flat),...  37.2 us
    pallas_call x1, Pallas kernels, run_scatter(): pl.pallas_call(scatter_kernel, out_shape=jax.ShapeDtypeStruct((rows, widt...  24.5 us
    pallas_call x1, Pallas kernels, run_gather(): pl.pallas_call(gather_kernel, out_shape=jax.ShapeDtypeStruct((8, 4, rows,...  23.9 us

profile of v3, /device:TPU:0, one launch (start us, length us, event | category | flops | bytes accessed | tf_op | source)
XLA Modules:
  0.0 226.3 jit_solution(4267219443449910161)
XLA Ops:
  0.7 0.1 pad.18.clone
  0.7 0.8 pad_maximum_fusion.2
  1.5 1.3 reshape.122.bias
  2.8 1.3 reshape.105.valid
  4.2 1.4 fusion.2.own
  5.6 23.9 %gather.1 = bf16[8,4,64,384]{3,2,1,0:T(8,128)(2,1)} custom-call(bf16[64,384]{1,0:T(8,128)(2,1)} %fusion.2.own), custom_call_target="tpu_custom_call" | custom-call | tf_op jit(solution)/shard_map/gather/pallas_call | solution.py:487
  29.5 1.1 slice_reduce_fusion
  30.5 2.4 %slice.56 = bf16[8,4,48,384]{3,2,1,0:T(8,128)(2,1)} slice(bf16[8,4,64,384]{3,2,1,0:T(8,128)(2,1)} %gather.1), slice={[0:8], [0:4], [0:48], [0:384]} | slice | bytes 2359296 | tf_op jit(solution)/shard_map/slice | solution.py:663
  33.0 0.1 slice.74
  33.1 0.1 reshape.108
  33.2 0.1 reshape.107
  33.3 0.1 slice_convert_fusion
  33.3 0.1 reshape.123
  33.4 0.7 reshape.109.table
  34.1 0.7 maximum_convert_fusion.vec
  34.8 37.2 %forward.1 = (bf16[6,576,384]{2,1,0:T(8,128)(2,1)}, bf16[6,576,384]{2,1,0:T(8,128)(2,1)}, bf16[6,576,384]{2,1,0:T(8,128)(2,1)}, bf16[6,6,576,576]{3,2,1,0:T(8,12...) custom-call(bf16[6,576,384]{2,1,0:T(8,128)(2,1)} %x.7, ...), custom_call_target="tpu_custom_call" | custom-call | tf_op jit(solution)/shard_map/forward/pallas_call | solution.py:255
  72.0 0.8 convert_reduce_fusion
  72.8 0.1 reshape.118
  72.8 58.1 %experts.1 = (f32[48,384]{1,0:T(8,128)}, f32[48,384]{1,0:T(8,128)}, f32[384,384]{1,0:T(8,128)}, f32[384,384]{1,0:T(8,128)}, f32[1,384]{1,0:T(1,128)}) custom-call(bf16[48,384]{1,0:T(8,128)(2,1)} %bitcast.39, bf16[48,384]{1,0:T(8,128)(2,1)} %bitcast.38, bf16[384,384]{1,0:T(8,128)(2,1)} %bitcast.36, f32[1,384]{1,0:T(1,128)} %reshape.122.bias, ...), custom_call_target="tpu_custom_call" | custom-call | tf_op jit(solution)/shard_map/experts/pallas_call | solution.py:594
  131.0 1.5 fusion.1.produced
  132.5 0.7 reduce.1
  133.1 0.7 reshape.120
  133.8 1.5 convert_bitcast_fusion.slot_grad
  135.3 53.3 %backward.1 = (bf16[6,576,384]{2,1,0:T(8,128)(2,1)}, bf16[6,576,384]{2,1,0:T(8,128)(2,1)}, f32[1536,384]{1,0:T(8,128)}, f32[8,384]{1,0:T(8,128)}, f32[8,384]{1,0:T(8,128)}) custom-call(bf16[6,576,384]{2,1,0:T(8,128)(2,1)} %x.7, bf16[6,576,384]{2,1,0:T(8,128)(2,1)} %g.3, f32[6,576,384]{2,1,0:T(8,128)} %get-tuple-element.32.middle, ...), custom_call_target="tpu_custom_call" | custom-call | tf_op jit(solution)/shard_map/backward/pallas_call | solution.py:275
  188.6 0.7 slice.62
  189.3 0.7 slice.63
  190.0 0.1 reshape.116
  190.1 0.1 reshape.115
  190.2 0.8 reshape.117
  191.0 0.1 pad_maximum_fusion.1
  191.1 0.1 pad.9
  191.2 3.7 %pad_maximum_fusion.parts_in = f32[8,4,64,384]{3,2,1,0:T(8,128)} fusion(f32[8,4,16,384]{3,2,1,0:T(8,128)S(1)} %bitcast.32, f32[8,4,48,384]{3,2,1,0:T(8,128)} %bitcast.33), kind=kLoop, calls=%fused_computation | loop fusion | flops 786432 | bytes 6291456 | tf_op jit(solution)/shard_map/concatenate | solution.py:710
  194.9 0.0 copy-start.1
  194.9 0.0 copy-start
  194.9 24.5 %scatter.1 = f32[64,384]{1,0:T(8,128)} custom-call(f32[8,4,64,384]{3,2,1,0:T(8,128)} %pad_maximum_fusion.parts_in), custom_call_target="tpu_custom_call" | custom-call | tf_op jit(solution)/shard_map/scatter/pallas_call | solution.py:512
  219.4 1.2 slice_bitcast_fusion.3
  220.6 1.2 slice_bitcast_fusion.4
  221.8 1.4 slice_bitcast_fusion.1
  223.2 1.5 slice_bitcast_fusion
  224.7 0.0 copy-done.1
  224.7 0.8 copy.24
  225.5 0.0 copy-done
  225.5 0.8 copy.25
  (5 shorter events, 0.1 us)
Async XLA Ops:
  194.9 29.8 %copy-start.1 = (f32[384,384]{1,0:T(8,128)S(1)}, f32[384,384]{1,0:T(8,128)}, u32[]{:S(2)}) copy-start(f32[384,384]{1,0:T(8,128)} %get-tuple-element.51) | copy-start | bytes 1769476
  194.9 30.6 %copy-start = (f32[384,384]{1,0:T(8,128)S(1)}, f32[384,384]{1,0:T(8,128)}, u32[]{:S(2)}) copy-start(f32[384,384]{1,0:T(8,128)} %get-tuple-element.53) | copy-start | bytes 1769476

commit v4 on v3

--- a/solution.py
+++ b/solution.py
@@ -1,3 +1,5 @@
+import functools
+
 import jax
 import jax.numpy as jnp
 from jax import lax
@@ -13,6 +15,7 @@
 F32 = jnp.float32
 MESH = pl.DeviceIdType.MESH
 VMEM_LIMIT = 60 * 1024 * 1024
+LAYER_LIMIT = 63 * 1024 * 1024
 GAIN1, GAIN2, BIAS1, VBIAS, OBIAS, BIAS2 = range(6)
 
 
@@ -48,15 +51,20 @@
     return jnp.where(low, own, other) if head % 2 == 0 else jnp.where(low, other, own)
 
 
-def forward_image(x, g, valid_row, wt, vec, table, q_ref, k_ref, v_ref, p_ref, att_ref, inv_ref):
+def forward_image(
+    x, g, valid_row, wt, vec, table, q_ref, k_ref, v_ref, p_ref, att_ref, inv_ref,
+    before_heads=None, after_head=None,
+):
     patches, width = x.shape
     heads = width // HEAD_DIM
-    images = x.astype(F32)
+    images = x[...].astype(F32)
     normed, _ = normalize(images)
     first = (normed * vec[GAIN1 : GAIN1 + 1] + vec[BIAS1 : BIAS1 + 1]).astype(BF16)
     q_ref[...] = (dot(first, wt[:width], 1, 1) * HEAD_DIM ** (-0.5)).astype(BF16)
     k_ref[...] = dot(first, wt[width : 2 * width], 1, 1).astype(BF16)
     v_ref[...] = (dot(first, wt[2 * width : 3 * width], 1, 1) + vec[VBIAS : VBIAS + 1]).astype(BF16)
+    if before_heads is not None:
+        before_heads()
     bias_row = jnp.where(valid_row > 0, 0.0, MASKED).astype(F32)
     fill = jnp.broadcast_to(bias_row * (1.0 / HEAD_DIM), (PAIR, patches)).T.astype(BF16)
     low = lower_half((patches, PAIR))
@@ -84,11 +92,13 @@
         prob = jnp.exp(raw - jnp.max(raw, axis=1, keepdims=True)).astype(BF16)
         p_ref[head] = prob
         sums[head] = dot(prob, own_half(low, head, pair_of(v_ref, head), one), 1, 0)
+        if after_head is not None:
+            after_head(head)
         if head % 2 == 1:
             even, odd = sums.pop(head - 1), sums.pop(head)
             inverse = 1.0 / pltpu.roll(jnp.where(low, odd, even), HEAD_DIM, 1)
             at = head // 2 * PAIR
-            inv_ref[:, at : at + PAIR] = inverse
+            inv_ref[:, at : at + PAIR] = inverse.astype(inv_ref.dtype)
             att_ref[:, at : at + PAIR] = (jnp.where(low, even, odd) * inverse).astype(BF16)
     branch = dot(att_ref[...], wt[3 * width :], 1, 1)
     middle = images + branch + vec[OBIAS : OBIAS + 1]
@@ -100,21 +110,26 @@
     dispatch = dispatch / jnp.sum(dispatch, axis=1, keepdims=True)
     combine = jnp.exp(logits - jnp.max(logits, axis=0, keepdims=True))
     combine = combine / jnp.sum(combine, axis=0, keepdims=True)
-    slots = dot(dispatch.astype(BF16), second, 1, 0).astype(BF16)
-    produced_grad = dot(combine.astype(BF16), g, 1, 0).astype(BF16)
-    return middle, second, dispatch, combine, slots, produced_grad
+    slots = dot(dispatch.astype(BF16), second, 1, 0)
+    produced_grad = dot(combine.astype(BF16), g[...], 1, 0)
+    return middle, dispatch, combine, slots, produced_grad
 
 
 def backward_image(
-    x, g, middle, second, dispatch, combine, produced, slot_grad, wt, vec, table,
-    q_ref, k_ref, v_ref, p_ref, att_ref, inv_ref, ds_ref, grad_t_ref, grad_ref,
+    x, g, middle_ref, dispatch, combine, produced, slot_grad, wt, vec, table,
+    q_ref, k_ref, v_ref, p_ref, att_ref, inv_ref, ds_ref, grad_t_ref, dq_ref, dk_ref, dv_ref, mixed_ref,
+    before_heads=None, before_head=None, after_heads=None,
 ):
     patches, width = x.shape
     heads = width // HEAD_DIM
     combine_low = combine.astype(BF16)
     dispatch_low = dispatch.astype(BF16)
+    middle = middle_ref[...]
+    normed, factor = normalize(middle)
+    second = (normed * vec[GAIN2 : GAIN2 + 1] + vec[BIAS2 : BIAS2 + 1]).astype(BF16)
+    upstream = g[...]
     mixed = (middle + dot(combine_low, produced, 0, 0)).astype(BF16)
-    combine_grad = dot(produced, g, 1, 1)
+    combine_grad = dot(produced, upstream, 1, 1)
     dispatch_grad = dot(slot_grad, second, 1, 1)
     logit_grad = dispatch * (
         dispatch_grad - jnp.sum(dispatch * dispatch_grad, axis=1, keepdims=True)
@@ -127,19 +142,23 @@
         0,
         0,
     )
-    normed, factor = normalize(middle)
     gain_two = jnp.sum(second_grad * normed, axis=0, keepdims=True)
     shift_two = jnp.sum(second_grad, axis=0, keepdims=True)
-    middle_grad = g.astype(F32) + norm_back(second_grad * vec[GAIN2 : GAIN2 + 1], normed, factor)
+    middle_grad = upstream.astype(F32) + norm_back(
+        second_grad * vec[GAIN2 : GAIN2 + 1], normed, factor
+    )
+    mixed_ref[...] = mixed
     branch_grad = middle_grad.astype(BF16)
     branch_shift = jnp.sum(branch_grad.astype(F32), axis=0, keepdims=True)
     output_grad = dot(branch_grad.T, att_ref[...], 1, 0)
     attended_grad = dot(branch_grad, wt[3 * width :], 1, 0).astype(BF16).astype(F32)
-    scaled = attended_grad * inv_ref[...]
-    drop = -(scaled * att_ref[...].astype(F32))
+    scaled = attended_grad * inv_ref[...].astype(F32)
+    drop = (-(scaled * att_ref[...].astype(F32))).astype(BF16)
     scaled = scaled.astype(BF16)
     scaled_t = scaled.T
     query_t = q_ref[...].T
+    if before_heads is not None:
+        before_heads()
     low = lower_half((patches, PAIR))
     one = jnp.ones((patches, PAIR), BF16)
     prob_grads = {}
@@ -149,7 +168,7 @@
         return ref[:, at : at + PAIR]
 
     def prob_grad(head):
-        rolled = pltpu.roll(pair_of(drop, head), HEAD_DIM, 1).astype(BF16)
+        rolled = pltpu.roll(pair_of(drop, head).astype(F32), HEAD_DIM, 1).astype(BF16)
         prob_grads[head] = dot(
             own_half(low, head, pair_of(scaled, head), rolled),
             own_half(low, head, pair_of(v_ref, head), one),
@@ -162,75 +181,83 @@
     for head in range(heads):
         if head + 1 < heads:
             prob_grad(head + 1)
+        if before_head is not None:
+            before_head(head)
         rows = slice(head * HEAD_DIM, (head + 1) * HEAD_DIM)
         prob = p_ref[head]
-        grad_t_ref[2 * width + rows.start : 2 * width + rows.stop, :] = dot(
+        grad_t_ref[width + rows.start : width + rows.stop, :] = dot(
             scaled_t[rows], prob, 1, 0
         ).astype(BF16)
         score_grad = (prob.astype(F32) * prob_grads.pop(head)).astype(BF16)
         ds_ref[head % 2] = score_grad
         score_grad = ds_ref[head % 2]
         query_grads[head] = dot(score_grad, pair_of(k_ref, head), 1, 0)
-        grad_t_ref[width + rows.start : width + rows.stop, :] = dot(
-            query_t[rows], score_grad, 1, 0
-        ).astype(BF16)
+        grad_t_ref[rows, :] = dot(query_t[rows], score_grad, 1, 0).astype(BF16)
         if head % 2 == 1:
             both = jnp.where(low, query_grads.pop(head - 1), query_grads.pop(head))
             at = head // 2 * PAIR
-            grad_ref[:, at : at + PAIR] = (both * HEAD_DIM ** (-0.5)).astype(BF16)
-    grad_t_ref[:width, :] = grad_ref[:, :width].T
-    grad_ref[:, width:] = grad_t_ref[width:, :].T
-    normed, factor = normalize(x.astype(F32))
+            dq_ref[:, at : at + PAIR] = (both * HEAD_DIM ** (-0.5)).astype(BF16)
+    if after_heads is not None:
+        after_heads()
+    dk_ref[...] = grad_t_ref[:width, :].T
+    dv_ref[...] = grad_t_ref[width:, :].T
+    normed, factor = normalize(x[...].astype(F32))
     first = (normed * vec[GAIN1 : GAIN1 + 1] + vec[BIAS1 : BIAS1 + 1]).astype(BF16)
-    front_grad = dot(grad_t_ref[...], first, 1, 0)
-    value_shift = jnp.sum(grad_ref[:, 2 * width :].astype(F32), axis=0, keepdims=True)
-    first_grad = dot(grad_ref[...], wt[: 3 * width], 1, 0)
+    query_front = dot(dq_ref[...].T, first, 1, 0)
+    other_front = dot(grad_t_ref[...], first, 1, 0)
+    value_shift = jnp.sum(dv_ref[...].astype(F32), axis=0, keepdims=True)
+    project_grad = jnp.concatenate([dq_ref[...], dk_ref[...], dv_ref[...]], axis=1)
+    first_grad = dot(project_grad, wt[: 3 * width], 1, 0)
     gain_one = jnp.sum(first_grad * normed, axis=0, keepdims=True)
     shift_one = jnp.sum(first_grad, axis=0, keepdims=True)
     patch_grad = middle_grad + norm_back(first_grad * vec[GAIN1 : GAIN1 + 1], normed, factor)
-    rows = jnp.concatenate(
+    sums = jnp.concatenate(
         [gain_one, gain_two, shift_one, value_shift, branch_shift, shift_two, jnp.zeros((2, width), F32)],
         axis=0,
     )
-    return mixed, patch_grad.astype(BF16), front_grad, output_grad, rows, table_grad
+    return patch_grad.astype(BF16), query_front, other_front, output_grad, sums, table_grad
 
 
 def forward_kernel(
     x, g, valid, wt, vec, table,
-    q, k, v, p, att, inv, middle, second, dispatch, combine, slots, produced_grad,
+    q, k, v, p, att, inv, middle, dispatch, combine, slots, produced_grad,
 ):
     got = forward_image(
-        x[0], g[0], valid[0], wt[...], vec[...], table[...],
+        x.at[0], g.at[0], valid[0], wt, vec[...], table[...],
         q.at[0], k.at[0], v.at[0], p.at[0], att.at[0], inv.at[0],
     )
-    for ref, value in zip((middle, second, dispatch, combine, slots, produced_grad), got):
-        ref[0] = value
+    for ref, value in zip((middle, dispatch, combine, slots, produced_grad), got):
+        ref[0] = value.astype(ref.dtype)
+
+
+def add_grads(weight_grad, sums, table_grad, got):
+    width = weight_grad.shape[1]
+    for ref, at, value in (
+        (weight_grad, 0, got[1]), (weight_grad, width, got[2]), (weight_grad, 3 * width, got[3]),
+        (sums, 0, got[4]), (table_grad, 0, got[5]),
+    ):
+        ref[at : at + value.shape[0], :] += value
 
 
 def backward_kernel(
-    x, g, middle, second, dispatch, combine, produced, slot_grad, wt, vec, table,
+    x, g, middle, dispatch, combine, produced, slot_grad, wt, vec, table,
     q, k, v, p, att, inv,
-    mixed, patch_grad, weight_grad, rows, table_grad,
-    ds, grad_t, grad,
+    mixed, patch_grad, weight_grad, sums, table_grad,
+    ds, grad_t, dq, dk, dv,
 ):
     @pl.when(pl.program_id(0) == 0)
     def _():
         weight_grad[...] = jnp.zeros_like(weight_grad)
-        rows[...] = jnp.zeros_like(rows)
+        sums[...] = jnp.zeros_like(sums)
         table_grad[...] = jnp.zeros_like(table_grad)
 
-    width = x.shape[-1]
     got = backward_image(
-        x[0], g[0], middle[0], second[0], dispatch[0], combine[0], produced[0], slot_grad[0],
-        wt[...], vec[...], table[...],
-        q.at[0], k.at[0], v.at[0], p.at[0], att.at[0], inv.at[0], ds, grad_t, grad,
-    )
-    mixed[0] = got[0]
-    patch_grad[0] = got[1]
-    weight_grad[: 3 * width, :] += got[2]
-    weight_grad[3 * width :, :] += got[3]
-    rows[...] += got[4]
-    table_grad[...] += got[5]
+        x.at[0], g.at[0], middle.at[0], dispatch[0], combine[0], produced[0], slot_grad[0],
+        wt, vec[...], table[...],
+        q.at[0], k.at[0], v.at[0], p.at[0], att.at[0], inv.at[0], ds, grad_t, dq, dk, dv, mixed.at[0],
+    )
+    patch_grad[0] = got[0]
+    add_grads(weight_grad, sums, table_grad, got)
 
 
 def per_image(*shape):
@@ -248,7 +275,7 @@
     flat = (patches, width)
     outs = [
         (flat, BF16), (flat, BF16), (flat, BF16), ((heads, patches, patches), BF16),
-        (flat, BF16), (flat, F32), (flat, F32), (flat, BF16),
+        (flat, BF16), (flat, F32), (flat, F32),
         ((experts, patches), F32), ((experts, patches), F32),
         ((experts, width), BF16), ((experts, width), BF16),
     ]
@@ -271,12 +298,12 @@
     heads = width // HEAD_DIM
     experts = table.shape[0]
     flat = (patches, width)
-    q, k, v, p, att, inv, middle, second, dispatch, combine = kept
+    q, k, v, p, att, inv, middle, dispatch, combine = kept
     return pl.pallas_call(
         backward_kernel,
         grid=(count,),
         in_specs=[
-            per_image(*flat), per_image(*flat), per_image(*flat), per_image(*flat),
+            per_image(*flat), per_image(*flat), per_image(*flat),
             per_image(experts, patches), per_image(experts, patches),
             per_image(experts, width), per_image(experts, width),
             whole(*wt.shape), whole(*vec.shape), whole(*table.shape),
@@ -294,12 +321,14 @@
         ],
         scratch_shapes=[
             pltpu.VMEM((2, patches, patches), BF16),
-            pltpu.VMEM((3 * width, patches), BF16),
-            pltpu.VMEM((patches, 3 * width), BF16),
+            pltpu.VMEM((2 * width, patches), BF16),
+            pltpu.VMEM(flat, BF16),
+            pltpu.VMEM(flat, BF16),
+            pltpu.VMEM(flat, BF16),
         ],
         compiler_params=pltpu.CompilerParams(vmem_limit_bytes=VMEM_LIMIT),
         name="backward",
-    )(x, g, middle, second, dispatch, combine, produced, slot_grad, wt, vec, table, q, k, v, p, att, inv)
+    )(x, g, middle, dispatch, combine, produced, slot_grad, wt, vec, table, q, k, v, p, att, inv)
 
 
 def here():
@@ -469,58 +498,6 @@
         pltpu.SemaphoreType.DMA((10,)),
         pltpu.SemaphoreType.DMA((10,)),
     ]
-
-def gather_kernel(own, out, every, send, recv):
-    w, z = here()
-    every[w, z] = own[...]
-    greet()
-    gather = Gather(every, send, recv)
-    gather.start_z()
-    gather.start_plane()
-    gather.start_core()
-    gather.finish()
-    out[...] = every[...]
-
-
-def run_gather(own):
-    rows, width = own.shape
-    return pl.pallas_call(
-        gather_kernel,
-        out_shape=jax.ShapeDtypeStruct((8, 4, rows, width), BF16),
-        in_specs=[pl.BlockSpec(memory_space=pltpu.VMEM)],
-        out_specs=pl.BlockSpec(memory_space=pltpu.VMEM),
-        scratch_shapes=gather_scratch(rows, width),
-        compiler_params=pltpu.CompilerParams(
-            collective_id=0, has_side_effects=True, vmem_limit_bytes=VMEM_LIMIT
-        ),
-        name="gather",
-    )(own)
-
-
-def scatter_kernel(parts_in, out, parts, *rest):
-    parts[...] = parts_in[...].astype(BF16)
-    greet()
-    scatter = Scatter(parts, *rest)
-    scatter.start_core()
-    scatter.start_plane()
-    scatter.start_z()
-    out[...] = scatter.finish()
-
-
-def run_scatter(parts):
-    _, rows, width = parts.shape
-    return pl.pallas_call(
-        scatter_kernel,
-        out_shape=jax.ShapeDtypeStruct((rows, width), F32),
-        in_specs=[pl.BlockSpec(memory_space=pltpu.VMEM)],
-        out_specs=pl.BlockSpec(memory_space=pltpu.VMEM),
-        scratch_shapes=scatter_scratch(rows, width),
-        compiler_params=pltpu.CompilerParams(
-            collective_id=1, has_side_effects=True, vmem_limit_bytes=VMEM_LIMIT
-        ),
-        name="scatter",
-    )(parts.reshape(8, 4, rows, width))
-
 
 def expert_rows(slots, grads, w_in, bias, w_out):
     rows, width = slots.shape
@@ -536,76 +513,282 @@
     active = jnp.where(keep, hidden * half, 0.0).astype(BF16)
     slope = half + hidden * jnp.exp(hidden * hidden * -0.5) * 0.3989422804014327
     hidden_grad = jnp.where(keep, active_grad * slope, 0.0).astype(BF16)
-    produced = dot(active, w_out, 1, 0).astype(BF16)
-    slot_grad = dot(hidden_grad, w_in, 1, 0).astype(BF16)
+    produced = dot(active, w_out, 1, 0)
+    slot_grad = dot(hidden_grad, w_in, 1, 0)
     in_grad = dot(hidden_grad, slots, 0, 0)
     out_grad = dot(active, grads, 0, 0)
     bias_grad = jnp.sum(hidden_grad.astype(F32), axis=0, keepdims=True)
     return produced, slot_grad, in_grad, out_grad, bias_grad
 
 
-def experts_kernel(
-    slots, grads, w_in, bias, w_out, produced, slot_grad, in_grad, out_grad, bias_grad,
-    every, g_send, g_recv, parts, *rest,
+def lanes_of(length, offset, width, transposed=False):
+    row = lax.broadcasted_iota(jnp.int32, (width, width), 1 if transposed else 0)
+    column = lax.broadcasted_iota(jnp.int32, (width, width), 0 if transposed else 1)
+    return (row == offset + lax.rem(column, length)).astype(BF16)
+
+
+def spread(blocks, length, offset):
+    width = blocks.shape[1]
+    per_row = width // length
+    wide = dot(blocks, lanes_of(length, offset, width), 1, 0)
+    row = lax.broadcasted_iota(jnp.int32, wide.shape, 0)
+    column = lax.broadcasted_iota(jnp.int32, wide.shape, 1)
+    keep = (lax.rem(row, 16) == 0) & (lax.rem(row // 16, per_row) == column // length)
+    wide = jnp.where(keep, wide, 0.0)
+    return jnp.sum(wide.reshape(-1, per_row * 16, width), axis=1)
+
+
+def gather_up(rows, length, offset):
+    count, width = rows.shape
+    per_row = width // length
+    tall = jnp.broadcast_to(rows[:, None], (count, per_row, width)).reshape(32, width)
+    row = lax.broadcasted_iota(jnp.int32, tall.shape, 0)
+    column = lax.broadcasted_iota(jnp.int32, tall.shape, 1)
+    tall = jnp.where(lax.rem(row, per_row) == column // length, tall, 0.0)
+    return dot(tall.astype(BF16), lanes_of(length, offset, width, True), 1, 0)
+
+
+def layer_kernel(
+    lengths,
+    x_hbm, g_hbm, valid, own_weights, own_vectors, w_in, own_bias, w_out,
+    mixed_hbm, patch_grad_hbm, p_hbm, weight_out, vectors_out, in_grad, out_grad, bias_grad,
+    x, g, q, k, v, att, inv, middle, dispatch, combine, p, ds, grad_t, wt, vec, table, shift, bias,
+    weight_grad, sums, table_grad, shift_grad,
+    x_sem, g_sem, p_out_sem, p_in_sem, mixed_sem, patch_sem,
+    w_every, w_send, w_recv,
+    every, g_send, g_recv,
+    parts, from_core, chips, from_plane, column, from_z, s_send, s_recv,
+    *last,
 ):
-    w, z = here()
-    count = slots.shape[0]
-    every[w, z, :count] = slots[...]
-    every[w, z, count:] = grads[...]
+    count, patches, width = x.shape
+    heads = width // HEAD_DIM
+    rows = own_weights.shape[0]
+    wide, narrow = here()
+
+    for i in range(count):
+        pltpu.make_async_copy(x_hbm.at[i], x.at[i], x_sem.at[i]).start()
+        pltpu.make_async_copy(g_hbm.at[i], g.at[i], g_sem.at[i]).start()
+    w_every[wide, narrow, :rows] = own_weights[...]
+    row = lax.broadcasted_iota(jnp.int32, (16, width), 0)
+    w_every[wide, narrow, rows:] = jnp.where(
+        row == 0, jnp.broadcast_to(own_vectors[...].astype(F32), (16, width)), 0.0
+    ).astype(BF16)
     greet()
-    gather = Gather(every, g_send, g_recv)
-    gather.start_z()
-    gather.start_plane()
-    gather.start_core()
-    gather.finish()
-    in_grad[...] = jnp.zeros_like(in_grad)
-    out_grad[...] = jnp.zeros_like(out_grad)
-    bias_grad[...] = jnp.zeros_like(bias_grad)
-    width = slots.shape[1]
-    rows = 8 * count
-
-    def step(n, carry):
-        at = pl.ds(n * 2, 2)
+    weights = Gather(w_every, w_send, w_recv)
+    weights.start_z()
+    for ref in (weight_grad, sums, table_grad, shift_grad, in_grad, out_grad, bias_grad):
+        ref[...] = jnp.zeros_like(ref)
+    units = w_in.shape[0] // 8
+    spread_bias = dot(own_bias[...], lanes_of(units, 0, width)[:units], 1, 0)
+    at = lax.broadcasted_iota(jnp.int32, spread_bias.shape, 0)
+    lane = lax.broadcasted_iota(jnp.int32, spread_bias.shape, 1)
+    bias[...] = jnp.sum(
+        jnp.where(lane // units == at, spread_bias, 0.0), axis=0, keepdims=True
+    )
+    weights.start_plane()
+    weights.start_core()
+    weights.finish()
+    wt[...] = w_every[:, :, :rows].reshape(4 * width, width)
+    packed = w_every[:, :, rows:].reshape(32 * 16, width)
+    offsets = [sum(lengths[:n]) for n in range(4)]
+    gains, biases, slot_rows, shift_rows = (
+        spread(packed, length, offset) for length, offset in zip(lengths, offsets)
+    )
+    vec[...] = jnp.concatenate([gains, biases, jnp.zeros((2, width), F32)], axis=0)
+    table[...] = slot_rows
+    shift[...] = shift_rows
+
+    def slots_way(i):
+        return Gather(every.at[i], g_send.at[i], g_recv.at[i])
+
+    def results_way(i):
+        ring = lax.rem(i, 3)
+        return Scatter(
+            parts.at[ring], from_core.at[ring], chips.at[ring], from_plane.at[ring],
+            column.at[i], from_z.at[i], s_send.at[i], s_recv.at[i],
+        )
+
+    def for_image(i, action):
+        @pl.when((i >= 0) & (i < count))
+        def _():
+            action(i)
+
+    def experts(i):
+        slots_way(i).finish()
+        both = every[i].astype(F32).reshape(32, 2, 8, width)
         got = expert_rows(
-            every[at, :, :count].reshape(rows, width), every[at, :, count:].reshape(rows, width),
+            both[:, 0].reshape(32 * 8, width).astype(BF16),
+            both[:, 1].reshape(32 * 8, width).astype(BF16),
             w_in[...], bias[...], w_out[...],
         )
-        parts[at, :, :count] = got[0].reshape(2, 4, count, width)
-        parts[at, :, count:] = got[1].reshape(2, 4, count, width)
+        back = jnp.stack([got[0].reshape(32, 8, width), got[1].reshape(32, 8, width)], axis=1)
+        parts[lax.rem(i, 3)] = back.reshape(8, 4, 16, width).astype(BF16)
         in_grad[...] += got[2]
         out_grad[...] += got[3]
         bias_grad[...] += got[4]
+        results_way(i).start_core()
+
+    def middle_of(step):
+        for_image(step - 3, experts)
+
+    def end_of(step):
+        for_image(step - 4, lambda i: results_way(i).start_z())
+        for_image(step - 3, lambda i: results_way(i).start_plane())
+        for_image(step - 2, lambda i: slots_way(i).start_core())
+        for_image(step - 1, lambda i: slots_way(i).start_plane())
+
+    def p_out(i, head):
+        return pltpu.make_async_copy(p.at[head], p_hbm.at[i, head], p_out_sem.at[head])
+
+    def p_in(i, head):
+        return pltpu.make_async_copy(p_hbm.at[i, head], p.at[head], p_in_sem.at[head])
+
+    def forward(i, carry):
+        pltpu.make_async_copy(x_hbm.at[i], x.at[i], x_sem.at[i]).wait()
+        pltpu.make_async_copy(g_hbm.at[i], g.at[i], g_sem.at[i]).wait()
+
+        def before_heads():
+            middle_of(i)
+
+            @pl.when(i > 0)
+            def _():
+                for head in range(heads):
+                    p_out(i - 1, head).wait()
+
+        got = forward_image(
+            x.at[i], g.at[i], valid[pl.ds(i, 1)], wt, vec[...], table[...].astype(BF16),
+            q.at[i], k.at[i], v.at[i], p, att.at[i], inv.at[i],
+            before_heads, lambda head: p_out(i, head).start(),
+        )
+        middle[i], dispatch[i], combine[i] = got[:3]
+        shift_grad[...] += got[4].astype(BF16).astype(F32)
+        every[i, wide, narrow] = jnp.concatenate([got[3], got[4]], axis=0).astype(BF16)
+        end_of(i)
+        slots_way(i).start_z()
         return carry
 
-    lax.fori_loop(0, 4, step, 0)
-    scatter = Scatter(parts, *rest)
+    lax.fori_loop(0, count, forward, 0)
+    for head in range(heads):
+        p_out(count - 1, head).wait()
+        p_in(0, head).start()
+
+    def backward(i, carry):
+        def after_heads():
+            @pl.when(i + 1 < count)
+            def _():
+                for head in range(heads):
+                    p_in(i + 1, head).start()
+
+        total = results_way(i).finish()
+        got = backward_image(
+            x.at[i], g.at[i], middle.at[i], dispatch[i], combine[i],
+            (total[:8] + shift[...]).astype(BF16), total[8:].astype(BF16),
+            wt, vec[...], table[...].astype(BF16),
+            q.at[i], k.at[i], v.at[i], p, att.at[i], inv.at[i], ds, grad_t,
+            q.at[i], k.at[i], v.at[i], g.at[i],
+            lambda: middle_of(count + i), lambda head: p_in(i, head).wait(), after_heads,
+        )
+        pltpu.make_async_copy(g.at[i], mixed_hbm.at[i], mixed_sem.at[i]).start()
+        x[i] = got[0]
+        pltpu.make_async_copy(x.at[i], patch_grad_hbm.at[i], patch_sem.at[i]).start()
+        add_grads(weight_grad, sums, table_grad, got)
+        end_of(count + i)
+        return carry
+
+    lax.fori_loop(0, count, backward, 0)
+
+    sent = last[0]
+    sent[:, :, :rows] = weight_grad[...].reshape(8, 4, rows, width).astype(BF16)
+    sources = (sums[:2], sums[2:6], table_grad[...], shift_grad[...])
+    pieces = [gather_up(s, length, offset) for s, length, offset in zip(sources, lengths, offsets)]
+    total = pieces[0] + pieces[1] + pieces[2] + pieces[3]
+    first_row = lax.broadcasted_iota(jnp.int32, (32, 16, width), 1) == 0
+    total = jnp.where(first_row, jnp.broadcast_to(total[:, None], (32, 16, width)), 0.0)
+    sent[:, :, rows:] = total.reshape(8, 4, 16, width).astype(BF16)
+    scatter = Scatter(*last)
     scatter.start_core()
     scatter.start_plane()
     scatter.start_z()
     total = scatter.finish()
-    produced[...] = total[:count]
-    slot_grad[...] = total[count:]
-
-
-def run_experts(slots, grads, w_in, bias, w_out):
-    count, width = slots.shape
-    units = w_in.shape[0]
-    full = pl.BlockSpec(memory_space=pltpu.VMEM)
-    return pl.pallas_call(
-        experts_kernel,
+    weight_out[...] = total[:rows]
+    vectors_out[...] = total[rows : rows + 1]
+    for i in range(count):
+        pltpu.make_async_copy(g.at[i], mixed_hbm.at[i], mixed_sem.at[i]).wait()
+        pltpu.make_async_copy(x.at[i], patch_grad_hbm.at[i], patch_sem.at[i]).wait()
+
+
+def run_layer(patches, valid, attn_weights, vectors, expert_in, expert_in_bias, expert_out, out_grad):
+    count, length, width = patches.shape
+    heads = width // HEAD_DIM
+    experts, _, units = expert_in.shape
+    rows = attn_weights.shape[1]
+    lengths = [v.shape[0] for v in vectors]
+    packed = jnp.concatenate(list(vectors) + [jnp.zeros((width - sum(lengths),), BF16)])
+    flat = (length, width)
+    dma = pltpu.SemaphoreType.DMA
+    vmem = pltpu.VMEM
+    anywhere = pl.BlockSpec(memory_space=pl.ANY)
+    here_all = pl.BlockSpec(memory_space=pltpu.VMEM)
+    mixed, patch_grad, _, weight_grad, vector_grads, in_grad, out_grads, bias_grad = pl.pallas_call(
+        functools.partial(layer_kernel, lengths),
+        in_specs=[anywhere] * 2 + [here_all] * 6,
+        out_specs=[anywhere] * 3 + [here_all] * 5,
         out_shape=[
-            jax.ShapeDtypeStruct((count, width), F32), jax.ShapeDtypeStruct((count, width), F32),
-            jax.ShapeDtypeStruct((units, width), F32), jax.ShapeDtypeStruct((units, width), F32),
-            jax.ShapeDtypeStruct((1, units), F32),
+            jax.ShapeDtypeStruct(patches.shape, BF16), jax.ShapeDtypeStruct(patches.shape, BF16),
+            jax.ShapeDtypeStruct((count, heads, length, length), BF16),
+            jax.ShapeDtypeStruct((rows, width), F32), jax.ShapeDtypeStruct((1, width), F32),
+            jax.ShapeDtypeStruct((experts * units, width), F32),
+            jax.ShapeDtypeStruct((experts * units, width), F32),
+            jax.ShapeDtypeStruct((1, experts * units), F32),
         ],
-        in_specs=[full] * 5,
-        out_specs=[full] * 5,
-        scratch_shapes=gather_scratch(2 * count, width) + scatter_scratch(2 * count, width),
+        scratch_shapes=[
+            vmem((count,) + flat, BF16), vmem((count,) + flat, BF16),
+            vmem((count,) + flat, BF16), vmem((count,) + flat, BF16), vmem((count,) + flat, BF16),
+            vmem((count,) + flat, BF16), vmem((count,) + flat, BF16), vmem((count,) + flat, F32),
+            vmem((count, experts, length), F32), vmem((count, experts, length), F32),
+            vmem((heads, length, length), BF16), vmem((2, length, length), BF16),
+            vmem((2 * width, length), BF16), vmem((4 * width, width), BF16),
+            vmem((8, width), F32), vmem((experts, width), F32), vmem((experts, width), F32),
+            vmem((1, experts * units), F32),
+            vmem((4 * width, width), F32), vmem((8, width), F32), vmem((experts, width), F32),
+            vmem((experts, width), F32),
+            dma((count,)), dma((count,)), dma((heads,)), dma((heads,)), dma((count,)), dma((count,)),
+        ]
+        + gather_scratch(rows + 16, width)
+        + [vmem((count, 8, 4, 16, width), BF16), dma((count, 10)), dma((count, 10))]
+        + [
+            vmem((3, 8, 4, 16, width), BF16), vmem((3, 4, 4, 16, width), BF16),
+            vmem((3, 4, 4, 16, width), BF16), vmem((3, 3, 4, 16, width), BF16),
+            vmem((count, 4, 16, width), BF16), vmem((count, 3, 16, width), BF16),
+            dma((count, 10)), dma((count, 10)),
+        ]
+        + scatter_scratch(rows + 16, width),
         compiler_params=pltpu.CompilerParams(
-            collective_id=2, has_side_effects=True, vmem_limit_bytes=VMEM_LIMIT
+            collective_id=0, has_side_effects=True, vmem_limit_bytes=LAYER_LIMIT
         ),
-        name="experts",
-    )(slots, grads, w_in, bias, w_out)
+        name="layer",
+    )(
+        patches, out_grad, valid, attn_weights.T, packed.reshape(1, width),
+        expert_in.transpose(0, 2, 1).reshape(experts * units, width), expert_in_bias,
+        expert_out.reshape(experts * units, width),
+    )
+    grads = []
+    at = 0
+    for piece in lengths:
+        grads.append(vector_grads[0, at : at + piece])
+        at += piece
+    return (
+        mixed,
+        patch_grad,
+        weight_grad.T,
+        grads[0],
+        grads[1],
+        grads[2],
+        in_grad.reshape(experts, units, width).transpose(0, 2, 1),
+        bias_grad.reshape(experts, units),
+        out_grads.reshape(experts, units, width),
+        grads[3],
+    )
 
 
 def scatter_sum(parts):
@@ -653,18 +836,12 @@
 
     vectors = (norm_gains, vec_biases, slot_params, expert_out_bias)
     lengths = [v.shape[0] for v in vectors]
-    small = jnp.concatenate(vectors)
-    by_hand = lax.axis_size("wide") == 8 and lax.axis_size("narrow") == 4
-    if by_hand:
-        rows = attn_weights.shape[1]
-        every = run_gather(
-            jnp.concatenate([attn_weights.T, jnp.pad(small[None], ((0, 15), (0, width - small.shape[0])))])
+    if lax.axis_size("wide") == 8 and lax.axis_size("narrow") == 4:
+        return run_layer(
+            patches, valid, attn_weights, vectors, expert_in, expert_in_bias, expert_out, out_grad
         )
-        wt = every[:, :, :rows].reshape(-1, width)
-        small = every[:, :, rows].reshape(devices, width)
-    else:
-        wt = lax.all_gather(attn_weights.T, AXES, axis=0, tiled=True)
-        small = lax.all_gather(small, AXES)
+    wt = lax.all_gather(attn_weights.T, AXES, axis=0, tiled=True)
+    small = lax.all_gather(jnp.concatenate(vectors), AXES)
     pieces = []
     at = 0
     for length in lengths:
@@ -676,23 +853,9 @@
     *kept, slots, produced_grad = run_forward(
         patches, out_grad, valid.reshape(local_images, 1, patch_count), wt, vec, table
     )
-    if by_hand:
-        units = expert_in.shape[2]
-        produced, slot_grad, expand_grad, contract_grad, inner_grad = run_experts(
-            slots.reshape(-1, width), produced_grad.reshape(-1, width),
-            expert_in.transpose(0, 2, 1).reshape(experts * units, width),
-            expert_in_bias.reshape(1, experts * units).astype(F32),
-            expert_out.reshape(experts * units, width),
-        )
-        produced = produced.reshape(slots.shape)
-        slot_grad = slot_grad.reshape(slots.shape)
-        expand_grad = expand_grad.reshape(experts, units, width).transpose(0, 2, 1)
-        contract_grad = contract_grad.reshape(experts, units, width)
-        inner_grad = inner_grad.reshape(experts, units)
-    else:
-        produced, slot_grad, expand_grad, inner_grad, contract_grad = experts_at_home(
-            slots, produced_grad, expert_in, expert_in_bias, expert_out, devices
-        )
+    produced, slot_grad, expand_grad, inner_grad, contract_grad = experts_at_home(
+        slots, produced_grad, expert_in, expert_in_bias, expert_out, devices
+    )
     produced = (produced + expert_shift.astype(F32)).astype(BF16)
     slot_grad = slot_grad.astype(BF16)
     shift_grad = jnp.sum(produced_grad.astype(F32), axis=0)
@@ -703,16 +866,8 @@
     small_grads = jnp.concatenate(
         [v.reshape(devices, -1) for v in (rows[:2], rows[2:6], table_grad, shift_grad)], axis=1
     )
-    if by_hand:
-        small_grads = jnp.pad(
-            small_grads[:, None], ((0, 0), (0, 15), (0, width - small_grads.shape[1]))
-        )
-        total = run_scatter(jnp.concatenate([weight_grad, small_grads], axis=1))
-        small_grads = total[weight_grad.shape[1]]
-        weight_grad = total[: weight_grad.shape[1]].T
-    else:
-        weight_grad = scatter_sum(weight_grad).T
-        small_grads = jnp.sum(lax.all_to_all(small_grads, AXES, 0, 0, tiled=True), axis=0)
+    weight_grad = scatter_sum(weight_grad).T
+    small_grads = jnp.sum(lax.all_to_all(small_grads, AXES, 0, 0, tiled=True), axis=0)
     grads = []
     at = 0
     for length in lengths:

time: 227 us -> 165 us (0.73)
  Pallas kernels: 197 us -> 148 us
  other arithmetic: 11.2 us -> 0.64 us
    pallas_call x5 -> x1, Pallas kernels: 197 us -> 148 us  [run_layer(): pl.pallas_call(functools.partial(layer_kernel, lengths), in_specs=[anywhe...]
    slice x9 -> x0, local copies, waits for them, and re-layouts: 8.77 us -> none  [the longest x3 3.78 us: on_device(): grads.append(small_grads[at:at + length])]
    concatenate x4 -> x0, other arithmetic: 5.98 us -> none  [the longest x1 3.71 us: on_device(): total = run_scatter(jnp.concatenate([weight_grad, small_grads], axis=1))]
    unnamed x6 -> x13, local copies, waits for them, and re-layouts: 1.64 us -> 7.45 us
    convert_element_type x4 -> x0, other arithmetic: 3.74 us -> none  [the longest x2 1.59 us: on_device(): produced = (produced + expert_shift.astype(F32)).astype(BF16)]
    squeeze x0 -> x3, local copies, waits for them, and re-layouts: none -> 3.74 us  [run_layer(): grads.append(vector_grads[0, at:at + piece])]
    concatenate x1, local copies, waits for them, and re-layouts: 0.08 us -> 2.77 us  [run_layer(): jnp.concatenate(list(vectors) + [jnp.zeros((width - sum(lengths),), BF16)])]
    reshape x9 -> x2, local copies, waits for them, and re-layouts: 3.89 us -> 1.25 us  [the longest x1 0.68 us: run_layer(): bias_grad.reshape(experts, units)]
where the time goes in v4:
time: 165 us
  Pallas kernels  148 us (90%)
  local copies, waits for them, and re-layouts  15.2 us (9%)
    pallas_call x1, Pallas kernels, run_layer(): pl.pallas_call(functools.partial(layer_kernel, lengths), in_specs=[anywhe...  148 us
    unnamed x13, local copies, waits for them, and re-layouts  7.45 us
    squeeze x3, local copies, waits for them, and re-layouts, run_layer(): grads.append(vector_grads[0, at:at + piece])  3.74 us

profile of v4, /device:TPU:0, one launch (start us, length us, event | category | flops | bytes accessed | tf_op | source)
XLA Modules:
  0.0 164.9 jit_solution(6468547998704063407)
XLA Ops:
  0.7 2.8 %concatenate.3 = bf16[384]{0:T(512)(128)(2,1)S(1)} concatenate(bf16[24]{0:T(256)(128)(2,1)} %param.14, bf16[48]{0:T(256)(128)(2,1)} %param.15, bf16[96]{0:T(256)(128)(2,1)} %param.16, bf16[96]{0:T(256)(128)(2,1)} %param.20, bf16[120]{0:T(256)(128)(2,1)S(1)} %broadcast_in_dim.3), dimensions={0} | concatenate | bytes 1536 | tf_op jit(solution)/shard_map/concatenate | solution.py:726
  3.4 0.6 reshape.38.own_vectors
  4.0 148.4 %layer.1 = (bf16[6,576,384]{2,1,0:T(8,128)(2,1)}, bf16[6,576,384]{2,1,0:T(8,128)(2,1)}, bf16[6,6,576,576]{3,2,1,0:T(8,128)(2,1)}, f32[48,384]{1,0:T(8,128)}, f32...) custom-call(bf16[6,576,384]{2,1,0:T(8,128)(2,1)} %x_hbm.1, ...), custom_call_target="tpu_custom_call" | custom-call | tf_op jit(solution)/shard_map/layer/pallas_call | solution.py:732
  152.4 1.2 slice_bitcast_fusion.2
  153.6 1.2 slice_bitcast_fusion.3
  154.8 1.3 slice_bitcast_fusion
  156.1 0.6 reduce
  156.8 0.7 reshape.42
  157.4 0.0 copy-start
  157.4 3.7 %copy.26 = bf16[6,576,384]{2,1,0:T(8,128)(2,1)} copy(bf16[6,576,384]{2,1,0:T(8,128)(2,1)} %get-tuple-element.36) | data formatting | bytes 5308416
  161.1 0.0 copy-done
  161.1 0.0 copy-start.3
  161.1 0.0 copy-start.2
  161.1 0.0 copy-start.1
  161.1 1.5 copy.27
  162.6 0.0 copy-done.3
  162.6 0.6 copy.28
  163.3 0.0 copy-done.2
  163.3 0.8 copy.29
  164.1 0.0 copy-done.1
  164.1 0.8 copy.30
  (1 shorter events, 0.0 us)
Async XLA Ops:
  157.4 3.7 %copy-start = (bf16[6,576,384]{2,1,0:T(8,128)(2,1)S(1)}, bf16[6,576,384]{2,1,0:T(8,128)(2,1)}, u32[]{:S(2)}) copy-start(bf16[6,576,384]{2,1,0:T(8,128)(2,1)} %get-tuple-element.37) | copy-start | bytes 7962628
  161.1 1.5 copy-start.3
  161.1 2.2 %copy-start.2 = (f32[384,384]{1,0:T(8,128)S(1)}, f32[384,384]{1,0:T(8,128)}, u32[]{:S(2)}) copy-start(f32[384,384]{1,0:T(8,128)} %get-tuple-element.21) | copy-start | bytes 1769476
  161.1 3.0 %copy-start.1 = (f32[384,384]{1,0:T(8,128)S(1)}, f32[384,384]{1,0:T(8,128)}, u32[]{:S(2)}) copy-start(f32[384,384]{1,0:T(8,128)} %get-tuple-element.23) | copy-start | bytes 1769476

commit v5 on v4

--- a/solution.py
+++ b/solution.py
@@ -117,7 +117,8 @@
 
 def backward_image(
     x, g, middle_ref, dispatch, combine, produced, slot_grad, wt, vec, table,
-    q_ref, k_ref, v_ref, p_ref, att_ref, inv_ref, ds_ref, grad_t_ref, dq_ref, dk_ref, dv_ref, mixed_ref,
+    q_ref, k_ref, v_ref, p_ref, att_ref, inv_ref, ds_ref, grad_t_ref, dq_ref, dk_ref, dv_ref,
+    mixed_ref, grad_ref,
     before_heads=None, before_head=None, after_heads=None,
 ):
     patches, width = x.shape
@@ -148,6 +149,7 @@
         second_grad * vec[GAIN2 : GAIN2 + 1], normed, factor
     )
     mixed_ref[...] = mixed
+    grad_ref[...] = middle_grad
     branch_grad = middle_grad.astype(BF16)
     branch_shift = jnp.sum(branch_grad.astype(F32), axis=0, keepdims=True)
     output_grad = dot(branch_grad.T, att_ref[...], 1, 0)
@@ -201,21 +203,40 @@
         after_heads()
     dk_ref[...] = grad_t_ref[:width, :].T
     dv_ref[...] = grad_t_ref[width:, :].T
-    normed, factor = normalize(x[...].astype(F32))
+    normed, _ = normalize(x[...].astype(F32))
     first = (normed * vec[GAIN1 : GAIN1 + 1] + vec[BIAS1 : BIAS1 + 1]).astype(BF16)
     query_front = dot(dq_ref[...].T, first, 1, 0)
     other_front = dot(grad_t_ref[...], first, 1, 0)
-    value_shift = jnp.sum(dv_ref[...].astype(F32), axis=0, keepdims=True)
+    columns = [
+        jnp.sum(ref[...].astype(F32), axis=0, keepdims=True) for ref in (dq_ref, dk_ref, dv_ref)
+    ]
+    sums = jnp.concatenate(
+        columns + [gain_two, branch_shift, shift_two, jnp.zeros((2, width), F32)], axis=0
+    )
+    return query_front, other_front, output_grad, sums, table_grad
+
+
+def finish_image(x, middle_grad, wt, vec, dq_ref, dk_ref, dv_ref):
+    width = x.shape[1]
+    normed, factor = normalize(x[...].astype(F32))
     project_grad = jnp.concatenate([dq_ref[...], dk_ref[...], dv_ref[...]], axis=1)
     first_grad = dot(project_grad, wt[: 3 * width], 1, 0)
-    gain_one = jnp.sum(first_grad * normed, axis=0, keepdims=True)
-    shift_one = jnp.sum(first_grad, axis=0, keepdims=True)
-    patch_grad = middle_grad + norm_back(first_grad * vec[GAIN1 : GAIN1 + 1], normed, factor)
-    sums = jnp.concatenate(
-        [gain_one, gain_two, shift_one, value_shift, branch_shift, shift_two, jnp.zeros((2, width), F32)],
-        axis=0,
-    )
-    return patch_grad.astype(BF16), query_front, other_front, output_grad, sums, table_grad
+    grad = middle_grad[...] + norm_back(first_grad * vec[GAIN1 : GAIN1 + 1], normed, factor)
+    return grad.astype(BF16)
+
+
+def norm_sums(sums, weight_grad, wt, vec):
+    width = wt.shape[1]
+    high = sums.astype(BF16)
+    both = jnp.concatenate([high, (sums - high.astype(F32)).astype(BF16)], axis=0)
+    shift_one = jnp.zeros((1, width), F32)
+    for part in range(3):
+        got = dot(both, wt[part * width : (part + 1) * width], 1, 0)
+        shift_one += got[part : part + 1] + got[8 + part : 9 + part]
+    product = jnp.sum(weight_grad * wt[: 3 * width].astype(F32), axis=0, keepdims=True)
+    gain_one = (product - vec[BIAS1 : BIAS1 + 1] * shift_one) / vec[GAIN1 : GAIN1 + 1]
+    gains = jnp.concatenate([gain_one, sums[3:4]], axis=0)
+    return gains, jnp.concatenate([shift_one, sums[2:3], sums[4:5], sums[5:6]], axis=0)
 
 
 def forward_kernel(
@@ -233,8 +254,8 @@
 def add_grads(weight_grad, sums, table_grad, got):
     width = weight_grad.shape[1]
     for ref, at, value in (
-        (weight_grad, 0, got[1]), (weight_grad, width, got[2]), (weight_grad, 3 * width, got[3]),
-        (sums, 0, got[4]), (table_grad, 0, got[5]),
+        (weight_grad, 0, got[0]), (weight_grad, width, got[1]), (weight_grad, 3 * width, got[2]),
+        (sums, 0, got[3]), (table_grad, 0, got[4]),
     ):
         ref[at : at + value.shape[0], :] += value
 
@@ -243,7 +264,7 @@
     x, g, middle, dispatch, combine, produced, slot_grad, wt, vec, table,
     q, k, v, p, att, inv,
     mixed, patch_grad, weight_grad, sums, table_grad,
-    ds, grad_t, dq, dk, dv,
+    ds, grad_t, dq, dk, dv, middle_grad,
 ):
     @pl.when(pl.program_id(0) == 0)
     def _():
@@ -254,9 +275,10 @@
     got = backward_image(
         x.at[0], g.at[0], middle.at[0], dispatch[0], combine[0], produced[0], slot_grad[0],
         wt, vec[...], table[...],
-        q.at[0], k.at[0], v.at[0], p.at[0], att.at[0], inv.at[0], ds, grad_t, dq, dk, dv, mixed.at[0],
-    )
-    patch_grad[0] = got[0]
+        q.at[0], k.at[0], v.at[0], p.at[0], att.at[0], inv.at[0], ds, grad_t, dq, dk, dv,
+        mixed.at[0], middle_grad,
+    )
+    patch_grad[0] = finish_image(x.at[0], middle_grad, wt, vec[...], dq, dk, dv)
     add_grads(weight_grad, sums, table_grad, got)
 
 
@@ -325,6 +347,7 @@
             pltpu.VMEM(flat, BF16),
             pltpu.VMEM(flat, BF16),
             pltpu.VMEM(flat, BF16),
+            pltpu.VMEM(flat, F32),
         ],
         compiler_params=pltpu.CompilerParams(vmem_limit_bytes=VMEM_LIMIT),
         name="backward",
@@ -383,13 +406,11 @@
             for n, peer in enumerate(in_plane(self.w, self.z))
         ]
 
-    def core_copies(self):
-        peer = other_core(self.w, self.z)
-        groups = [self.w] + [there for there, _ in in_plane(self.w, self.z)]
-        return [
-            remote(self.every.at[g], self.every.at[g], self.send.at[6 + n], self.recv.at[6 + n], peer)
-            for n, g in enumerate(groups)
-        ]
+    def core_copy(self, n, group):
+        own = self.every.at[group]
+        return remote(
+            own, own, self.send.at[6 + n], self.recv.at[6 + n], other_core(self.w, self.z)
+        )
 
     def start_z(self):
         for copy in self.z_copies():
@@ -400,16 +421,17 @@
             copy.wait()
         for copy in self.plane_copies():
             copy.start()
-        self.core_copies()[0].start()
+        self.core_copy(0, self.w).start()
 
     def start_core(self):
-        for copy, onward in zip(self.plane_copies(), self.core_copies()[1:]):
+        peers = in_plane(self.w, self.z)
+        for n, (copy, peer) in enumerate(zip(self.plane_copies(), peers)):
             copy.wait()
-            onward.start()
+            self.core_copy(n + 1, peer[0]).start()
 
     def finish(self):
-        for copy in self.core_copies():
-            copy.wait()
+        for n in range(4):
+            self.core_copy(n, self.w).wait()
 
 
 class Scatter:
@@ -420,15 +442,14 @@
         self.w, self.z = here()
         self.core = lax.rem(self.w, 2)
 
-    def core_copies(self):
-        peer = other_core(self.w, self.z)
-        return [
-            remote(
-                self.parts.at[2 * chip + 1 - self.core], self.from_core.at[chip],
-                self.send.at[chip], self.recv.at[chip], peer,
-            )
-            for chip in range(4)
-        ]
+    def core_copy(self, chip):
+        return remote(
+            self.parts.at[2 * chip + 1 - self.core], self.from_core.at[chip],
+            self.send.at[chip], self.recv.at[chip], other_core(self.w, self.z),
+        )
+
+    def chip_order(self):
+        return [there // 2 for there, _ in in_plane(self.w, self.z)] + [self.w // 2]
 
     def plane_copies(self):
         return [
@@ -449,16 +470,17 @@
         ]
 
     def start_core(self):
-        for copy in self.core_copies():
-            copy.start()
+        for chip in self.chip_order():
+            self.core_copy(chip).start()
 
     def start_plane(self):
-        for chip, copy in enumerate(self.core_copies()):
-            copy.wait()
+        onward = self.plane_copies() + [None]
+        for chip, copy in zip(self.chip_order(), onward):
+            self.core_copy(chip).wait()
             own = self.parts[2 * chip + self.core].astype(F32)
             self.chips[chip] = (own + self.from_core[chip].astype(F32)).astype(BF16)
-        for copy in self.plane_copies():
-            copy.start()
+            if copy is not None:
+                copy.start()
 
     def start_z(self):
         for copy in self.plane_copies():
@@ -477,6 +499,67 @@
         for n in range(3):
             total = total + self.from_z[n].astype(F32)
         return total
+
+
+class FineGather:
+    def __init__(self, every, z_send, z_recv, p_send, p_recv, c_send, c_recv):
+        self.every = every
+        self.z_sems, self.p_sems, self.c_sems = (z_send, z_recv), (p_send, p_recv), (c_send, c_recv)
+        self.w, self.z = here()
+        self.plane = in_plane(self.w, self.z)
+
+    def block(self, w, k):
+        return self.every.at[w, lax.rem(self.z + 4 - k, 4)]
+
+    def z_copy(self, n):
+        own = self.block(self.w, 0)
+        peer = along_z(self.w, self.z)[n]
+        return remote(own, own, self.z_sems[0].at[n], self.z_sems[1].at[n], peer)
+
+    def plane_copy(self, n, k):
+        own = self.block(self.w, k)
+        return remote(own, own, self.p_sems[0].at[n, k], self.p_sems[1].at[n, k], self.plane[n])
+
+    def core_copy(self, group, k):
+        own = self.block(self.w if group == 0 else self.plane[group - 1][0], k)
+        return remote(
+            own, own, self.c_sems[0].at[group, k], self.c_sems[1].at[group, k],
+            other_core(self.w, self.z),
+        )
+
+    def pass_on(self, k):
+        for n in range(3):
+            self.plane_copy(n, k).start()
+        self.core_copy(0, k).start()
+
+    def start(self):
+        for n in range(3):
+            self.z_copy(n).start()
+        self.pass_on(0)
+
+    def start_plane(self):
+        for n in range(3):
+            self.z_copy(n).wait()
+            self.pass_on(n + 1)
+
+    def start_core(self):
+        for k in range(4):
+            for n in range(3):
+                self.plane_copy(n, k).wait()
+                self.core_copy(n + 1, k).start()
+
+    def finish(self):
+        for group in range(4):
+            for k in range(4):
+                self.core_copy(group, k).wait()
+
+
+def fine_scratch(rows, width):
+    dma = pltpu.SemaphoreType.DMA
+    return [
+        pltpu.VMEM((8, 4, rows, width), BF16),
+        dma((3,)), dma((3,)), dma((3, 4)), dma((3, 4)), dma((4, 4)), dma((4, 4)),
+    ]
 
 
 def gather_scratch(rows, width):
@@ -517,86 +600,91 @@
     slot_grad = dot(hidden_grad, w_in, 1, 0)
     in_grad = dot(hidden_grad, slots, 0, 0)
     out_grad = dot(active, grads, 0, 0)
-    bias_grad = jnp.sum(hidden_grad.astype(F32), axis=0, keepdims=True)
+    bias_grad = jnp.sum(hidden_grad.astype(F32).reshape(-1, 8, units), axis=0)
     return produced, slot_grad, in_grad, out_grad, bias_grad
 
 
-def lanes_of(length, offset, width, transposed=False):
-    row = lax.broadcasted_iota(jnp.int32, (width, width), 1 if transposed else 0)
-    column = lax.broadcasted_iota(jnp.int32, (width, width), 0 if transposed else 1)
-    return (row == offset + lax.rem(column, length)).astype(BF16)
-
-
-def spread(blocks, length, offset):
-    width = blocks.shape[1]
-    per_row = width // length
-    wide = dot(blocks, lanes_of(length, offset, width), 1, 0)
-    row = lax.broadcasted_iota(jnp.int32, wide.shape, 0)
-    column = lax.broadcasted_iota(jnp.int32, wide.shape, 1)
-    keep = (lax.rem(row, 16) == 0) & (lax.rem(row // 16, per_row) == column // length)
-    wide = jnp.where(keep, wide, 0.0)
-    return jnp.sum(wide.reshape(-1, per_row * 16, width), axis=1)
-
-
-def gather_up(rows, length, offset):
+def one_hot(length, width):
+    row = lax.broadcasted_iota(jnp.int32, (128, width), 0)
+    column = lax.broadcasted_iota(jnp.int32, (128, width), 1)
+    return (row == lax.rem(column, length)).astype(BF16)
+
+
+def own_piece(shape, length):
+    device = lax.broadcasted_iota(jnp.int32, shape, 0)
+    column = lax.broadcasted_iota(jnp.int32, shape, 1)
+    return lax.rem(device, shape[1] // length) == column // length
+
+
+def spread(pieces, length, width):
+    devices = pieces.shape[0]
+    tall = dot(pieces.astype(BF16), one_hot(length, width), 1, 0)
+    tall = jnp.where(own_piece(tall.shape, length), tall, 0.0).astype(BF16)
+    row = lax.broadcasted_iota(jnp.int32, (8, devices), 0)
+    device = lax.broadcasted_iota(jnp.int32, (8, devices), 1)
+    return dot((device // (width // length) == row).astype(BF16), tall, 1, 0)
+
+
+def pieces_of(rows, length, devices):
     count, width = rows.shape
     per_row = width // length
-    tall = jnp.broadcast_to(rows[:, None], (count, per_row, width)).reshape(32, width)
-    row = lax.broadcasted_iota(jnp.int32, tall.shape, 0)
-    column = lax.broadcasted_iota(jnp.int32, tall.shape, 1)
-    tall = jnp.where(lax.rem(row, per_row) == column // length, tall, 0.0)
-    return dot(tall.astype(BF16), lanes_of(length, offset, width, True), 1, 0)
+    tall = jnp.broadcast_to(rows[:, None], (count, per_row, width)).reshape(devices, width)
+    tall = jnp.where(own_piece(tall.shape, length), tall, 0.0)
+    return dot(tall.astype(BF16), one_hot(length, width), 1, 1)
 
 
 def layer_kernel(
     lengths,
-    x_hbm, g_hbm, valid, own_weights, own_vectors, w_in, own_bias, w_out,
+    x_hbm, g_hbm, valid, own_weights, own_gains, own_biases, own_table, own_shift, w_in, own_bias, w_out,
     mixed_hbm, patch_grad_hbm, p_hbm, weight_out, vectors_out, in_grad, out_grad, bias_grad,
     x, g, q, k, v, att, inv, middle, dispatch, combine, p, ds, grad_t, wt, vec, table, shift, bias,
-    weight_grad, sums, table_grad, shift_grad,
+    weight_grad, sums, table_grad, shift_grad, own_pieces,
     x_sem, g_sem, p_out_sem, p_in_sem, mixed_sem, patch_sem,
-    w_every, w_send, w_recv,
     every, g_send, g_recv,
     parts, from_core, chips, from_plane, column, from_z, s_send, s_recv,
-    *last,
+    *rest,
 ):
     count, patches, width = x.shape
     heads = width // HEAD_DIM
     rows = own_weights.shape[0]
     wide, narrow = here()
+    (w_every, *w_sems), (v_every, *v_sems) = rest[:7], rest[7:10]
+    w_last, v_last = rest[10:18], rest[18:26]
 
     for i in range(count):
         pltpu.make_async_copy(x_hbm.at[i], x.at[i], x_sem.at[i]).start()
         pltpu.make_async_copy(g_hbm.at[i], g.at[i], g_sem.at[i]).start()
-    w_every[wide, narrow, :rows] = own_weights[...]
-    row = lax.broadcasted_iota(jnp.int32, (16, width), 0)
-    w_every[wide, narrow, rows:] = jnp.where(
-        row == 0, jnp.broadcast_to(own_vectors[...].astype(F32), (16, width)), 0.0
-    ).astype(BF16)
+    w_every[wide, narrow] = own_weights[...]
+    own_pieces[...] = jnp.zeros_like(own_pieces)
+    for n, ref in enumerate((own_gains, own_biases, own_table, own_shift)):
+        own_pieces[n : n + 1, : lengths[n]] = ref[...].astype(F32).reshape(1, lengths[n])
+    v_every[wide, narrow] = own_pieces[...].astype(BF16)
     greet()
-    weights = Gather(w_every, w_send, w_recv)
-    weights.start_z()
+    weights = FineGather(w_every, *w_sems)
+    vectors = Gather(v_every, *v_sems)
+    vectors.start_z()
+    weights.start()
     for ref in (weight_grad, sums, table_grad, shift_grad, in_grad, out_grad, bias_grad):
         ref[...] = jnp.zeros_like(ref)
     units = w_in.shape[0] // 8
-    spread_bias = dot(own_bias[...], lanes_of(units, 0, width)[:units], 1, 0)
+    spread_bias = dot(own_bias[...], one_hot(units, 8 * units)[:units], 1, 0)
     at = lax.broadcasted_iota(jnp.int32, spread_bias.shape, 0)
     lane = lax.broadcasted_iota(jnp.int32, spread_bias.shape, 1)
-    bias[...] = jnp.sum(
-        jnp.where(lane // units == at, spread_bias, 0.0), axis=0, keepdims=True
-    )
+    bias[...] = jnp.sum(jnp.where(lane // units == at, spread_bias, 0.0), axis=0, keepdims=True)
+    vectors.start_plane()
     weights.start_plane()
+    vectors.start_core()
     weights.start_core()
-    weights.finish()
-    wt[...] = w_every[:, :, :rows].reshape(4 * width, width)
-    packed = w_every[:, :, rows:].reshape(32 * 16, width)
-    offsets = [sum(lengths[:n]) for n in range(4)]
+    vectors.finish()
+    packed = v_every[...].astype(F32).reshape(32, 16, 128)
     gains, biases, slot_rows, shift_rows = (
-        spread(packed, length, offset) for length, offset in zip(lengths, offsets)
-    )
-    vec[...] = jnp.concatenate([gains, biases, jnp.zeros((2, width), F32)], axis=0)
+        spread(packed[:, n], length, width) for n, length in enumerate(lengths)
+    )
+    vec[...] = jnp.concatenate([gains[:2], biases[:4], jnp.zeros((2, width), F32)], axis=0)
     table[...] = slot_rows
     shift[...] = shift_rows
+    weights.finish()
+    wt[...] = w_every[...].reshape(4 * width, width)
 
     def slots_way(i):
         return Gather(every.at[i], g_send.at[i], g_recv.at[i])
@@ -685,36 +773,83 @@
             (total[:8] + shift[...]).astype(BF16), total[8:].astype(BF16),
             wt, vec[...], table[...].astype(BF16),
             q.at[i], k.at[i], v.at[i], p, att.at[i], inv.at[i], ds, grad_t,
-            q.at[i], k.at[i], v.at[i], g.at[i],
+            q.at[i], k.at[i], v.at[i], g.at[i], middle.at[i],
             lambda: middle_of(count + i), lambda head: p_in(i, head).wait(), after_heads,
         )
         pltpu.make_async_copy(g.at[i], mixed_hbm.at[i], mixed_sem.at[i]).start()
-        x[i] = got[0]
-        pltpu.make_async_copy(x.at[i], patch_grad_hbm.at[i], patch_sem.at[i]).start()
         add_grads(weight_grad, sums, table_grad, got)
         end_of(count + i)
         return carry
 
     lax.fori_loop(0, count, backward, 0)
 
-    sent = last[0]
-    sent[:, :, :rows] = weight_grad[...].reshape(8, 4, rows, width).astype(BF16)
-    sources = (sums[:2], sums[2:6], table_grad[...], shift_grad[...])
-    pieces = [gather_up(s, length, offset) for s, length, offset in zip(sources, lengths, offsets)]
-    total = pieces[0] + pieces[1] + pieces[2] + pieces[3]
-    first_row = lax.broadcasted_iota(jnp.int32, (32, 16, width), 1) == 0
-    total = jnp.where(first_row, jnp.broadcast_to(total[:, None], (32, 16, width)), 0.0)
-    sent[:, :, rows:] = total.reshape(8, 4, 16, width).astype(BF16)
-    scatter = Scatter(*last)
-    scatter.start_core()
-    scatter.start_plane()
-    scatter.start_z()
-    total = scatter.finish()
-    weight_out[...] = total[:rows]
-    vectors_out[...] = total[rows : rows + 1]
+    w_last[0][...] = weight_grad[...].reshape(8, 4, rows, width).astype(BF16)
+    weights = Scatter(*w_last)
+    weights.start_core()
+    gains, biases = norm_sums(sums[...], weight_grad[: 3 * width, :], wt, vec[...])
+    pieces = [
+        pieces_of(value, length, 32)
+        for value, length in zip((gains, biases, table_grad[...], shift_grad[...]), lengths)
+    ]
+    pieces.append(jnp.zeros((32, 128), F32))
+    pieces = jnp.stack([pieces[min(n, 4)] for n in range(16)], axis=1)
+    v_last[0][...] = pieces.reshape(8, 4, 16, 128).astype(BF16)
+    vectors = Scatter(*v_last)
+    vectors.start_core()
+    weights.start_plane()
+    vectors.start_plane()
+
+    def finish(i, carry):
+        x[i] = finish_image(x.at[i], middle.at[i], wt, vec[...], q.at[i], k.at[i], v.at[i])
+        pltpu.make_async_copy(x.at[i], patch_grad_hbm.at[i], patch_sem.at[i]).start()
+
+        @pl.when(i == count // 2)
+        def _():
+            weights.start_z()
+            vectors.start_z()
+
+        return carry
+
+    lax.fori_loop(0, count, finish, 0)
+    weight_out[...] = weights.finish()
+    vectors_out[...] = vectors.finish()
     for i in range(count):
         pltpu.make_async_copy(g.at[i], mixed_hbm.at[i], mixed_sem.at[i]).wait()
         pltpu.make_async_copy(x.at[i], patch_grad_hbm.at[i], patch_sem.at[i]).wait()
+
+
+def hand_over_kernel(
+    mixed, patch_grad, weight_grad, in_grad, out_grad, vectors, bias_grad,
+    mixed_out, patch_grad_out, weight_out, in_out, out_out, gains, biases, table, shift, bias_out,
+    images, weights, arrived, left,
+):
+    count = mixed.shape[0]
+    moves = []
+    for n, (src, dst) in enumerate(((mixed, mixed_out), (patch_grad, patch_grad_out))):
+        moves += [(src.at[i], images.at[n, i], dst.at[i]) for i in range(count)]
+    at = 0
+    for src, dst in ((weight_grad, weight_out), (in_grad, in_out), (out_grad, out_out)):
+        moves.append((src, weights.at[pl.ds(at, src.shape[0])], dst))
+        at += src.shape[0]
+    copies = [
+        (
+            pltpu.make_async_copy(src, stage, arrived.at[n]),
+            pltpu.make_async_copy(stage, dst, left.at[n]),
+        )
+        for n, (src, stage, dst) in enumerate(moves)
+    ]
+    for come, _ in copies:
+        come.start()
+    for n, ref in enumerate((gains, biases, table, shift)):
+        ref[...] = vectors[n : n + 1, : ref.shape[0]].reshape(ref.shape[0])
+    experts, units = bias_out.shape
+    for e in range(experts):
+        bias_out[e : e + 1, :] = bias_grad[e : e + 1, e * units : (e + 1) * units]
+    for come, go in copies:
+        come.wait()
+        go.start()
+    for _, go in copies:
+        go.wait()
 
 
 def run_layer(patches, valid, attn_weights, vectors, expert_in, expert_in_bias, expert_out, out_grad):
@@ -723,7 +858,6 @@
     experts, _, units = expert_in.shape
     rows = attn_weights.shape[1]
     lengths = [v.shape[0] for v in vectors]
-    packed = jnp.concatenate(list(vectors) + [jnp.zeros((width - sum(lengths),), BF16)])
     flat = (length, width)
     dma = pltpu.SemaphoreType.DMA
     vmem = pltpu.VMEM
@@ -731,15 +865,15 @@
     here_all = pl.BlockSpec(memory_space=pltpu.VMEM)
     mixed, patch_grad, _, weight_grad, vector_grads, in_grad, out_grads, bias_grad = pl.pallas_call(
         functools.partial(layer_kernel, lengths),
-        in_specs=[anywhere] * 2 + [here_all] * 6,
+        in_specs=[anywhere] * 2 + [here_all] * 9,
         out_specs=[anywhere] * 3 + [here_all] * 5,
         out_shape=[
             jax.ShapeDtypeStruct(patches.shape, BF16), jax.ShapeDtypeStruct(patches.shape, BF16),
             jax.ShapeDtypeStruct((count, heads, length, length), BF16),
-            jax.ShapeDtypeStruct((rows, width), F32), jax.ShapeDtypeStruct((1, width), F32),
+            jax.ShapeDtypeStruct((rows, width), F32), jax.ShapeDtypeStruct((16, 128), F32),
             jax.ShapeDtypeStruct((experts * units, width), F32),
             jax.ShapeDtypeStruct((experts * units, width), F32),
-            jax.ShapeDtypeStruct((1, experts * units), F32),
+            jax.ShapeDtypeStruct((experts, experts * units), F32),
         ],
         scratch_shapes=[
             vmem((count,) + flat, BF16), vmem((count,) + flat, BF16),
@@ -751,10 +885,9 @@
             vmem((8, width), F32), vmem((experts, width), F32), vmem((experts, width), F32),
             vmem((1, experts * units), F32),
             vmem((4 * width, width), F32), vmem((8, width), F32), vmem((experts, width), F32),
-            vmem((experts, width), F32),
+            vmem((experts, width), F32), vmem((16, 128), F32),
             dma((count,)), dma((count,)), dma((heads,)), dma((heads,)), dma((count,)), dma((count,)),
         ]
-        + gather_scratch(rows + 16, width)
         + [vmem((count, 8, 4, 16, width), BF16), dma((count, 10)), dma((count, 10))]
         + [
             vmem((3, 8, 4, 16, width), BF16), vmem((3, 4, 4, 16, width), BF16),
@@ -762,32 +895,46 @@
             vmem((count, 4, 16, width), BF16), vmem((count, 3, 16, width), BF16),
             dma((count, 10)), dma((count, 10)),
         ]
-        + scatter_scratch(rows + 16, width),
+        + fine_scratch(rows, width) + gather_scratch(16, 128)
+        + scatter_scratch(rows, width) + scatter_scratch(16, 128),
         compiler_params=pltpu.CompilerParams(
             collective_id=0, has_side_effects=True, vmem_limit_bytes=LAYER_LIMIT
         ),
         name="layer",
     )(
-        patches, out_grad, valid, attn_weights.T, packed.reshape(1, width),
+        patches, out_grad, valid, attn_weights.T, *vectors,
         expert_in.transpose(0, 2, 1).reshape(experts * units, width), expert_in_bias,
         expert_out.reshape(experts * units, width),
     )
-    grads = []
-    at = 0
-    for piece in lengths:
-        grads.append(vector_grads[0, at : at + piece])
-        at += piece
+    results = pl.pallas_call(
+        hand_over_kernel,
+        in_specs=[anywhere] * 5 + [here_all] * 2,
+        out_specs=[anywhere] * 5 + [here_all] * 5,
+        out_shape=[
+            jax.ShapeDtypeStruct(value.shape, value.dtype)
+            for value in (mixed, patch_grad, weight_grad, in_grad, out_grads)
+        ]
+        + [jax.ShapeDtypeStruct((piece,), F32) for piece in lengths]
+        + [jax.ShapeDtypeStruct((experts, units), F32)],
+        scratch_shapes=[
+            vmem((2,) + patches.shape, BF16), vmem((rows + 2 * experts * units, width), F32),
+            dma((2 * count + 3,)), dma((2 * count + 3,)),
+        ],
+        compiler_params=pltpu.CompilerParams(vmem_limit_bytes=VMEM_LIMIT),
+        name="hand_over",
+    )(mixed, patch_grad, weight_grad, in_grad, out_grads, vector_grads, bias_grad)
+    mixed, patch_grad, weight_grad, in_grad, out_grads, gains, biases, table, shift, bias_grad = results
     return (
         mixed,
         patch_grad,
         weight_grad.T,
-        grads[0],
-        grads[1],
-        grads[2],
+        gains,
+        biases,
+        table,
         in_grad.reshape(experts, units, width).transpose(0, 2, 1),
-        bias_grad.reshape(experts, units),
+        bias_grad,
         out_grads.reshape(experts, units, width),
-        grads[3],
+        shift,
     )
 
 
@@ -862,9 +1009,11 @@
     mixed_out, patch_grad, weight_grad, rows, table_grad = run_backward(
         patches, out_grad, kept, produced, slot_grad, wt, vec, table
     )
+    weight_front = weight_grad[: 3 * width]
     weight_grad = weight_grad.reshape(devices, -1, width)
+    gain_grads, bias_grads = norm_sums(rows, weight_front, wt, vec)
     small_grads = jnp.concatenate(
-        [v.reshape(devices, -1) for v in (rows[:2], rows[2:6], table_grad, shift_grad)], axis=1
+        [v.reshape(devices, -1) for v in (gain_grads, bias_grads, table_grad, shift_grad)], axis=1
     )
     weight_grad = scatter_sum(weight_grad).T
     small_grads = jnp.sum(lax.all_to_all(small_grads, AXES, 0, 0, tiled=True), axis=0)

time: 165 us -> 142 us (0.86)
  local copies, waits for them, and re-layouts: 15.2 us -> 0 us
  Pallas kernels: 148 us -> 141 us
    pallas_call x1, Pallas kernels: 148 us -> 134 us  [run_layer(): pl.pallas_call(functools.partial(layer_kernel, lengths), in_specs=[anywhe...]
    unnamed x13 -> x0, local copies, waits for them, and re-layouts: 7.45 us -> none
    pallas_call x0 -> x1, Pallas kernels: none -> 7.02 us  [run_layer(): pl.pallas_call(hand_over_kernel, in_specs=[anywhere] * 5 + [here_all] * 2...]
    squeeze x3 -> x0, local copies, waits for them, and re-layouts: 3.74 us -> none  [run_layer(): grads.append(vector_grads[0, at:at + piece])]
    concatenate x1 -> x0, local copies, waits for them, and re-layouts: 2.77 us -> none  [run_layer(): jnp.concatenate(list(vectors) + [jnp.zeros((width - sum(lengths),), BF16)])]
where the time goes in v5:
time: 142 us
  Pallas kernels  141 us (99%)
    pallas_call x1, Pallas kernels, run_layer(): pl.pallas_call(functools.partial(layer_kernel, lengths), in_specs=[anywhe...  134 us
    pallas_call x1, Pallas kernels, run_layer(): pl.pallas_call(hand_over_kernel, in_specs=[anywhere] * 5 + [here_all] * 2...  7.02 us

profile of v5, /device:TPU:0, one launch (start us, length us, event | category | flops | bytes accessed | tf_op | source)
XLA Modules:
  0.0 141.9 jit_solution(911518331443749852)
XLA Ops:
  0.6 134.1 %layer.1 = (bf16[6,576,384]{2,1,0:T(8,128)(2,1)}, bf16[6,576,384]{2,1,0:T(8,128)(2,1)}, bf16[6,6,576,576]{3,2,1,0:T(8,128)(2,1)}, f32[48,384]{1,0:T(8,128)}, f32...) custom-call(bf16[6,576,384]{2,1,0:T(8,128)(2,1)} %x_hbm.1, ...), custom_call_target="tpu_custom_call" | custom-call | tf_op jit(solution)/shard_map/layer/pallas_call | solution.py:866
  134.8 7.0 %hand_over.1 = (bf16[6,576,384]{2,1,0:T(8,128)(2,1)}, bf16[6,576,384]{2,1,0:T(8,128)(2,1)}, f32[48,384]{1,0:T(8,128)}, f32[384,384]{1,0:T(8,128)}, f32[384,384]{...) custom-call(bf16[6,576,384]{2,1,0:T(8,128)(2,1)} %get-tuple-element.27.mixed, ...), custom_call_target="tpu_custom_call" | custom-call | tf_op jit(solution)/shard_map/hand_over/pallas_call | solution.py:909

commit v6 on v5

--- a/solution.py
+++ b/solution.py
@@ -51,20 +51,33 @@
     return jnp.where(low, own, other) if head % 2 == 0 else jnp.where(low, other, own)
 
 
+def projections(x, wt, vec, q_ref, k_ref, v_ref):
+    width = x.shape[1]
+    kept = []
+
+    def start():
+        normed, _ = normalize(x[...].astype(F32))
+        kept.append((normed * vec[GAIN1 : GAIN1 + 1] + vec[BIAS1 : BIAS1 + 1]).astype(BF16))
+
+    def query():
+        q_ref[...] = (dot(kept[0], wt[:width], 1, 1) * HEAD_DIM ** (-0.5)).astype(BF16)
+
+    def key():
+        k_ref[...] = dot(kept[0], wt[width : 2 * width], 1, 1).astype(BF16)
+
+    def value():
+        got = dot(kept[0], wt[2 * width : 3 * width], 1, 1)
+        v_ref[...] = (got + vec[VBIAS : VBIAS + 1]).astype(BF16)
+
+    return [start, query, key, value]
+
+
 def forward_image(
     x, g, valid_row, wt, vec, table, q_ref, k_ref, v_ref, p_ref, att_ref, inv_ref,
-    before_heads=None, after_head=None,
+    after_head=None,
 ):
     patches, width = x.shape
     heads = width // HEAD_DIM
-    images = x[...].astype(F32)
-    normed, _ = normalize(images)
-    first = (normed * vec[GAIN1 : GAIN1 + 1] + vec[BIAS1 : BIAS1 + 1]).astype(BF16)
-    q_ref[...] = (dot(first, wt[:width], 1, 1) * HEAD_DIM ** (-0.5)).astype(BF16)
-    k_ref[...] = dot(first, wt[width : 2 * width], 1, 1).astype(BF16)
-    v_ref[...] = (dot(first, wt[2 * width : 3 * width], 1, 1) + vec[VBIAS : VBIAS + 1]).astype(BF16)
-    if before_heads is not None:
-        before_heads()
     bias_row = jnp.where(valid_row > 0, 0.0, MASKED).astype(F32)
     fill = jnp.broadcast_to(bias_row * (1.0 / HEAD_DIM), (PAIR, patches)).T.astype(BF16)
     low = lower_half((patches, PAIR))
@@ -101,7 +114,7 @@
             inv_ref[:, at : at + PAIR] = inverse.astype(inv_ref.dtype)
             att_ref[:, at : at + PAIR] = (jnp.where(low, even, odd) * inverse).astype(BF16)
     branch = dot(att_ref[...], wt[3 * width :], 1, 1)
-    middle = images + branch + vec[OBIAS : OBIAS + 1]
+    middle = x[...].astype(F32) + branch + vec[OBIAS : OBIAS + 1]
     normed, _ = normalize(middle)
     second = (normed * vec[GAIN2 : GAIN2 + 1] + vec[BIAS2 : BIAS2 + 1]).astype(BF16)
     logits = dot(table, second, 1, 1)
@@ -119,7 +132,7 @@
     x, g, middle_ref, dispatch, combine, produced, slot_grad, wt, vec, table,
     q_ref, k_ref, v_ref, p_ref, att_ref, inv_ref, ds_ref, grad_t_ref, dq_ref, dk_ref, dv_ref,
     mixed_ref, grad_ref,
-    before_heads=None, before_head=None, after_heads=None,
+    before_heads=None, after_heads=None,
 ):
     patches, width = x.shape
     heads = width // HEAD_DIM
@@ -183,8 +196,6 @@
     for head in range(heads):
         if head + 1 < heads:
             prob_grad(head + 1)
-        if before_head is not None:
-            before_head(head)
         rows = slice(head * HEAD_DIM, (head + 1) * HEAD_DIM)
         prob = p_ref[head]
         grad_t_ref[width + rows.start : width + rows.stop, :] = dot(
@@ -243,6 +254,8 @@
     x, g, valid, wt, vec, table,
     q, k, v, p, att, inv, middle, dispatch, combine, slots, produced_grad,
 ):
+    for step in projections(x.at[0], wt, vec[...], q.at[0], k.at[0], v.at[0]):
+        step()
     got = forward_image(
         x.at[0], g.at[0], valid[0], wt, vec[...], table[...],
         q.at[0], k.at[0], v.at[0], p.at[0], att.at[0], inv.at[0],
@@ -391,26 +404,25 @@
     def __init__(self, every, send, recv):
         self.every, self.send, self.recv = every, send, recv
         self.w, self.z = here()
+        self.core, self.chip = lax.rem(self.w, 2), self.w // 2
 
     def z_copies(self):
-        own = self.every.at[self.w, self.z]
+        own = self.every.at[self.core, self.chip, self.z]
         return [
             remote(own, own, self.send.at[n], self.recv.at[n], peer)
             for n, peer in enumerate(along_z(self.w, self.z))
         ]
 
     def plane_copies(self):
-        own = self.every.at[self.w]
+        own = self.every.at[self.core, self.chip]
         return [
             remote(own, own, self.send.at[3 + n], self.recv.at[3 + n], peer)
             for n, peer in enumerate(in_plane(self.w, self.z))
         ]
 
-    def core_copy(self, n, group):
-        own = self.every.at[group]
-        return remote(
-            own, own, self.send.at[6 + n], self.recv.at[6 + n], other_core(self.w, self.z)
-        )
+    def core_copy(self):
+        own = self.every.at[self.core]
+        return remote(own, own, self.send.at[6], self.recv.at[6], other_core(self.w, self.z))
 
     def start_z(self):
         for copy in self.z_copies():
@@ -421,32 +433,85 @@
             copy.wait()
         for copy in self.plane_copies():
             copy.start()
-        self.core_copy(0, self.w).start()
 
     def start_core(self):
-        peers = in_plane(self.w, self.z)
-        for n, (copy, peer) in enumerate(zip(self.plane_copies(), peers)):
+        for copy in self.plane_copies():
             copy.wait()
-            self.core_copy(n + 1, peer[0]).start()
+        self.core_copy().start()
 
     def finish(self):
-        for n in range(4):
-            self.core_copy(n, self.w).wait()
+        self.core_copy().wait()
+
+
+class FineGather:
+    def __init__(self, every, z_send, z_recv, p_send, p_recv, c_send, c_recv):
+        self.every = every
+        self.z_sems, self.p_sems, self.c_sems = (z_send, z_recv), (p_send, p_recv), (c_send, c_recv)
+        self.w, self.z = here()
+        self.plane = in_plane(self.w, self.z)
+
+    def block(self, w, k):
+        return self.every.at[lax.rem(w, 2), w // 2, lax.rem(self.z + 4 - k, 4)]
+
+    def z_copy(self, n):
+        own = self.block(self.w, 0)
+        peer = along_z(self.w, self.z)[n]
+        return remote(own, own, self.z_sems[0].at[n], self.z_sems[1].at[n], peer)
+
+    def plane_copy(self, n, k):
+        own = self.block(self.w, k)
+        return remote(own, own, self.p_sems[0].at[n, k], self.p_sems[1].at[n, k], self.plane[n])
+
+    def core_copy(self, group, k):
+        own = self.block(self.w if group == 0 else self.plane[group - 1][0], k)
+        return remote(
+            own, own, self.c_sems[0].at[group, k], self.c_sems[1].at[group, k],
+            other_core(self.w, self.z),
+        )
+
+    def pass_on(self, k):
+        for n in range(3):
+            self.plane_copy(n, k).start()
+        self.core_copy(0, k).start()
+
+    def start(self):
+        for n in range(3):
+            self.z_copy(n).start()
+        self.pass_on(0)
+
+    def start_plane(self):
+        for n in range(3):
+            self.z_copy(n).wait()
+            self.pass_on(n + 1)
+
+    def start_core(self):
+        for k in range(4):
+            for n in range(3):
+                self.plane_copy(n, k).wait()
+                self.core_copy(n + 1, k).start()
+
+    def finish(self):
+        for group in range(4):
+            for k in range(4):
+                self.core_copy(group, k).wait()
 
 
 class Scatter:
-    def __init__(self, parts, from_core, chips, from_plane, column, from_z, send, recv):
+    def __init__(
+        self, parts, from_core, chips, from_plane, column, from_z, send, recv, by_chip=False
+    ):
         self.parts, self.from_core, self.chips = parts, from_core, chips
         self.from_plane, self.column, self.from_z = from_plane, column, from_z
-        self.send, self.recv = send, recv
+        self.send, self.recv, self.by_chip = send, recv, by_chip
         self.w, self.z = here()
         self.core = lax.rem(self.w, 2)
 
-    def core_copy(self, chip):
-        return remote(
-            self.parts.at[2 * chip + 1 - self.core], self.from_core.at[chip],
-            self.send.at[chip], self.recv.at[chip], other_core(self.w, self.z),
-        )
+    def core_copy(self, chip=None):
+        src, dst = self.parts.at[1 - self.core], self.from_core
+        if chip is not None:
+            src, dst = src.at[chip], dst.at[chip]
+        at = 0 if chip is None else chip
+        return remote(src, dst, self.send.at[at], self.recv.at[at], other_core(self.w, self.z))
 
     def chip_order(self):
         return [there // 2 for there, _ in in_plane(self.w, self.z)] + [self.w // 2]
@@ -470,14 +535,23 @@
         ]
 
     def start_core(self):
+        if not self.by_chip:
+            self.core_copy().start()
+            return
         for chip in self.chip_order():
             self.core_copy(chip).start()
 
     def start_plane(self):
-        onward = self.plane_copies() + [None]
-        for chip, copy in zip(self.chip_order(), onward):
+        if not self.by_chip:
+            self.core_copy().wait()
+            total = self.parts[self.core].astype(F32) + self.from_core[...].astype(F32)
+            self.chips[...] = total.astype(BF16)
+            for copy in self.plane_copies():
+                copy.start()
+            return
+        for chip, copy in zip(self.chip_order(), self.plane_copies() + [None]):
             self.core_copy(chip).wait()
-            own = self.parts[2 * chip + self.core].astype(F32)
+            own = self.parts[self.core, chip].astype(F32)
             self.chips[chip] = (own + self.from_core[chip].astype(F32)).astype(BF16)
             if copy is not None:
                 copy.start()
@@ -495,84 +569,41 @@
     def finish(self):
         for copy in self.z_copies():
             copy.wait()
+
+    def total(self):
         total = self.column[self.z].astype(F32)
         for n in range(3):
             total = total + self.from_z[n].astype(F32)
         return total
 
 
-class FineGather:
-    def __init__(self, every, z_send, z_recv, p_send, p_recv, c_send, c_recv):
-        self.every = every
-        self.z_sems, self.p_sems, self.c_sems = (z_send, z_recv), (p_send, p_recv), (c_send, c_recv)
-        self.w, self.z = here()
-        self.plane = in_plane(self.w, self.z)
-
-    def block(self, w, k):
-        return self.every.at[w, lax.rem(self.z + 4 - k, 4)]
-
-    def z_copy(self, n):
-        own = self.block(self.w, 0)
-        peer = along_z(self.w, self.z)[n]
-        return remote(own, own, self.z_sems[0].at[n], self.z_sems[1].at[n], peer)
-
-    def plane_copy(self, n, k):
-        own = self.block(self.w, k)
-        return remote(own, own, self.p_sems[0].at[n, k], self.p_sems[1].at[n, k], self.plane[n])
-
-    def core_copy(self, group, k):
-        own = self.block(self.w if group == 0 else self.plane[group - 1][0], k)
-        return remote(
-            own, own, self.c_sems[0].at[group, k], self.c_sems[1].at[group, k],
-            other_core(self.w, self.z),
-        )
-
-    def pass_on(self, k):
-        for n in range(3):
-            self.plane_copy(n, k).start()
-        self.core_copy(0, k).start()
-
-    def start(self):
-        for n in range(3):
-            self.z_copy(n).start()
-        self.pass_on(0)
-
-    def start_plane(self):
-        for n in range(3):
-            self.z_copy(n).wait()
-            self.pass_on(n + 1)
-
-    def start_core(self):
-        for k in range(4):
-            for n in range(3):
-                self.plane_copy(n, k).wait()
-                self.core_copy(n + 1, k).start()
-
-    def finish(self):
-        for group in range(4):
-            for k in range(4):
-                self.core_copy(group, k).wait()
+def by_device(blocks):
+    return jnp.concatenate([blocks[core, chip] for chip in range(4) for core in range(2)], axis=0)
+
+
+def fill_blocks(blocks, values):
+    for chip in range(4):
+        for core in range(2):
+            at = (2 * chip + core) * 4
+            blocks[core, chip] = values[at : at + 4].astype(blocks.dtype)
+
+
+def gather_scratch(rows, width):
+    dma = pltpu.SemaphoreType.DMA
+    return [pltpu.VMEM((2, 4, 4, rows, width), BF16), dma((7,)), dma((7,))]
 
 
 def fine_scratch(rows, width):
     dma = pltpu.SemaphoreType.DMA
     return [
-        pltpu.VMEM((8, 4, rows, width), BF16),
+        pltpu.VMEM((2, 4, 4, rows, width), BF16),
         dma((3,)), dma((3,)), dma((3, 4)), dma((3, 4)), dma((4, 4)), dma((4, 4)),
     ]
 
 
-def gather_scratch(rows, width):
-    return [
-        pltpu.VMEM((8, 4, rows, width), BF16),
-        pltpu.SemaphoreType.DMA((10,)),
-        pltpu.SemaphoreType.DMA((10,)),
-    ]
-
-
 def scatter_scratch(rows, width):
     return [
-        pltpu.VMEM((8, 4, rows, width), BF16),
+        pltpu.VMEM((2, 4, 4, rows, width), BF16),
         pltpu.VMEM((4, 4, rows, width), BF16),
         pltpu.VMEM((4, 4, rows, width), BF16),
         pltpu.VMEM((3, 4, rows, width), BF16),
@@ -581,6 +612,7 @@
         pltpu.SemaphoreType.DMA((10,)),
         pltpu.SemaphoreType.DMA((10,)),
     ]
+
 
 def expert_rows(slots, grads, w_in, bias, w_out):
     rows, width = slots.shape
@@ -648,17 +680,18 @@
     heads = width // HEAD_DIM
     rows = own_weights.shape[0]
     wide, narrow = here()
+    me = (lax.rem(wide, 2), wide // 2, narrow)
     (w_every, *w_sems), (v_every, *v_sems) = rest[:7], rest[7:10]
     w_last, v_last = rest[10:18], rest[18:26]
 
     for i in range(count):
         pltpu.make_async_copy(x_hbm.at[i], x.at[i], x_sem.at[i]).start()
         pltpu.make_async_copy(g_hbm.at[i], g.at[i], g_sem.at[i]).start()
-    w_every[wide, narrow] = own_weights[...]
+    w_every[me] = own_weights[...]
     own_pieces[...] = jnp.zeros_like(own_pieces)
     for n, ref in enumerate((own_gains, own_biases, own_table, own_shift)):
         own_pieces[n : n + 1, : lengths[n]] = ref[...].astype(F32).reshape(1, lengths[n])
-    v_every[wide, narrow] = own_pieces[...].astype(BF16)
+    v_every[me] = own_pieces[...].astype(BF16)
     greet()
     weights = FineGather(w_every, *w_sems)
     vectors = Gather(v_every, *v_sems)
@@ -676,7 +709,7 @@
     vectors.start_core()
     weights.start_core()
     vectors.finish()
-    packed = v_every[...].astype(F32).reshape(32, 16, 128)
+    packed = by_device(v_every).astype(F32)
     gains, biases, slot_rows, shift_rows = (
         spread(packed[:, n], length, width) for n, length in enumerate(lengths)
     )
@@ -684,16 +717,16 @@
     table[...] = slot_rows
     shift[...] = shift_rows
     weights.finish()
-    wt[...] = w_every[...].reshape(4 * width, width)
+    wt[...] = by_device(w_every).reshape(4 * width, width)
 
     def slots_way(i):
         return Gather(every.at[i], g_send.at[i], g_recv.at[i])
 
     def results_way(i):
-        ring = lax.rem(i, 3)
+        ring = lax.rem(i, 2)
         return Scatter(
-            parts.at[ring], from_core.at[ring], chips.at[ring], from_plane.at[ring],
-            column.at[i], from_z.at[i], s_send.at[i], s_recv.at[i],
+            parts.at[ring], from_core.at[ring], chips.at[ring], from_plane.at[i], column.at[i],
+            from_z.at[i], s_send.at[i], s_recv.at[i],
         )
 
     def for_image(i, action):
@@ -710,7 +743,7 @@
             w_in[...], bias[...], w_out[...],
         )
         back = jnp.stack([got[0].reshape(32, 8, width), got[1].reshape(32, 8, width)], axis=1)
-        parts[lax.rem(i, 3)] = back.reshape(8, 4, 16, width).astype(BF16)
+        parts[lax.rem(i, 2)] = back.reshape(2, 4, 4, 16, width).astype(BF16)
         in_grad[...] += got[2]
         out_grad[...] += got[3]
         bias_grad[...] += got[4]
@@ -731,26 +764,28 @@
     def p_in(i, head):
         return pltpu.make_async_copy(p_hbm.at[i, head], p.at[head], p_in_sem.at[head])
 
+    def arrive(hbm, ref, sem, i):
+        pltpu.make_async_copy(hbm.at[i], ref.at[i], sem.at[i]).wait()
+
     def forward(i, carry):
-        pltpu.make_async_copy(x_hbm.at[i], x.at[i], x_sem.at[i]).wait()
-        pltpu.make_async_copy(g_hbm.at[i], g.at[i], g_sem.at[i]).wait()
-
-        def before_heads():
-            middle_of(i)
-
-            @pl.when(i > 0)
-            def _():
-                for head in range(heads):
-                    p_out(i - 1, head).wait()
+        arrive(x_hbm, x, x_sem, i)
+        for step in projections(x.at[i], wt, vec[...], q.at[i], k.at[i], v.at[i]):
+            step()
+        arrive(g_hbm, g, g_sem, i)
+        middle_of(i)
+
+        @pl.when(i > 0)
+        def _():
+            for head in range(heads):
+                p_out(i - 1, head).wait()
 
         got = forward_image(
             x.at[i], g.at[i], valid[pl.ds(i, 1)], wt, vec[...], table[...].astype(BF16),
-            q.at[i], k.at[i], v.at[i], p, att.at[i], inv.at[i],
-            before_heads, lambda head: p_out(i, head).start(),
+            q.at[i], k.at[i], v.at[i], p, att.at[i], inv.at[i], lambda head: p_out(i, head).start(),
         )
         middle[i], dispatch[i], combine[i] = got[:3]
         shift_grad[...] += got[4].astype(BF16).astype(F32)
-        every[i, wide, narrow] = jnp.concatenate([got[3], got[4]], axis=0).astype(BF16)
+        every[(i,) + me] = jnp.concatenate([got[3], got[4]], axis=0).astype(BF16)
         end_of(i)
         slots_way(i).start_z()
         return carry
@@ -761,20 +796,26 @@
         p_in(0, head).start()
 
     def backward(i, carry):
+        def before_heads():
+            middle_of(count + i)
+            for head in range(heads):
+                p_in(i, head).wait()
+
         def after_heads():
             @pl.when(i + 1 < count)
             def _():
                 for head in range(heads):
                     p_in(i + 1, head).start()
 
-        total = results_way(i).finish()
+        results_way(i).finish()
+        total = results_way(i).total()
         got = backward_image(
             x.at[i], g.at[i], middle.at[i], dispatch[i], combine[i],
             (total[:8] + shift[...]).astype(BF16), total[8:].astype(BF16),
             wt, vec[...], table[...].astype(BF16),
             q.at[i], k.at[i], v.at[i], p, att.at[i], inv.at[i], ds, grad_t,
             q.at[i], k.at[i], v.at[i], g.at[i], middle.at[i],
-            lambda: middle_of(count + i), lambda head: p_in(i, head).wait(), after_heads,
+            before_heads, after_heads,
         )
         pltpu.make_async_copy(g.at[i], mixed_hbm.at[i], mixed_sem.at[i]).start()
         add_grads(weight_grad, sums, table_grad, got)
@@ -783,8 +824,8 @@
 
     lax.fori_loop(0, count, backward, 0)
 
-    w_last[0][...] = weight_grad[...].reshape(8, 4, rows, width).astype(BF16)
-    weights = Scatter(*w_last)
+    fill_blocks(w_last[0], weight_grad[...].reshape(32, rows, width))
+    weights = Scatter(*w_last, by_chip=True)
     weights.start_core()
     gains, biases = norm_sums(sums[...], weight_grad[: 3 * width, :], wt, vec[...])
     pieces = [
@@ -793,7 +834,7 @@
     ]
     pieces.append(jnp.zeros((32, 128), F32))
     pieces = jnp.stack([pieces[min(n, 4)] for n in range(16)], axis=1)
-    v_last[0][...] = pieces.reshape(8, 4, 16, 128).astype(BF16)
+    fill_blocks(v_last[0], pieces)
     vectors = Scatter(*v_last)
     vectors.start_core()
     weights.start_plane()
@@ -811,8 +852,10 @@
         return carry
 
     lax.fori_loop(0, count, finish, 0)
-    weight_out[...] = weights.finish()
-    vectors_out[...] = vectors.finish()
+    weights.finish()
+    weight_out[...] = weights.total()
+    vectors.finish()
+    vectors_out[...] = vectors.total()
     for i in range(count):
         pltpu.make_async_copy(g.at[i], mixed_hbm.at[i], mixed_sem.at[i]).wait()
         pltpu.make_async_copy(x.at[i], patch_grad_hbm.at[i], patch_sem.at[i]).wait()
@@ -888,10 +931,10 @@
             vmem((experts, width), F32), vmem((16, 128), F32),
             dma((count,)), dma((count,)), dma((heads,)), dma((heads,)), dma((count,)), dma((count,)),
         ]
-        + [vmem((count, 8, 4, 16, width), BF16), dma((count, 10)), dma((count, 10))]
+        + [vmem((count, 2, 4, 4, 16, width), BF16), dma((count, 7)), dma((count, 7))]
         + [
-            vmem((3, 8, 4, 16, width), BF16), vmem((3, 4, 4, 16, width), BF16),
-            vmem((3, 4, 4, 16, width), BF16), vmem((3, 3, 4, 16, width), BF16),
+            vmem((2, 2, 4, 4, 16, width), BF16), vmem((2, 4, 4, 16, width), BF16),
+            vmem((2, 4, 4, 16, width), BF16), vmem((count, 3, 4, 16, width), BF16),
             vmem((count, 4, 16, width), BF16), vmem((count, 3, 16, width), BF16),
             dma((count, 10)), dma((count, 10)),
         ]

time: 142 us -> 133 us (0.937)
  Pallas kernels: 141 us -> 132 us
    pallas_call x1, Pallas kernels: 134 us -> 125 us  [run_layer(): pl.pallas_call(functools.partial(layer_kernel, lengths), in_specs=[anywhe...]
where the time goes in v6:
time: 133 us
  Pallas kernels  132 us (99%)
    pallas_call x1, Pallas kernels, run_layer(): pl.pallas_call(functools.partial(layer_kernel, lengths), in_specs=[anywhe...  125 us
    pallas_call x1, Pallas kernels, run_layer(): pl.pallas_call(hand_over_kernel, in_specs=[anywhere] * 5 + [here_all] * 2...  7.02 us

profile of v6, /device:TPU:0, one launch (start us, length us, event | category | flops | bytes accessed | tf_op | source)
XLA Modules:
  0.0 132.6 jit_solution(16290916150358388035)
XLA Ops:
  0.6 124.8 %layer.1 = (bf16[6,576,384]{2,1,0:T(8,128)(2,1)}, bf16[6,576,384]{2,1,0:T(8,128)(2,1)}, bf16[6,6,576,576]{3,2,1,0:T(8,128)(2,1)}, f32[48,384]{1,0:T(8,128)}, f32...) custom-call(bf16[6,576,384]{2,1,0:T(8,128)(2,1)} %x_hbm.1, ...), custom_call_target="tpu_custom_call" | custom-call | tf_op jit(solution)/shard_map/layer/pallas_call | solution.py:909
  125.4 7.0 %hand_over.1 = (bf16[6,576,384]{2,1,0:T(8,128)(2,1)}, bf16[6,576,384]{2,1,0:T(8,128)(2,1)}, f32[48,384]{1,0:T(8,128)}, f32[384,384]{1,0:T(8,128)}, f32[384,384]{...) custom-call(bf16[6,576,384]{2,1,0:T(8,128)(2,1)} %get-tuple-element.27.mixed, ...), custom_call_target="tpu_custom_call" | custom-call | tf_op jit(solution)/shard_map/hand_over/pallas_call | solution.py:952

commit v7 on v6

--- a/solution.py
+++ b/solution.py
@@ -15,7 +15,7 @@
 F32 = jnp.float32
 MESH = pl.DeviceIdType.MESH
 VMEM_LIMIT = 60 * 1024 * 1024
-LAYER_LIMIT = 63 * 1024 * 1024
+LAYER_LIMIT = 56 * 1024 * 1024
 GAIN1, GAIN2, BIAS1, VBIAS, OBIAS, BIAS2 = range(6)
 
 
@@ -51,25 +51,13 @@
     return jnp.where(low, own, other) if head % 2 == 0 else jnp.where(low, other, own)
 
 
-def projections(x, wt, vec, q_ref, k_ref, v_ref):
-    width = x.shape[1]
-    kept = []
-
-    def start():
-        normed, _ = normalize(x[...].astype(F32))
-        kept.append((normed * vec[GAIN1 : GAIN1 + 1] + vec[BIAS1 : BIAS1 + 1]).astype(BF16))
-
-    def query():
-        q_ref[...] = (dot(kept[0], wt[:width], 1, 1) * HEAD_DIM ** (-0.5)).astype(BF16)
-
-    def key():
-        k_ref[...] = dot(kept[0], wt[width : 2 * width], 1, 1).astype(BF16)
-
-    def value():
-        got = dot(kept[0], wt[2 * width : 3 * width], 1, 1)
-        v_ref[...] = (got + vec[VBIAS : VBIAS + 1]).astype(BF16)
-
-    return [start, query, key, value]
+def projections(normed, wt, vec, q_ref, k_ref, v_ref):
+    width = wt.shape[1]
+    first = (normed[...] * vec[GAIN1 : GAIN1 + 1] + vec[BIAS1 : BIAS1 + 1]).astype(BF16)
+    got = dot(first, wt[: 3 * width], 1, 1)
+    q_ref[...] = (got[:, :width] * HEAD_DIM ** (-0.5)).astype(BF16)
+    k_ref[...] = got[:, width : 2 * width].astype(BF16)
+    v_ref[...] = (got[:, 2 * width :] + vec[VBIAS : VBIAS + 1]).astype(BF16)
 
 
 def forward_image(
@@ -130,19 +118,16 @@
 
 def backward_image(
     x, g, middle_ref, dispatch, combine, produced, slot_grad, wt, vec, table,
-    q_ref, k_ref, v_ref, p_ref, att_ref, inv_ref, ds_ref, grad_t_ref, dq_ref, dk_ref, dv_ref,
-    mixed_ref, grad_ref,
+    q_ref, k_ref, v_ref, p_ref, att_ref, inv_ref, ds_ref, grad_t_ref, dq_ref, dk_ref, dv_ref, grad_ref,
     before_heads=None, after_heads=None,
 ):
     patches, width = x.shape
     heads = width // HEAD_DIM
-    combine_low = combine.astype(BF16)
     dispatch_low = dispatch.astype(BF16)
     middle = middle_ref[...]
     normed, factor = normalize(middle)
     second = (normed * vec[GAIN2 : GAIN2 + 1] + vec[BIAS2 : BIAS2 + 1]).astype(BF16)
     upstream = g[...]
-    mixed = (middle + dot(combine_low, produced, 0, 0)).astype(BF16)
     combine_grad = dot(produced, upstream, 1, 1)
     dispatch_grad = dot(slot_grad, second, 1, 1)
     logit_grad = dispatch * (
@@ -161,7 +146,6 @@
     middle_grad = upstream.astype(F32) + norm_back(
         second_grad * vec[GAIN2 : GAIN2 + 1], normed, factor
     )
-    mixed_ref[...] = mixed
     grad_ref[...] = middle_grad
     branch_grad = middle_grad.astype(BF16)
     branch_shift = jnp.sum(branch_grad.astype(F32), axis=0, keepdims=True)
@@ -227,13 +211,14 @@
     return query_front, other_front, output_grad, sums, table_grad
 
 
-def finish_image(x, middle_grad, wt, vec, dq_ref, dk_ref, dv_ref):
+def finish_image(x, middle, middle_grad, combine, produced, wt, vec, dq_ref, dk_ref, dv_ref):
     width = x.shape[1]
+    mixed = middle[...] + dot(combine.astype(BF16), produced, 0, 0)
     normed, factor = normalize(x[...].astype(F32))
     project_grad = jnp.concatenate([dq_ref[...], dk_ref[...], dv_ref[...]], axis=1)
     first_grad = dot(project_grad, wt[: 3 * width], 1, 0)
     grad = middle_grad[...] + norm_back(first_grad * vec[GAIN1 : GAIN1 + 1], normed, factor)
-    return grad.astype(BF16)
+    return mixed.astype(BF16), grad.astype(BF16)
 
 
 def norm_sums(sums, weight_grad, wt, vec):
@@ -254,8 +239,8 @@
     x, g, valid, wt, vec, table,
     q, k, v, p, att, inv, middle, dispatch, combine, slots, produced_grad,
 ):
-    for step in projections(x.at[0], wt, vec[...], q.at[0], k.at[0], v.at[0]):
-        step()
+    middle[0] = normalize(x[0].astype(F32))[0]
+    projections(middle.at[0], wt, vec[...], q.at[0], k.at[0], v.at[0])
     got = forward_image(
         x.at[0], g.at[0], valid[0], wt, vec[...], table[...],
         q.at[0], k.at[0], v.at[0], p.at[0], att.at[0], inv.at[0],
@@ -289,9 +274,11 @@
         x.at[0], g.at[0], middle.at[0], dispatch[0], combine[0], produced[0], slot_grad[0],
         wt, vec[...], table[...],
         q.at[0], k.at[0], v.at[0], p.at[0], att.at[0], inv.at[0], ds, grad_t, dq, dk, dv,
-        mixed.at[0], middle_grad,
-    )
-    patch_grad[0] = finish_image(x.at[0], middle_grad, wt, vec[...], dq, dk, dv)
+        middle_grad,
+    )
+    mixed[0], patch_grad[0] = finish_image(
+        x.at[0], middle.at[0], middle_grad, combine[0], produced[0], wt, vec[...], dq, dk, dv
+    )
     add_grads(weight_grad, sums, table_grad, got)
 
 
@@ -497,30 +484,24 @@
 
 
 class Scatter:
-    def __init__(
-        self, parts, from_core, chips, from_plane, column, from_z, send, recv, by_chip=False
-    ):
+    def __init__(self, parts, from_core, chips, from_plane, column, from_z, send, recv):
         self.parts, self.from_core, self.chips = parts, from_core, chips
         self.from_plane, self.column, self.from_z = from_plane, column, from_z
-        self.send, self.recv, self.by_chip = send, recv, by_chip
+        self.send, self.recv = send, recv
         self.w, self.z = here()
         self.core = lax.rem(self.w, 2)
 
-    def core_copy(self, chip=None):
-        src, dst = self.parts.at[1 - self.core], self.from_core
-        if chip is not None:
-            src, dst = src.at[chip], dst.at[chip]
-        at = 0 if chip is None else chip
-        return remote(src, dst, self.send.at[at], self.recv.at[at], other_core(self.w, self.z))
-
-    def chip_order(self):
-        return [there // 2 for there, _ in in_plane(self.w, self.z)] + [self.w // 2]
+    def core_copy(self):
+        return remote(
+            self.parts.at[1 - self.core], self.from_core, self.send.at[0], self.recv.at[0],
+            other_core(self.w, self.z),
+        )
 
     def plane_copies(self):
         return [
             remote(
                 self.chips.at[peer[0] // 2], self.from_plane.at[n],
-                self.send.at[4 + n], self.recv.at[4 + n], peer,
+                self.send.at[1 + n], self.recv.at[1 + n], peer,
             )
             for n, peer in enumerate(in_plane(self.w, self.z))
         ]
@@ -529,32 +510,20 @@
         return [
             remote(
                 self.column.at[peer[1]], self.from_z.at[n],
-                self.send.at[7 + n], self.recv.at[7 + n], peer,
+                self.send.at[4 + n], self.recv.at[4 + n], peer,
             )
             for n, peer in enumerate(along_z(self.w, self.z))
         ]
 
     def start_core(self):
-        if not self.by_chip:
-            self.core_copy().start()
-            return
-        for chip in self.chip_order():
-            self.core_copy(chip).start()
+        self.core_copy().start()
 
     def start_plane(self):
-        if not self.by_chip:
-            self.core_copy().wait()
-            total = self.parts[self.core].astype(F32) + self.from_core[...].astype(F32)
-            self.chips[...] = total.astype(BF16)
-            for copy in self.plane_copies():
-                copy.start()
-            return
-        for chip, copy in zip(self.chip_order(), self.plane_copies() + [None]):
-            self.core_copy(chip).wait()
-            own = self.parts[self.core, chip].astype(F32)
-            self.chips[chip] = (own + self.from_core[chip].astype(F32)).astype(BF16)
-            if copy is not None:
-                copy.start()
+        self.core_copy().wait()
+        total = self.parts[self.core].astype(F32) + self.from_core[...].astype(F32)
+        self.chips[...] = total.astype(BF16)
+        for copy in self.plane_copies():
+            copy.start()
 
     def start_z(self):
         for copy in self.plane_copies():
@@ -577,6 +546,73 @@
         return total
 
 
+class FineScatter:
+    def __init__(
+        self, parts, from_core, chips, from_plane, column, from_z,
+        c_send, c_recv, p_send, p_recv, z_send, z_recv,
+    ):
+        self.parts, self.from_core, self.chips = parts, from_core, chips
+        self.from_plane, self.column, self.from_z = from_plane, column, from_z
+        self.c_sems, self.p_sems, self.z_sems = (c_send, c_recv), (p_send, p_recv), (z_send, z_recv)
+        self.w, self.z = here()
+        self.core = lax.rem(self.w, 2)
+        self.plane = in_plane(self.w, self.z)
+
+    def goal(self, k):
+        return lax.rem(self.z + k, 4)
+
+    def core_copy(self, chip):
+        return remote(
+            self.parts.at[1 - self.core, chip], self.from_core.at[chip],
+            self.c_sems[0].at[chip], self.c_sems[1].at[chip], other_core(self.w, self.z),
+        )
+
+    def plane_copy(self, n, k):
+        z = self.goal(k)
+        return remote(
+            self.chips.at[self.plane[n][0] // 2, z], self.from_plane.at[n, z],
+            self.p_sems[0].at[n, k], self.p_sems[1].at[n, k], self.plane[n],
+        )
+
+    def z_copy(self, k):
+        return remote(
+            self.column.at[self.goal(k)], self.from_z.at[k - 1],
+            self.z_sems[0].at[k - 1], self.z_sems[1].at[k - 1], (self.w, self.goal(k)),
+        )
+
+    def start_core(self):
+        for chip in [there // 2 for there, _ in self.plane] + [self.w // 2]:
+            self.core_copy(chip).start()
+
+    def start_plane(self):
+        for n, chip in enumerate([there // 2 for there, _ in self.plane] + [self.w // 2]):
+            self.core_copy(chip).wait()
+            own = self.parts[self.core, chip].astype(F32)
+            self.chips[chip] = (own + self.from_core[chip].astype(F32)).astype(BF16)
+        for k in (1, 2, 3, 0):
+            for n in range(3):
+                self.plane_copy(n, k).start()
+
+    def plane_sum(self, k):
+        z = self.goal(k)
+        total = self.chips[self.w // 2, z].astype(F32)
+        for n in range(3):
+            self.plane_copy(n, k).wait()
+            total = total + self.from_plane[n, z].astype(F32)
+        return total
+
+    def start_z(self, k):
+        self.column[self.goal(k)] = self.plane_sum(k).astype(BF16)
+        self.z_copy(k).start()
+
+    def total(self):
+        total = self.plane_sum(0)
+        for k in (1, 2, 3):
+            self.z_copy(k).wait()
+            total = total + self.from_z[k - 1].astype(F32)
+        return total
+
+
 def by_device(blocks):
     return jnp.concatenate([blocks[core, chip] for chip in range(4) for core in range(2)], axis=0)
 
@@ -609,8 +645,8 @@
         pltpu.VMEM((3, 4, rows, width), BF16),
         pltpu.VMEM((4, rows, width), BF16),
         pltpu.VMEM((3, rows, width), BF16),
-        pltpu.SemaphoreType.DMA((10,)),
-        pltpu.SemaphoreType.DMA((10,)),
+        pltpu.SemaphoreType.DMA((7,)),
+        pltpu.SemaphoreType.DMA((7,)),
     ]
 
 
@@ -630,10 +666,7 @@
     hidden_grad = jnp.where(keep, active_grad * slope, 0.0).astype(BF16)
     produced = dot(active, w_out, 1, 0)
     slot_grad = dot(hidden_grad, w_in, 1, 0)
-    in_grad = dot(hidden_grad, slots, 0, 0)
-    out_grad = dot(active, grads, 0, 0)
-    bias_grad = jnp.sum(hidden_grad.astype(F32).reshape(-1, 8, units), axis=0)
-    return produced, slot_grad, in_grad, out_grad, bias_grad
+    return produced, slot_grad, active, hidden_grad
 
 
 def one_hot(length, width):
@@ -668,10 +701,11 @@
 def layer_kernel(
     lengths,
     x_hbm, g_hbm, valid, own_weights, own_gains, own_biases, own_table, own_shift, w_in, own_bias, w_out,
-    mixed_hbm, patch_grad_hbm, p_hbm, weight_out, vectors_out, in_grad, out_grad, bias_grad,
-    x, g, q, k, v, att, inv, middle, dispatch, combine, p, ds, grad_t, wt, vec, table, shift, bias,
+    g, x, p_hbm, weight_out, vectors_out, in_grad, out_grad, bias_grad,
+    q, k, v, att, inv, middle, dispatch, combine, p, ds, grad_t, wt, vec, table, shift, bias,
     weight_grad, sums, table_grad, shift_grad, own_pieces,
-    x_sem, g_sem, p_out_sem, p_in_sem, mixed_sem, patch_sem,
+    middle_grad, produced, active, hidden_grad,
+    x_sem, g_sem, p_out_sem, p_in_sem,
     every, g_send, g_recv,
     parts, from_core, chips, from_plane, column, from_z, s_send, s_recv,
     *rest,
@@ -682,7 +716,7 @@
     wide, narrow = here()
     me = (lax.rem(wide, 2), wide // 2, narrow)
     (w_every, *w_sems), (v_every, *v_sems) = rest[:7], rest[7:10]
-    w_last, v_last = rest[10:18], rest[18:26]
+    w_last, v_last = rest[10:22], rest[22:30]
 
     for i in range(count):
         pltpu.make_async_copy(x_hbm.at[i], x.at[i], x_sem.at[i]).start()
@@ -704,6 +738,15 @@
     at = lax.broadcasted_iota(jnp.int32, spread_bias.shape, 0)
     lane = lax.broadcasted_iota(jnp.int32, spread_bias.shape, 1)
     bias[...] = jnp.sum(jnp.where(lane // units == at, spread_bias, 0.0), axis=0, keepdims=True)
+    def arrive(hbm, ref, sem, i):
+        pltpu.make_async_copy(hbm.at[i], ref.at[i], sem.at[i]).wait()
+
+    def first_norm(i, carry):
+        arrive(x_hbm, x, x_sem, i)
+        middle[i] = normalize(x[i].astype(F32))[0]
+        return carry
+
+    lax.fori_loop(0, count, first_norm, 0)
     vectors.start_plane()
     weights.start_plane()
     vectors.start_core()
@@ -734,19 +777,16 @@
         def _():
             action(i)
 
+    def arrived_rows(i):
+        both = every[i].astype(F32).reshape(32, 2, 8, width)
+        return [both[:, n].reshape(32 * 8, width).astype(BF16) for n in range(2)]
+
     def experts(i):
         slots_way(i).finish()
-        both = every[i].astype(F32).reshape(32, 2, 8, width)
-        got = expert_rows(
-            both[:, 0].reshape(32 * 8, width).astype(BF16),
-            both[:, 1].reshape(32 * 8, width).astype(BF16),
-            w_in[...], bias[...], w_out[...],
-        )
+        got = expert_rows(*arrived_rows(i), w_in[...], bias[...], w_out[...])
         back = jnp.stack([got[0].reshape(32, 8, width), got[1].reshape(32, 8, width)], axis=1)
         parts[lax.rem(i, 2)] = back.reshape(2, 4, 4, 16, width).astype(BF16)
-        in_grad[...] += got[2]
-        out_grad[...] += got[3]
-        bias_grad[...] += got[4]
+        active[i], hidden_grad[i] = got[2:]
         results_way(i).start_core()
 
     def middle_of(step):
@@ -764,13 +804,8 @@
     def p_in(i, head):
         return pltpu.make_async_copy(p_hbm.at[i, head], p.at[head], p_in_sem.at[head])
 
-    def arrive(hbm, ref, sem, i):
-        pltpu.make_async_copy(hbm.at[i], ref.at[i], sem.at[i]).wait()
-
     def forward(i, carry):
-        arrive(x_hbm, x, x_sem, i)
-        for step in projections(x.at[i], wt, vec[...], q.at[i], k.at[i], v.at[i]):
-            step()
+        projections(middle.at[i], wt, vec[...], q.at[i], k.at[i], v.at[i])
         arrive(g_hbm, g, g_sem, i)
         middle_of(i)
 
@@ -809,15 +844,15 @@
 
         results_way(i).finish()
         total = results_way(i).total()
+        produced[i] = total[:8] + shift[...]
         got = backward_image(
             x.at[i], g.at[i], middle.at[i], dispatch[i], combine[i],
-            (total[:8] + shift[...]).astype(BF16), total[8:].astype(BF16),
+            produced[i].astype(BF16), total[8:].astype(BF16),
             wt, vec[...], table[...].astype(BF16),
             q.at[i], k.at[i], v.at[i], p, att.at[i], inv.at[i], ds, grad_t,
-            q.at[i], k.at[i], v.at[i], g.at[i], middle.at[i],
+            q.at[i], k.at[i], v.at[i], middle_grad.at[i],
             before_heads, after_heads,
         )
-        pltpu.make_async_copy(g.at[i], mixed_hbm.at[i], mixed_sem.at[i]).start()
         add_grads(weight_grad, sums, table_grad, got)
         end_of(count + i)
         return carry
@@ -825,7 +860,7 @@
     lax.fori_loop(0, count, backward, 0)
 
     fill_blocks(w_last[0], weight_grad[...].reshape(32, rows, width))
-    weights = Scatter(*w_last, by_chip=True)
+    weights = FineScatter(*w_last)
     weights.start_core()
     gains, biases = norm_sums(sums[...], weight_grad[: 3 * width, :], wt, vec[...])
     pieces = [
@@ -841,58 +876,51 @@
     vectors.start_plane()
 
     def finish(i, carry):
-        x[i] = finish_image(x.at[i], middle.at[i], wt, vec[...], q.at[i], k.at[i], v.at[i])
-        pltpu.make_async_copy(x.at[i], patch_grad_hbm.at[i], patch_sem.at[i]).start()
-
-        @pl.when(i == count // 2)
+        g[i], x[i] = finish_image(
+            x.at[i], middle.at[i], middle_grad.at[i], combine[i], produced[i].astype(BF16),
+            wt, vec[...], q.at[i], k.at[i], v.at[i],
+        )
+        all_slots, all_grads = arrived_rows(i)
+        in_grad[...] += dot(hidden_grad[i], all_slots, 0, 0)
+        out_grad[...] += dot(active[i], all_grads, 0, 0)
+        bias_grad[...] += jnp.sum(hidden_grad[i].astype(F32).reshape(32, 8, -1), axis=0)
+
+        for block in (1, 2, 3):
+
+            @pl.when(i == block)
+            def _(block=block):
+                weights.start_z(block)
+
+        @pl.when(i == 3)
         def _():
-            weights.start_z()
             vectors.start_z()
 
         return carry
 
     lax.fori_loop(0, count, finish, 0)
-    weights.finish()
     weight_out[...] = weights.total()
     vectors.finish()
     vectors_out[...] = vectors.total()
-    for i in range(count):
-        pltpu.make_async_copy(g.at[i], mixed_hbm.at[i], mixed_sem.at[i]).wait()
-        pltpu.make_async_copy(x.at[i], patch_grad_hbm.at[i], patch_sem.at[i]).wait()
 
 
 def hand_over_kernel(
     mixed, patch_grad, weight_grad, in_grad, out_grad, vectors, bias_grad,
-    mixed_out, patch_grad_out, weight_out, in_out, out_out, gains, biases, table, shift, bias_out,
-    images, weights, arrived, left,
+    mixed_out, patch_grad_out, weight_out, in_out, out_out, gains, biases, table, shift, bias_out, sems,
 ):
-    count = mixed.shape[0]
-    moves = []
-    for n, (src, dst) in enumerate(((mixed, mixed_out), (patch_grad, patch_grad_out))):
-        moves += [(src.at[i], images.at[n, i], dst.at[i]) for i in range(count)]
-    at = 0
-    for src, dst in ((weight_grad, weight_out), (in_grad, in_out), (out_grad, out_out)):
-        moves.append((src, weights.at[pl.ds(at, src.shape[0])], dst))
-        at += src.shape[0]
-    copies = [
-        (
-            pltpu.make_async_copy(src, stage, arrived.at[n]),
-            pltpu.make_async_copy(stage, dst, left.at[n]),
-        )
-        for n, (src, stage, dst) in enumerate(moves)
-    ]
-    for come, _ in copies:
-        come.start()
+    moves = (
+        (mixed, mixed_out), (patch_grad, patch_grad_out), (weight_grad, weight_out),
+        (in_grad, in_out), (out_grad, out_out),
+    )
+    copies = [pltpu.make_async_copy(src, dst, sems.at[n]) for n, (src, dst) in enumerate(moves)]
+    for copy in copies:
+        copy.start()
     for n, ref in enumerate((gains, biases, table, shift)):
         ref[...] = vectors[n : n + 1, : ref.shape[0]].reshape(ref.shape[0])
     experts, units = bias_out.shape
     for e in range(experts):
         bias_out[e : e + 1, :] = bias_grad[e : e + 1, e * units : (e + 1) * units]
-    for come, go in copies:
-        come.wait()
-        go.start()
-    for _, go in copies:
-        go.wait()
+    for copy in copies:
+        copy.wait()
 
 
 def run_layer(patches, valid, attn_weights, vectors, expert_in, expert_in_bias, expert_out, out_grad):
@@ -909,17 +937,15 @@
     mixed, patch_grad, _, weight_grad, vector_grads, in_grad, out_grads, bias_grad = pl.pallas_call(
         functools.partial(layer_kernel, lengths),
         in_specs=[anywhere] * 2 + [here_all] * 9,
-        out_specs=[anywhere] * 3 + [here_all] * 5,
+        out_specs=[here_all] * 2 + [anywhere] + [here_all] * 5,
         out_shape=[
-            jax.ShapeDtypeStruct(patches.shape, BF16), jax.ShapeDtypeStruct(patches.shape, BF16),
+            vmem(patches.shape, BF16), vmem(patches.shape, BF16),
             jax.ShapeDtypeStruct((count, heads, length, length), BF16),
-            jax.ShapeDtypeStruct((rows, width), F32), jax.ShapeDtypeStruct((16, 128), F32),
-            jax.ShapeDtypeStruct((experts * units, width), F32),
-            jax.ShapeDtypeStruct((experts * units, width), F32),
-            jax.ShapeDtypeStruct((experts, experts * units), F32),
+            vmem((rows, width), F32), vmem((16, 128), F32),
+            vmem((experts * units, width), F32), vmem((experts * units, width), F32),
+            vmem((experts, experts * units), F32),
         ],
         scratch_shapes=[
-            vmem((count,) + flat, BF16), vmem((count,) + flat, BF16),
             vmem((count,) + flat, BF16), vmem((count,) + flat, BF16), vmem((count,) + flat, BF16),
             vmem((count,) + flat, BF16), vmem((count,) + flat, BF16), vmem((count,) + flat, F32),
             vmem((count, experts, length), F32), vmem((count, experts, length), F32),
@@ -929,17 +955,22 @@
             vmem((1, experts * units), F32),
             vmem((4 * width, width), F32), vmem((8, width), F32), vmem((experts, width), F32),
             vmem((experts, width), F32), vmem((16, 128), F32),
-            dma((count,)), dma((count,)), dma((heads,)), dma((heads,)), dma((count,)), dma((count,)),
+            vmem((count,) + flat, F32), vmem((count, experts, width), F32),
+            vmem((count, 32 * experts, experts * units), BF16),
+            vmem((count, 32 * experts, experts * units), BF16),
+            dma((count,)), dma((count,)), dma((heads,)), dma((heads,)),
         ]
         + [vmem((count, 2, 4, 4, 16, width), BF16), dma((count, 7)), dma((count, 7))]
         + [
             vmem((2, 2, 4, 4, 16, width), BF16), vmem((2, 4, 4, 16, width), BF16),
             vmem((2, 4, 4, 16, width), BF16), vmem((count, 3, 4, 16, width), BF16),
             vmem((count, 4, 16, width), BF16), vmem((count, 3, 16, width), BF16),
-            dma((count, 10)), dma((count, 10)),
+            dma((count, 7)), dma((count, 7)),
         ]
         + fine_scratch(rows, width) + gather_scratch(16, 128)
-        + scatter_scratch(rows, width) + scatter_scratch(16, 128),
+        + scatter_scratch(rows, width)[:6]
+        + [dma((4,)), dma((4,)), dma((3, 4)), dma((3, 4)), dma((3,)), dma((3,))]
+        + scatter_scratch(16, 128),
         compiler_params=pltpu.CompilerParams(
             collective_id=0, has_side_effects=True, vmem_limit_bytes=LAYER_LIMIT
         ),
@@ -951,7 +982,7 @@
     )
     results = pl.pallas_call(
         hand_over_kernel,
-        in_specs=[anywhere] * 5 + [here_all] * 2,
+        in_specs=[here_all] * 7,
         out_specs=[anywhere] * 5 + [here_all] * 5,
         out_shape=[
             jax.ShapeDtypeStruct(value.shape, value.dtype)
@@ -959,11 +990,8 @@
         ]
         + [jax.ShapeDtypeStruct((piece,), F32) for piece in lengths]
         + [jax.ShapeDtypeStruct((experts, units), F32)],
-        scratch_shapes=[
-            vmem((2,) + patches.shape, BF16), vmem((rows + 2 * experts * units, width), F32),
-            dma((2 * count + 3,)), dma((2 * count + 3,)),
-        ],
-        compiler_params=pltpu.CompilerParams(vmem_limit_bytes=VMEM_LIMIT),
+        scratch_shapes=[dma((5,))],
+        compiler_params=pltpu.CompilerParams(vmem_limit_bytes=8 * 1024 * 1024),
         name="hand_over",
     )(mixed, patch_grad, weight_grad, in_grad, out_grads, vector_grads, bias_grad)
     mixed, patch_grad, weight_grad, in_grad, out_grads, gains, biases, table, shift, bias_grad = results

time: 133 us -> 124 us (0.932)
  Pallas kernels: 132 us -> 123 us
    pallas_call x1, Pallas kernels: 125 us -> 120 us  [run_layer(): pl.pallas_call(functools.partial(layer_kernel, lengths), in_specs=[anywhe...]
    pallas_call x1, Pallas kernels: 7.02 us -> 3.42 us  [run_layer(): pl.pallas_call(hand_over_kernel, in_specs=[here_all] * 7, out_specs=[anyw...]
where the time goes in v7:
time: 124 us
  Pallas kernels  123 us (99%)
    pallas_call x1, Pallas kernels, run_layer(): pl.pallas_call(functools.partial(layer_kernel, lengths), in_specs=[anywhe...  120 us
    pallas_call x1, Pallas kernels, run_layer(): pl.pallas_call(hand_over_kernel, in_specs=[here_all] * 7, out_specs=[anyw...  3.42 us

profile of v7, /device:TPU:0, one launch (start us, length us, event | category | flops | bytes accessed | tf_op | source)
XLA Modules:
  0.0 124.0 jit_solution(7238448650582498418)
XLA Ops:
  0.6 119.7 %layer.1 = (bf16[6,576,384]{2,1,0:T(8,128)(2,1)S(1)}, bf16[6,576,384]{2,1,0:T(8,128)(2,1)S(1)}, bf16[6,6,576,576]{3,2,1,0:T(8,128)(2,1)}, f32[48,384]{1,0:T(8,12...) custom-call(bf16[6,576,384]{2,1,0:T(8,128)(2,1)} %x_hbm.1, ...), custom_call_target="tpu_custom_call" | custom-call | tf_op jit(solution)/shard_map/layer/pallas_call | solution.py:937
  120.4 3.4 %hand_over.1 = (bf16[6,576,384]{2,1,0:T(8,128)(2,1)}, bf16[6,576,384]{2,1,0:T(8,128)(2,1)}, f32[48,384]{1,0:T(8,128)}, f32[384,384]{1,0:T(8,128)}, f32[384,384]{...) custom-call(bf16[6,576,384]{2,1,0:T(8,128)(2,1)S(1)} %get-tuple-element.27.mixed, ...), custom_call_target="tpu_custom_call" | custom-call | tf_op jit(solution)/shard_map/hand_over/pallas_call | solution.py:983

commit v8 on v7

--- a/solution.py
+++ b/solution.py
@@ -51,9 +51,10 @@
     return jnp.where(low, own, other) if head % 2 == 0 else jnp.where(low, other, own)
 
 
-def projections(normed, wt, vec, q_ref, k_ref, v_ref):
+def projections(normed, wt, vec, h1_ref, q_ref, k_ref, v_ref):
     width = wt.shape[1]
     first = (normed[...] * vec[GAIN1 : GAIN1 + 1] + vec[BIAS1 : BIAS1 + 1]).astype(BF16)
+    h1_ref[...] = first
     got = dot(first, wt[: 3 * width], 1, 1)
     q_ref[...] = (got[:, :width] * HEAD_DIM ** (-0.5)).astype(BF16)
     k_ref[...] = got[:, width : 2 * width].astype(BF16)
@@ -85,14 +86,9 @@
         )
 
     sums = {}
-    score(0)
-    for head in range(heads):
-        if head + 1 < heads:
-            score(head + 1)
-        raw = scores.pop(head)
-        prob = jnp.exp(raw - jnp.max(raw, axis=1, keepdims=True)).astype(BF16)
-        p_ref[head] = prob
-        sums[head] = dot(prob, own_half(low, head, pair_of(v_ref, head), one), 1, 0)
+
+    def product(head):
+        sums[head] = dot(p_ref[head], own_half(low, head, pair_of(v_ref, head), one), 1, 0)
         if after_head is not None:
             after_head(head)
         if head % 2 == 1:
@@ -101,6 +97,16 @@
             at = head // 2 * PAIR
             inv_ref[:, at : at + PAIR] = inverse.astype(inv_ref.dtype)
             att_ref[:, at : at + PAIR] = (jnp.where(low, even, odd) * inverse).astype(BF16)
+
+    score(0)
+    for head in range(heads):
+        if head + 1 < heads:
+            score(head + 1)
+        if head > 0:
+            product(head - 1)
+        raw = scores.pop(head)
+        p_ref[head] = jnp.exp(raw - jnp.max(raw, axis=1, keepdims=True)).astype(BF16)
+    product(heads - 1)
     branch = dot(att_ref[...], wt[3 * width :], 1, 1)
     middle = x[...].astype(F32) + branch + vec[OBIAS : OBIAS + 1]
     normed, _ = normalize(middle)
@@ -118,8 +124,9 @@
 
 def backward_image(
     x, g, middle_ref, dispatch, combine, produced, slot_grad, wt, vec, table,
-    q_ref, k_ref, v_ref, p_ref, att_ref, inv_ref, ds_ref, grad_t_ref, dq_ref, dk_ref, dv_ref, grad_ref,
-    before_heads=None, after_heads=None,
+    q_ref, k_ref, v_ref, p_ref, att_ref, inv_ref, ds_ref, grad_t_ref, dq_ref,
+    mixed_ref, grad_ref,
+    before_heads=None, after_heads=None, between=(),
 ):
     patches, width = x.shape
     heads = width // HEAD_DIM
@@ -128,12 +135,21 @@
     normed, factor = normalize(middle)
     second = (normed * vec[GAIN2 : GAIN2 + 1] + vec[BIAS2 : BIAS2 + 1]).astype(BF16)
     upstream = g[...]
+    other_work = list(between)
+
+    def other():
+        if other_work:
+            other_work.pop(0)()
+
+    other()
+    mixed = (middle + dot(combine.astype(BF16), produced, 0, 0)).astype(BF16)
     combine_grad = dot(produced, upstream, 1, 1)
     dispatch_grad = dot(slot_grad, second, 1, 1)
     logit_grad = dispatch * (
         dispatch_grad - jnp.sum(dispatch * dispatch_grad, axis=1, keepdims=True)
     ) + combine * (combine_grad - jnp.sum(combine * combine_grad, axis=0, keepdims=True))
     logit_grad = logit_grad.astype(BF16)
+    other()
     table_grad = dot(logit_grad, second, 1, 0)
     second_grad = dot(
         jnp.concatenate([dispatch_low, logit_grad], axis=0),
@@ -146,10 +162,11 @@
     middle_grad = upstream.astype(F32) + norm_back(
         second_grad * vec[GAIN2 : GAIN2 + 1], normed, factor
     )
+    mixed_ref[...] = mixed
     grad_ref[...] = middle_grad
+    other()
     branch_grad = middle_grad.astype(BF16)
     branch_shift = jnp.sum(branch_grad.astype(F32), axis=0, keepdims=True)
-    output_grad = dot(branch_grad.T, att_ref[...], 1, 0)
     attended_grad = dot(branch_grad, wt[3 * width :], 1, 0).astype(BF16).astype(F32)
     scaled = attended_grad * inv_ref[...].astype(F32)
     drop = (-(scaled * att_ref[...].astype(F32))).astype(BF16)
@@ -196,29 +213,38 @@
             dq_ref[:, at : at + PAIR] = (both * HEAD_DIM ** (-0.5)).astype(BF16)
     if after_heads is not None:
         after_heads()
-    dk_ref[...] = grad_t_ref[:width, :].T
-    dv_ref[...] = grad_t_ref[width:, :].T
-    normed, _ = normalize(x[...].astype(F32))
-    first = (normed * vec[GAIN1 : GAIN1 + 1] + vec[BIAS1 : BIAS1 + 1]).astype(BF16)
-    query_front = dot(dq_ref[...].T, first, 1, 0)
-    other_front = dot(grad_t_ref[...], first, 1, 0)
-    columns = [
-        jnp.sum(ref[...].astype(F32), axis=0, keepdims=True) for ref in (dq_ref, dk_ref, dv_ref)
-    ]
     sums = jnp.concatenate(
-        columns + [gain_two, branch_shift, shift_two, jnp.zeros((2, width), F32)], axis=0
-    )
-    return query_front, other_front, output_grad, sums, table_grad
-
-
-def finish_image(x, middle, middle_grad, combine, produced, wt, vec, dq_ref, dk_ref, dv_ref):
+        [jnp.zeros((3, width), F32), gain_two, branch_shift, shift_two, jnp.zeros((2, width), F32)],
+        axis=0,
+    )
+    return sums, table_grad
+
+
+def front_grads(first, grad_t_ref, dq_ref, dk_ref, dv_ref, weight_grad, sums):
+    width = first.shape[1]
+
+    def turn():
+        dk_ref[...] = grad_t_ref[:width, :].T
+        dv_ref[...] = grad_t_ref[width:, :].T
+
+    def key_and_value():
+        weight_grad[width : 3 * width, :] += dot(grad_t_ref[...], first[...], 1, 0)
+
+    def query():
+        weight_grad[:width, :] += dot(dq_ref[...].T, first[...], 1, 0)
+        for n, ref in enumerate((dq_ref, dk_ref, dv_ref)):
+            sums[n : n + 1, :] += jnp.sum(ref[...].astype(F32), axis=0, keepdims=True)
+
+    return [turn, key_and_value, query]
+
+
+def finish_image(x, middle_grad, wt, vec, dq_ref, dk_ref, dv_ref):
     width = x.shape[1]
-    mixed = middle[...] + dot(combine.astype(BF16), produced, 0, 0)
     normed, factor = normalize(x[...].astype(F32))
     project_grad = jnp.concatenate([dq_ref[...], dk_ref[...], dv_ref[...]], axis=1)
     first_grad = dot(project_grad, wt[: 3 * width], 1, 0)
     grad = middle_grad[...] + norm_back(first_grad * vec[GAIN1 : GAIN1 + 1], normed, factor)
-    return mixed.astype(BF16), grad.astype(BF16)
+    return grad.astype(BF16)
 
 
 def norm_sums(sums, weight_grad, wt, vec):
@@ -237,10 +263,10 @@
 
 def forward_kernel(
     x, g, valid, wt, vec, table,
-    q, k, v, p, att, inv, middle, dispatch, combine, slots, produced_grad,
+    h1, q, k, v, p, att, inv, middle, dispatch, combine, slots, produced_grad,
 ):
     middle[0] = normalize(x[0].astype(F32))[0]
-    projections(middle.at[0], wt, vec[...], q.at[0], k.at[0], v.at[0])
+    projections(middle.at[0], wt, vec[...], h1.at[0], q.at[0], k.at[0], v.at[0])
     got = forward_image(
         x.at[0], g.at[0], valid[0], wt, vec[...], table[...],
         q.at[0], k.at[0], v.at[0], p.at[0], att.at[0], inv.at[0],
@@ -249,18 +275,15 @@
         ref[0] = value.astype(ref.dtype)
 
 
-def add_grads(weight_grad, sums, table_grad, got):
+def add_output_grad(weight_grad, middle_grad, att):
     width = weight_grad.shape[1]
-    for ref, at, value in (
-        (weight_grad, 0, got[0]), (weight_grad, width, got[1]), (weight_grad, 3 * width, got[2]),
-        (sums, 0, got[3]), (table_grad, 0, got[4]),
-    ):
-        ref[at : at + value.shape[0], :] += value
+    branch_grad = middle_grad.astype(BF16).reshape(-1, width)
+    weight_grad[3 * width :, :] += dot(branch_grad.T, att.reshape(-1, width), 1, 0)
 
 
 def backward_kernel(
     x, g, middle, dispatch, combine, produced, slot_grad, wt, vec, table,
-    q, k, v, p, att, inv,
+    h1, q, k, v, p, att, inv,
     mixed, patch_grad, weight_grad, sums, table_grad,
     ds, grad_t, dq, dk, dv, middle_grad,
 ):
@@ -273,13 +296,15 @@
     got = backward_image(
         x.at[0], g.at[0], middle.at[0], dispatch[0], combine[0], produced[0], slot_grad[0],
         wt, vec[...], table[...],
-        q.at[0], k.at[0], v.at[0], p.at[0], att.at[0], inv.at[0], ds, grad_t, dq, dk, dv,
-        middle_grad,
-    )
-    mixed[0], patch_grad[0] = finish_image(
-        x.at[0], middle.at[0], middle_grad, combine[0], produced[0], wt, vec[...], dq, dk, dv
-    )
-    add_grads(weight_grad, sums, table_grad, got)
+        q.at[0], k.at[0], v.at[0], p.at[0], att.at[0], inv.at[0], ds, grad_t, dq,
+        mixed.at[0], middle_grad,
+    )
+    sums[...] += got[0]
+    table_grad[...] += got[1]
+    for step in front_grads(h1.at[0], grad_t, dq, dk, dv, weight_grad, sums):
+        step()
+    add_output_grad(weight_grad, middle_grad[...], att[0])
+    patch_grad[0] = finish_image(x.at[0], middle_grad, wt, vec[...], dq, dk, dv)
 
 
 def per_image(*shape):
@@ -296,7 +321,7 @@
     experts = table.shape[0]
     flat = (patches, width)
     outs = [
-        (flat, BF16), (flat, BF16), (flat, BF16), ((heads, patches, patches), BF16),
+        (flat, BF16), (flat, BF16), (flat, BF16), (flat, BF16), ((heads, patches, patches), BF16),
         (flat, BF16), (flat, F32), (flat, F32),
         ((experts, patches), F32), ((experts, patches), F32),
         ((experts, width), BF16), ((experts, width), BF16),
@@ -320,7 +345,7 @@
     heads = width // HEAD_DIM
     experts = table.shape[0]
     flat = (patches, width)
-    q, k, v, p, att, inv, middle, dispatch, combine = kept
+    h1, q, k, v, p, att, inv, middle, dispatch, combine = kept
     return pl.pallas_call(
         backward_kernel,
         grid=(count,),
@@ -329,7 +354,7 @@
             per_image(experts, patches), per_image(experts, patches),
             per_image(experts, width), per_image(experts, width),
             whole(*wt.shape), whole(*vec.shape), whole(*table.shape),
-            per_image(*flat), per_image(*flat), per_image(*flat),
+            per_image(*flat), per_image(*flat), per_image(*flat), per_image(*flat),
             per_image(heads, patches, patches), per_image(*flat), per_image(*flat),
         ],
         out_specs=[
@@ -351,7 +376,7 @@
         ],
         compiler_params=pltpu.CompilerParams(vmem_limit_bytes=VMEM_LIMIT),
         name="backward",
-    )(x, g, middle, dispatch, combine, produced, slot_grad, wt, vec, table, q, k, v, p, att, inv)
+    )(x, g, middle, dispatch, combine, produced, slot_grad, wt, vec, table, h1, q, k, v, p, att, inv)
 
 
 def here():
@@ -580,18 +605,19 @@
             self.z_sems[0].at[k - 1], self.z_sems[1].at[k - 1], (self.w, self.goal(k)),
         )
 
-    def start_core(self):
-        for chip in [there // 2 for there, _ in self.plane] + [self.w // 2]:
-            self.core_copy(chip).start()
-
-    def start_plane(self):
-        for n, chip in enumerate([there // 2 for there, _ in self.plane] + [self.w // 2]):
-            self.core_copy(chip).wait()
-            own = self.parts[self.core, chip].astype(F32)
-            self.chips[chip] = (own + self.from_core[chip].astype(F32)).astype(BF16)
-        for k in (1, 2, 3, 0):
-            for n in range(3):
-                self.plane_copy(n, k).start()
+    def start_core(self, chip):
+        self.core_copy(chip).start()
+
+    def start_plane(self, chip):
+        self.core_copy(chip).wait()
+        own = self.parts[self.core, chip].astype(F32)
+        self.chips[chip] = (own + self.from_core[chip].astype(F32)).astype(BF16)
+        for n, peer in enumerate(self.plane):
+
+            @pl.when(peer[0] // 2 == chip)
+            def _(n=n):
+                for k in (1, 2, 3, 0):
+                    self.plane_copy(n, k).start()
 
     def plane_sum(self, k):
         z = self.goal(k)
@@ -702,9 +728,9 @@
     lengths,
     x_hbm, g_hbm, valid, own_weights, own_gains, own_biases, own_table, own_shift, w_in, own_bias, w_out,
     g, x, p_hbm, weight_out, vectors_out, in_grad, out_grad, bias_grad,
-    q, k, v, att, inv, middle, dispatch, combine, p, ds, grad_t, wt, vec, table, shift, bias,
+    h1, q, k, v, att, inv, middle, dispatch, combine, p, ds, grad_t, wt, vec, table, shift, bias,
     weight_grad, sums, table_grad, shift_grad, own_pieces,
-    middle_grad, produced, active, hidden_grad,
+    active, hidden_grad,
     x_sem, g_sem, p_out_sem, p_in_sem,
     every, g_send, g_recv,
     parts, from_core, chips, from_plane, column, from_z, s_send, s_recv,
@@ -805,7 +831,7 @@
         return pltpu.make_async_copy(p_hbm.at[i, head], p.at[head], p_in_sem.at[head])
 
     def forward(i, carry):
-        projections(middle.at[i], wt, vec[...], q.at[i], k.at[i], v.at[i])
+        projections(middle.at[i], wt, vec[...], h1.at[i], q.at[i], k.at[i], v.at[i])
         arrive(g_hbm, g, g_sem, i)
         middle_of(i)
 
@@ -826,9 +852,18 @@
         return carry
 
     lax.fori_loop(0, count, forward, 0)
+    q[count] = jnp.zeros_like(q[count])
+    h1[count] = jnp.zeros_like(h1[count])
+    grad_t[...] = jnp.zeros_like(grad_t)
     for head in range(heads):
         p_out(count - 1, head).wait()
         p_in(0, head).start()
+
+    def front(i):
+        place = lax.rem(i + count + 1, count + 1)
+        return front_grads(
+            h1.at[place], grad_t, q.at[place], k.at[place], v.at[place], weight_grad, sums
+        )
 
     def backward(i, carry):
         def before_heads():
@@ -844,24 +879,38 @@
 
         results_way(i).finish()
         total = results_way(i).total()
-        produced[i] = total[:8] + shift[...]
         got = backward_image(
             x.at[i], g.at[i], middle.at[i], dispatch[i], combine[i],
-            produced[i].astype(BF16), total[8:].astype(BF16),
+            (total[:8] + shift[...]).astype(BF16), total[8:].astype(BF16),
             wt, vec[...], table[...].astype(BF16),
             q.at[i], k.at[i], v.at[i], p, att.at[i], inv.at[i], ds, grad_t,
-            q.at[i], k.at[i], v.at[i], middle_grad.at[i],
-            before_heads, after_heads,
+            q.at[i], g.at[i], middle.at[i], before_heads, after_heads, front(i - 1),
         )
-        add_grads(weight_grad, sums, table_grad, got)
+        sums[...] += got[0]
+        table_grad[...] += got[1]
         end_of(count + i)
         return carry
 
     lax.fori_loop(0, count, backward, 0)
-
-    fill_blocks(w_last[0], weight_grad[...].reshape(32, rows, width))
+    for step in front(count - 1):
+        step()
+
     weights = FineScatter(*w_last)
-    weights.start_core()
+
+    def depart(chip):
+        for core in range(2):
+            block = weight_grad[pl.ds((2 * chip + core) * 4 * rows, 4 * rows), :]
+            w_last[0][core, chip] = block.reshape(4, rows, width).astype(BF16)
+        weights.start_core(chip)
+
+    for chip in range(3):
+        depart(chip)
+    for i in range(0, count, 2):
+        add_output_grad(weight_grad, middle[i : i + 2], att[i : i + 2])
+        if i == 0:
+            for chip in range(3):
+                weights.start_plane(chip)
+    depart(3)
     gains, biases = norm_sums(sums[...], weight_grad[: 3 * width, :], wt, vec[...])
     pieces = [
         pieces_of(value, length, 32)
@@ -872,14 +921,11 @@
     fill_blocks(v_last[0], pieces)
     vectors = Scatter(*v_last)
     vectors.start_core()
-    weights.start_plane()
+    weights.start_plane(3)
     vectors.start_plane()
 
     def finish(i, carry):
-        g[i], x[i] = finish_image(
-            x.at[i], middle.at[i], middle_grad.at[i], combine[i], produced[i].astype(BF16),
-            wt, vec[...], q.at[i], k.at[i], v.at[i],
-        )
+        x[i] = finish_image(x.at[i], middle.at[i], wt, vec[...], q.at[i], k.at[i], v.at[i])
         all_slots, all_grads = arrived_rows(i)
         in_grad[...] += dot(hidden_grad[i], all_slots, 0, 0)
         out_grad[...] += dot(active[i], all_grads, 0, 0)
@@ -946,7 +992,8 @@
             vmem((experts, experts * units), F32),
         ],
         scratch_shapes=[
-            vmem((count,) + flat, BF16), vmem((count,) + flat, BF16), vmem((count,) + flat, BF16),
+            vmem((count + 1,) + flat, BF16), vmem((count + 1,) + flat, BF16),
+            vmem((count + 1,) + flat, BF16), vmem((count + 1,) + flat, BF16),
             vmem((count,) + flat, BF16), vmem((count,) + flat, BF16), vmem((count,) + flat, F32),
             vmem((count, experts, length), F32), vmem((count, experts, length), F32),
             vmem((heads, length, length), BF16), vmem((2, length, length), BF16),
@@ -955,7 +1002,6 @@
             vmem((1, experts * units), F32),
             vmem((4 * width, width), F32), vmem((8, width), F32), vmem((experts, width), F32),
             vmem((experts, width), F32), vmem((16, 128), F32),
-            vmem((count,) + flat, F32), vmem((count, experts, width), F32),
             vmem((count, 32 * experts, experts * units), BF16),
             vmem((count, 32 * experts, experts * units), BF16),
             dma((count,)), dma((count,)), dma((heads,)), dma((heads,)),

time: 124 us -> 119 us (0.960)
  Pallas kernels: 123 us -> 118 us
    pallas_call x1, Pallas kernels: 120 us -> 114 us  [run_layer(): pl.pallas_call(functools.partial(layer_kernel, lengths), in_specs=[anywhe...]
where the time goes in v8:
time: 119 us
  Pallas kernels  118 us (99%)
    pallas_call x1, Pallas kernels, run_layer(): pl.pallas_call(functools.partial(layer_kernel, lengths), in_specs=[anywhe...  114 us
    pallas_call x1, Pallas kernels, run_layer(): pl.pallas_call(hand_over_kernel, in_specs=[here_all] * 7, out_specs=[anyw...  3.42 us

profile of v8, /device:TPU:0, one launch (start us, length us, event | category | flops | bytes accessed | tf_op | source)
XLA Modules:
  0.0 118.5 jit_solution(9113404554859124914)
XLA Ops:
  0.6 114.3 %layer.1 = (bf16[6,576,384]{2,1,0:T(8,128)(2,1)S(1)}, bf16[6,576,384]{2,1,0:T(8,128)(2,1)S(1)}, bf16[6,6,576,576]{3,2,1,0:T(8,128)(2,1)}, f32[48,384]{1,0:T(8,12...) custom-call(bf16[6,576,384]{2,1,0:T(8,128)(2,1)} %x_hbm.1, ...), custom_call_target="tpu_custom_call" | custom-call | tf_op jit(solution)/shard_map/layer/pallas_call | solution.py:983
  114.9 3.4 %hand_over.1 = (bf16[6,576,384]{2,1,0:T(8,128)(2,1)}, bf16[6,576,384]{2,1,0:T(8,128)(2,1)}, f32[48,384]{1,0:T(8,128)}, f32[384,384]{1,0:T(8,128)}, f32[384,384]{...) custom-call(bf16[6,576,384]{2,1,0:T(8,128)(2,1)S(1)} %get-tuple-element.27.mixed, ...), custom_call_target="tpu_custom_call" | custom-call | tf_op jit(solution)/shard_map/hand_over/pallas_call | solution.py:1029

commit v9 on v8

--- a/solution.py
+++ b/solution.py
@@ -51,6 +51,11 @@
     return jnp.where(low, own, other) if head % 2 == 0 else jnp.where(low, other, own)
 
 
+def own_rows(head, rows, other):
+    own = rows[head * HEAD_DIM : (head + 1) * HEAD_DIM]
+    return jnp.concatenate([own, other] if head % 2 == 0 else [other, own], axis=0)
+
+
 def projections(normed, wt, vec, h1_ref, q_ref, k_ref, v_ref):
     width = wt.shape[1]
     first = (normed[...] * vec[GAIN1 : GAIN1 + 1] + vec[BIAS1 : BIAS1 + 1]).astype(BF16)
@@ -63,12 +68,13 @@
 
 def forward_image(
     x, g, valid_row, wt, vec, table, q_ref, k_ref, v_ref, p_ref, att_ref, inv_ref,
-    after_head=None,
+    after_head=None, after_heads=None,
 ):
     patches, width = x.shape
     heads = width // HEAD_DIM
     bias_row = jnp.where(valid_row > 0, 0.0, MASKED).astype(F32)
-    fill = jnp.broadcast_to(bias_row * (1.0 / HEAD_DIM), (PAIR, patches)).T.astype(BF16)
+    fill = jnp.broadcast_to(bias_row * (1.0 / HEAD_DIM), (HEAD_DIM, patches)).astype(BF16)
+    key_t = k_ref[...].T
     low = lower_half((patches, PAIR))
     one = jnp.ones((patches, PAIR), BF16)
     scores = {}
@@ -80,9 +86,9 @@
     def score(head):
         scores[head] = dot(
             own_half(low, head, pair_of(q_ref, head), one),
-            own_half(low, head, pair_of(k_ref, head), fill),
+            own_rows(head, key_t, fill),
             1,
-            1,
+            0,
         )
 
     sums = {}
@@ -107,6 +113,8 @@
         raw = scores.pop(head)
         p_ref[head] = jnp.exp(raw - jnp.max(raw, axis=1, keepdims=True)).astype(BF16)
     product(heads - 1)
+    if after_heads is not None:
+        after_heads()
     branch = dot(att_ref[...], wt[3 * width :], 1, 1)
     middle = x[...].astype(F32) + branch + vec[OBIAS : OBIAS + 1]
     normed, _ = normalize(middle)
@@ -173,6 +181,8 @@
     scaled = scaled.astype(BF16)
     scaled_t = scaled.T
     query_t = q_ref[...].T
+    value_t = v_ref[...].T
+    one_t = jnp.ones((HEAD_DIM, patches), BF16)
     if before_heads is not None:
         before_heads()
     low = lower_half((patches, PAIR))
@@ -187,9 +197,9 @@
         rolled = pltpu.roll(pair_of(drop, head).astype(F32), HEAD_DIM, 1).astype(BF16)
         prob_grads[head] = dot(
             own_half(low, head, pair_of(scaled, head), rolled),
-            own_half(low, head, pair_of(v_ref, head), one),
+            own_rows(head, value_t, one_t),
             1,
-            1,
+            0,
         )
 
     query_grads = {}
@@ -831,18 +841,18 @@
         return pltpu.make_async_copy(p_hbm.at[i, head], p.at[head], p_in_sem.at[head])
 
     def forward(i, carry):
-        projections(middle.at[i], wt, vec[...], h1.at[i], q.at[i], k.at[i], v.at[i])
         arrive(g_hbm, g, g_sem, i)
-        middle_of(i)
 
         @pl.when(i > 0)
         def _():
             for head in range(heads):
                 p_out(i - 1, head).wait()
 
+        projections(middle.at[i], wt, vec[...], h1.at[i], q.at[i], k.at[i], v.at[i])
         got = forward_image(
             x.at[i], g.at[i], valid[pl.ds(i, 1)], wt, vec[...], table[...].astype(BF16),
             q.at[i], k.at[i], v.at[i], p, att.at[i], inv.at[i], lambda head: p_out(i, head).start(),
+            lambda: middle_of(i),
         )
         middle[i], dispatch[i], combine[i] = got[:3]
         shift_grad[...] += got[4].astype(BF16).astype(F32)
@@ -892,9 +902,6 @@
         return carry
 
     lax.fori_loop(0, count, backward, 0)
-    for step in front(count - 1):
-        step()
-
     weights = FineScatter(*w_last)
 
     def depart(chip):
@@ -903,12 +910,17 @@
             w_last[0][core, chip] = block.reshape(4, rows, width).astype(BF16)
         weights.start_core(chip)
 
-    for chip in range(3):
-        depart(chip)
+    turn, key_and_value, query = front(count - 1)
+    turn()
+    key_and_value()
+    depart(1)
+    depart(2)
+    query()
+    depart(0)
     for i in range(0, count, 2):
         add_output_grad(weight_grad, middle[i : i + 2], att[i : i + 2])
         if i == 0:
-            for chip in range(3):
+            for chip in (1, 2, 0):
                 weights.start_plane(chip)
     depart(3)
     gains, biases = norm_sums(sums[...], weight_grad[: 3 * width, :], wt, vec[...])
@@ -931,11 +943,11 @@
         out_grad[...] += dot(active[i], all_grads, 0, 0)
         bias_grad[...] += jnp.sum(hidden_grad[i].astype(F32).reshape(32, 8, -1), axis=0)
 
-        for block in (1, 2, 3):
+        for block in (2, 3, 4):
 
             @pl.when(i == block)
             def _(block=block):
-                weights.start_z(block)
+                weights.start_z(block - 1)
 
         @pl.when(i == 3)
         def _():

time: 119 us -> 118 us (level)
  no operation moved by 1% of the time
where the time goes in v9:
time: 118 us; the launch traced here: 117 us
  Pallas kernels  117 us (99%)
    pallas_call x1, Pallas kernels, run_layer(): pl.pallas_call(functools.partial(layer_kernel, lengths), in_specs=[anywhe...  113 us
    pallas_call x1, Pallas kernels, run_layer(): pl.pallas_call(hand_over_kernel, in_specs=[here_all] * 7, out_specs=[anyw...  3.42 us

profile of v9, /device:TPU:0, one launch (start us, length us, event | category | flops | bytes accessed | tf_op | source)
XLA Modules:
  0.0 117.4 jit_solution(7150698652297050682)
XLA Ops:
  0.6 113.2 %layer.1 = (bf16[6,576,384]{2,1,0:T(8,128)(2,1)S(1)}, bf16[6,576,384]{2,1,0:T(8,128)(2,1)S(1)}, bf16[6,6,576,576]{3,2,1,0:T(8,128)(2,1)}, f32[48,384]{1,0:T(8,12...) custom-call(bf16[6,576,384]{2,1,0:T(8,128)(2,1)} %x_hbm.1, ...), custom_call_target="tpu_custom_call" | custom-call | tf_op jit(solution)/shard_map/layer/pallas_call | solution.py:995
  113.8 3.4 %hand_over.1 = (bf16[6,576,384]{2,1,0:T(8,128)(2,1)}, bf16[6,576,384]{2,1,0:T(8,128)(2,1)}, f32[48,384]{1,0:T(8,128)}, f32[384,384]{1,0:T(8,128)}, f32[384,384]{...) custom-call(bf16[6,576,384]{2,1,0:T(8,128)(2,1)S(1)} %get-tuple-element.27.mixed, ...), custom_call_target="tpu_custom_call" | custom-call | tf_op jit(solution)/shard_map/hand_over/pallas_call | solution.py:1041
